TPU v7x, 32 devices: a whole 2x2x4 slice. The times are simulated.
32 devices in a mesh: seq: 8 (over y, x, core), grp: 4 (over z).
Axes of the slice: x: 2, y: 2, z: 4, core: 2. Of those that a mesh axis runs over, the one named last changes fastest.
Arguments:
- tokens: bfloat16 [8192, 2048], P(('seq', 'grp')), may hold values from -6 to 6
- cotangent: bfloat16 [8192, 2048], P(('seq', 'grp')), may hold values from -6 to 6
- lengths: int32 [8], replicated, may hold values from 1 to 7936, as said below
- pad_mask: int32 [8192], P(('seq', 'grp')), may hold values 0 or 1
- mixer_gain: bfloat16 [2048], P(('seq', 'grp')), may hold values from 0.5 to 1.5
- query_weight: bfloat16 [2048, 2048], P(('seq', 'grp')), may hold values from -0.125 to 0.125
- key_weight: bfloat16 [2048, 2048], P(('seq', 'grp')), may hold values from -0.125 to 0.125
- value_weight: bfloat16 [2048, 2048], P(('seq', 'grp')), may hold values from -0.125 to 0.125
- conv_query: bfloat16 [2048, 4], P(('seq', 'grp')), may hold values from -3 to 3
- conv_key: bfloat16 [2048, 4], P(('seq', 'grp')), may hold values from -3 to 3
- conv_value: bfloat16 [2048, 4], P(('seq', 'grp')), may hold values from -3 to 3
- beta_weight: bfloat16 [2048, 16], P(('seq', 'grp')), may hold values from -0.125 to 0.125
- beta_bias: float32 [16], replicated, may hold values from -9 to 1
- head_gain: float32 [128], replicated, may hold values from 0.5 to 1.5
- out_weight: bfloat16 [2048, 2048], P(('seq', 'grp')), may hold values from -0.125 to 0.125
- feed_gain: bfloat16 [2048], P(('seq', 'grp')), may hold values from 0.5 to 1.5
- gate_weight: bfloat16 [2048, 5632], P(('seq', 'grp')), may hold values from -0.125 to 0.125
- up_weight: bfloat16 [2048, 5632], P(('seq', 'grp')), may hold values from -0.125 to 0.125
- down_weight: bfloat16 [2048, 5632], P(('seq', 'grp')), may hold values from -0.078125 to 0.078125
Outputs:
- block_out: bfloat16 [8192, 2048], P(('seq', 'grp'))
- input_grad: bfloat16 [8192, 2048], P(('seq', 'grp'))
- mixer_gain_grad: float32 [2048], P(('seq', 'grp'))
- query_grad: float32 [2048, 2048], P(('seq', 'grp'))
- key_grad: float32 [2048, 2048], P(('seq', 'grp'))
- value_grad: float32 [2048, 2048], P(('seq', 'grp'))
- conv_query_grad: float32 [2048, 4], P(('seq', 'grp'))
- conv_key_grad: float32 [2048, 4], P(('seq', 'grp'))
- conv_value_grad: float32 [2048, 4], P(('seq', 'grp'))
- beta_weight_grad: float32 [2048, 16], P(('seq', 'grp'))
- beta_bias_grad: float32 [16], replicated
- head_gain_grad: float32 [128], replicated
- out_weight_grad: float32 [2048, 2048], P(('seq', 'grp'))
- feed_gain_grad: float32 [2048], P(('seq', 'grp'))
- gate_grad: float32 [2048, 5632], P(('seq', 'grp'))
- up_grad: float32 [2048, 5632], P(('seq', 'grp'))
- down_grad: float32 [2048, 5632], P(('seq', 'grp'))
Inputs may be any that keep to these rules, and one draw needn't show every extreme that they name: The 8 documents lie end to end from position 0 and their lengths sum to 8192; exactly one document, neither the first nor the last, holds the longest length, and the others together hold 256 positions.
All inputs are finite; a program needn't handle non-finite values. No bound on the sum of `pad_mask` on one device may be relied on, other than what follows from the above.
Results may differ from a plain program's by a relative error of at most 0.012.
The roundings to bfloat16 on the way count: a program that leaves them out, or rounds other values in their place, can miss the bound.
Values may be sent and summed in bfloat16 or wider, within the bound.
A program may use at most 704 MiB of HBM per device.

v0:
```python
import jax
import jax.numpy as jnp
from jax import lax
from jax.sharding import PartitionSpec as P

BLOCK = 64


HIGH = lax.Precision.HIGHEST
EPSILON = 1e-06


def passed_along(value, axis, steps):
    count = lax.axis_size(axis)
    first, last = (max(0, -steps), min(count, count - steps))
    return lax.ppermute(value, axis, [(source, source + steps) for source in range(first, last)])


def rms_scale(values, gain):
    return values * lax.rsqrt(jnp.mean(values * values, axis=-1, keepdims=True) + EPSILON) * gain


def unit_rows(values):
    return values * lax.rsqrt(jnp.sum(values * values, axis=-1, keepdims=True) + EPSILON)


def matmul_high(left, right):
    return jnp.matmul(left, right, precision=HIGH)


def contract(left, right):
    return lax.dot_general(
        left, right, (((1,), (1,)), ((), ())), preferred_element_type=jnp.float32
    )


def compose(earlier, later):
    return (matmul_high(later[0], earlier[0]), matmul_high(later[0], earlier[1]) + later[1])


def choose_pair(flag, first_pair, second_pair):
    return (
        jnp.where(flag, first_pair[0], second_pair[0]),
        jnp.where(flag, first_pair[1], second_pair[1]),
    )


def inverse_unit(lower_part):
    length = lower_part.shape[-1]
    identity_small = jnp.eye(length, dtype=jnp.float32)
    result = identity_small - lower_part
    power = lower_part
    reach = 2
    while reach < length:
        power = matmul_high(power, power)
        result = matmul_high(result, identity_small + power)
        reach = reach * 2
    return result


def block_masks(row_start, anchor, length):
    count = row_start.shape[0] // length
    starts = row_start.reshape(count, length)
    begins = anchor + jnp.arange(count, dtype=jnp.int32) * length
    first_rows = (starts < begins[:, None]).astype(jnp.float32)
    same_doc = (starts[:, :, None] == starts[:, None, :]).astype(jnp.float32)
    last_part = (starts == starts[:, -1:]).astype(jnp.float32)
    return (first_rows, same_doc, last_part, first_rows[:, -1])


def blocks_of(stacked, length):
    return stacked.reshape((stacked.shape[0] // length, length) + stacked.shape[1:])


def block_terms(keys_now, values_now, betas_now, first_rows, same_doc):
    length = keys_now.shape[0]
    strict = jnp.tril(jnp.ones((length, length), jnp.float32), -1)
    intersection = jnp.einsum("chd,jhd->hcj", keys_now, keys_now, precision=HIGH)
    lower_part = jnp.transpose(betas_now)[:, :, None] * intersection * (same_doc * strict)[None]
    inverse = inverse_unit(lower_part)
    weights_wy = jnp.einsum(
        "hcj,jhd->hcd",
        inverse,
        keys_now * (betas_now * first_rows[:, None])[:, :, None],
        precision=HIGH,
    )
    updates = jnp.einsum(
        "hcj,jhd->hcd", inverse, values_now * betas_now[:, :, None], precision=HIGH
    )
    return (weights_wy, updates)


def block_output(
    memory, queries_now, keys_now, weights_wy, updates, first_rows, same_doc, last_part, carries
):
    length = queries_now.shape[0]
    causal = jnp.tril(jnp.ones((length, length), jnp.float32))
    fresh_rows = updates - matmul_high(weights_wy, memory)
    scores = (
        jnp.einsum("chd,jhd->hcj", queries_now, keys_now, precision=HIGH)
        * (same_doc * causal)[None]
    )
    outputs = first_rows[:, None, None] * jnp.einsum(
        "chd,hde->che", queries_now, memory, precision=HIGH
    )
    outputs = outputs + jnp.einsum("hcj,hje->che", scores, fresh_rows, precision=HIGH)
    updated = carries * memory + jnp.einsum(
        "chd,hce->hde", keys_now * last_part[:, None, None], fresh_rows, precision=HIGH
    )
    return (updated, outputs)


def span_pass(key_rows, value_rows, beta_rows, masks, length):
    head_count, head_width = (key_rows.shape[1], key_rows.shape[2])
    identity_big = jnp.broadcast_to(
        jnp.eye(head_width, dtype=jnp.float32), (head_count, head_width, head_width)
    )

    def advance(pair_now, inputs):
        keys_now, values_now, betas_now, first_rows, same_doc, last_part, carries = inputs
        weights_wy, updates = block_terms(keys_now, values_now, betas_now, first_rows, same_doc)
        kept_keys = keys_now * last_part[:, None, None]
        local_a = carries * identity_big - jnp.einsum(
            "chd,hce->hde", kept_keys, weights_wy, precision=HIGH
        )
        local_b = jnp.einsum("chd,hce->hde", kept_keys, updates, precision=HIGH)
        return (compose(pair_now, (local_a, local_b)), (weights_wy, updates))

    inputs = (
        blocks_of(key_rows, length),
        blocks_of(value_rows, length),
        blocks_of(beta_rows, length),
    ) + masks
    return lax.scan(advance, (identity_big, jnp.zeros_like(identity_big)), inputs)


def mixer_apply(memory, query_rows, key_rows, stored, masks, length):

    def advance(current, inputs):
        queries_now, keys_now, weights_wy, updates, first_rows, same_doc, last_part, carries = (
            inputs
        )
        return block_output(
            current,
            queries_now,
            keys_now,
            weights_wy,
            updates,
            first_rows,
            same_doc,
            last_part,
            carries,
        )

    inputs = (
        blocks_of(query_rows, length),
        blocks_of(key_rows, length),
        stored[0],
        stored[1],
    ) + masks
    final, outputs = lax.scan(advance, memory, inputs)
    return (outputs.reshape(query_rows.shape), final)


def mixer_run(memory, query_rows, key_rows, value_rows, beta_rows, masks, length):

    def advance(current, inputs):
        queries_now, keys_now, values_now, betas_now, first_rows, same_doc, last_part, carries = (
            inputs
        )
        weights_wy, updates = block_terms(keys_now, values_now, betas_now, first_rows, same_doc)
        return block_output(
            current,
            queries_now,
            keys_now,
            weights_wy,
            updates,
            first_rows,
            same_doc,
            last_part,
            carries,
        )

    inputs = (
        blocks_of(query_rows, length),
        blocks_of(key_rows, length),
        blocks_of(value_rows, length),
        blocks_of(beta_rows, length),
    ) + masks
    final, outputs = lax.scan(advance, memory, inputs)
    return (outputs.reshape(query_rows.shape), final)


def state_adjoint(query_rows, key_rows, stored, grad_rows, masks, length):
    head_count, head_width = (key_rows.shape[1], key_rows.shape[2])
    identity_big = jnp.broadcast_to(
        jnp.eye(head_width, dtype=jnp.float32), (head_count, head_width, head_width)
    )

    def advance(adjoint, inputs):
        queries_now, keys_now, weights_wy, grad_now, first_rows, same_doc, last_part, carries = (
            inputs
        )
        causal = jnp.tril(jnp.ones((length, length), jnp.float32))
        scores = (
            jnp.einsum("chd,jhd->hcj", queries_now, keys_now, precision=HIGH)
            * (same_doc * causal)[None]
        )
        pulled = jnp.einsum("hcj,che->hje", scores, grad_now, precision=HIGH)
        local_c = jnp.einsum(
            "chd,che->hde", queries_now * first_rows[:, None, None], grad_now, precision=HIGH
        )
        local_c = local_c - jnp.einsum("hjd,hje->hde", weights_wy, pulled, precision=HIGH)
        turned = carries * identity_big - jnp.einsum(
            "hcd,che->hde", weights_wy * last_part[None, :, None], keys_now, precision=HIGH
        )
        return (matmul_high(turned, adjoint) + local_c, None)

    inputs = (
        blocks_of(query_rows, length),
        blocks_of(key_rows, length),
        stored[0],
        blocks_of(grad_rows, length),
    ) + masks
    final, _ = lax.scan(advance, jnp.zeros_like(identity_big), inputs, reverse=True)
    return final


def local(
    tokens,
    cotangent,
    lengths,
    pad_mask,
    mixer_gain,
    query_weight,
    key_weight,
    value_weight,
    conv_query,
    conv_key,
    conv_value,
    beta_weight,
    beta_bias,
    head_gain,
    out_weight,
    feed_gain,
    gate_weight,
    up_weight,
    down_weight,
):
    row_count, model_width = tokens.shape
    head_count = beta_bias.shape[0]
    head_width = head_gain.shape[0]
    tap_count = conv_query.shape[1]
    fetched = (
        lax.all_gather(mixer_gain, ("seq", "grp"), axis=0, tiled=True),
        lax.all_gather(query_weight, ("seq", "grp"), axis=0, tiled=True),
        lax.all_gather(key_weight, ("seq", "grp"), axis=0, tiled=True),
        lax.all_gather(value_weight, ("seq", "grp"), axis=0, tiled=True),
        lax.all_gather(conv_query, ("seq", "grp"), axis=0, tiled=True),
        lax.all_gather(conv_key, ("seq", "grp"), axis=0, tiled=True),
        lax.all_gather(conv_value, ("seq", "grp"), axis=0, tiled=True),
        lax.all_gather(beta_weight, ("seq", "grp"), axis=0, tiled=True),
        lax.all_gather(out_weight, ("seq", "grp"), axis=0, tiled=True),
        lax.all_gather(feed_gain, ("seq", "grp"), axis=0, tiled=True),
        lax.all_gather(gate_weight, ("seq", "grp"), axis=0, tiled=True),
        lax.all_gather(up_weight, ("seq", "grp"), axis=0, tiled=True),
        lax.all_gather(down_weight, ("seq", "grp"), axis=0, tiled=True),
    )
    (
        gain_mixer,
        w_query,
        w_key,
        w_value,
        c_query,
        c_key,
        c_value,
        w_beta,
        w_out,
        gain_feed,
        w_gate,
        w_up,
        w_down,
    ) = fetched
    anchor = lax.axis_index(("seq", "grp")) * row_count
    places = anchor + jnp.arange(row_count, dtype=jnp.int32)
    starts = jnp.cumsum(lengths) - lengths
    row_start = jnp.max(jnp.where(starts[None, :] <= places[:, None], starts[None, :], 0), axis=1)
    valid = jnp.stack(
        [(places - offset >= row_start).astype(jnp.float32) for offset in range(1, tap_count)]
    )
    live_rows = pad_mask.astype(jnp.float32)
    inputs32 = tokens.astype(jnp.float32)
    normed_a, norm_a_back = jax.vjp(rms_scale, inputs32, gain_mixer.astype(jnp.float32))
    normed_low = normed_a.astype(jnp.bfloat16)
    query_pre = jnp.dot(normed_low, w_query, preferred_element_type=jnp.float32).astype(
        jnp.bfloat16
    )
    key_pre = jnp.dot(normed_low, w_key, preferred_element_type=jnp.float32).astype(jnp.bfloat16)
    value_pre = jnp.dot(normed_low, w_value, preferred_element_type=jnp.float32).astype(
        jnp.bfloat16
    )
    logit_part = jnp.dot(normed_low, w_beta, preferred_element_type=jnp.float32)
    sigmoid_val = jax.nn.sigmoid(logit_part + beta_bias)
    beta_rows = sigmoid_val * live_rows[:, None]
    own_pre = jnp.concatenate([query_pre, key_pre, value_pre], axis=1)
    earlier_rows = passed_along(own_pre[row_count - (tap_count - 1) :], ("seq", "grp"), 1)
    extended = jnp.concatenate([earlier_rows, own_pre], axis=0).astype(jnp.float32)
    kernel = jnp.concatenate([c_query, c_key, c_value], axis=0).astype(jnp.float32)

    def conv_act(padded, kernel_all):
        summed = padded[tap_count - 1 :] * kernel_all[:, tap_count - 1]
        for offset in range(1, tap_count):
            moved = padded[tap_count - 1 - offset : tap_count - 1 - offset + row_count]
            summed = (
                summed + moved * valid[offset - 1][:, None] * kernel_all[:, tap_count - 1 - offset]
            )
        active = jax.nn.silu(summed)
        queries_out = unit_rows(active[:, :model_width].reshape(row_count, head_count, head_width))
        keys_out = unit_rows(
            active[:, model_width : 2 * model_width].reshape(row_count, head_count, head_width)
        )
        values_out = active[:, 2 * model_width :].reshape(row_count, head_count, head_width)
        return (queries_out, keys_out, values_out)

    (queries, key_rows, value_rows), conv_pull = jax.vjp(conv_act, extended, kernel)
    masks = block_masks(row_start, anchor, BLOCK)
    (span_a, span_b), stored = span_pass(key_rows, value_rows, beta_rows, masks, BLOCK)
    identity_big = jnp.broadcast_to(
        jnp.eye(head_width, dtype=jnp.float32), (head_count, head_width, head_width)
    )
    zero_state = jnp.zeros_like(identity_big)
    identity = (identity_big, zero_state)
    group_size = lax.axis_size("grp")
    seq_size = lax.axis_size("seq")
    my_group = lax.axis_index("grp")
    my_seq = lax.axis_index("seq")
    group_a, group_b = (
        lax.all_gather(span_a[None], "grp", axis=0, tiled=True),
        lax.all_gather(span_b[None], "grp", axis=0, tiled=True),
    )
    group_total = identity
    before = identity
    for member in range(group_size):
        element = (group_a[member], group_b[member])
        before = choose_pair(member < my_group, compose(before, element), before)
        group_total = compose(group_total, element)
    seq_a, seq_b = (
        lax.all_gather(group_total[0][None], "seq", axis=0, tiled=True),
        lax.all_gather(group_total[1][None], "seq", axis=0, tiled=True),
    )

    def forward_groups(index_now, current):
        return jnp.where(
            index_now < my_seq, matmul_high(seq_a[index_now], current) + seq_b[index_now], current
        )

    from_groups = lax.fori_loop(0, seq_size, forward_groups, zero_state)
    start_state = matmul_high(before[0], from_groups) + before[1]
    mixed, _ = mixer_apply(start_state, queries, key_rows, stored, masks, BLOCK)

    def head_norm(mixed_in, gain_in):
        return (rms_scale(mixed_in, gain_in) * live_rows[:, None, None]).reshape(
            row_count, model_width
        )

    head_out, head_pull = jax.vjp(head_norm, mixed, head_gain)
    head_low = head_out.astype(jnp.bfloat16)
    hidden_one = inputs32 + jnp.dot(head_low, w_out, preferred_element_type=jnp.float32)
    normed_f, norm_f_back = jax.vjp(rms_scale, hidden_one, gain_feed.astype(jnp.float32))
    feed_low = normed_f.astype(jnp.bfloat16)
    gate = jnp.dot(feed_low, w_gate, preferred_element_type=jnp.float32)
    upper = jnp.dot(feed_low, w_up, preferred_element_type=jnp.float32)
    gate_sig = jax.nn.sigmoid(gate)
    gate_act = gate * gate_sig
    inner_low = (gate_act * upper).astype(jnp.bfloat16)
    block_out = (hidden_one + contract(inner_low, w_down)).astype(jnp.bfloat16)
    w_query, w_key, w_value, w_beta, w_out, w_gate, w_up, w_down = (
        lax.all_gather(query_weight, ("seq", "grp"), axis=0, tiled=True),
        lax.all_gather(key_weight, ("seq", "grp"), axis=0, tiled=True),
        lax.all_gather(value_weight, ("seq", "grp"), axis=0, tiled=True),
        lax.all_gather(beta_weight, ("seq", "grp"), axis=0, tiled=True),
        lax.all_gather(out_weight, ("seq", "grp"), axis=0, tiled=True),
        lax.all_gather(gate_weight, ("seq", "grp"), axis=0, tiled=True),
        lax.all_gather(up_weight, ("seq", "grp"), axis=0, tiled=True),
        lax.all_gather(down_weight, ("seq", "grp"), axis=0, tiled=True),
    )
    grad_out = cotangent.astype(jnp.float32)
    d_inner = jnp.dot(cotangent, w_down, preferred_element_type=jnp.float32)
    d_gate = (d_inner * upper * gate_sig * (1.0 + gate * (1.0 - gate_sig))).astype(jnp.bfloat16)
    d_upper = (d_inner * gate_act).astype(jnp.bfloat16)
    d_feed = contract(d_gate, w_gate) + contract(d_upper, w_up)
    d_hidden_part, d_gain_feed = norm_f_back(d_feed)
    d_hidden = grad_out + d_hidden_part
    d_attn = d_hidden.astype(jnp.bfloat16)
    d_head = contract(d_attn, w_out)
    d_mixed, d_head_gain = head_pull(d_head)
    adjoint_c = state_adjoint(queries, key_rows, stored, d_mixed, masks, BLOCK)
    adjoint_a = jnp.swapaxes(span_a, 1, 2)
    back_a, back_c = (
        lax.all_gather(adjoint_a[None], "grp", axis=0, tiled=True),
        lax.all_gather(adjoint_c[None], "grp", axis=0, tiled=True),
    )
    back_total = identity
    after = identity
    for member in reversed(range(group_size)):
        element = (back_a[member], back_c[member])
        after = choose_pair(member > my_group, compose(after, element), after)
        back_total = compose(back_total, element)
    later_a, later_c = (
        lax.all_gather(back_total[0][None].astype(jnp.bfloat16), "seq", axis=0, tiled=True).astype(
            jnp.float32
        ),
        lax.all_gather(back_total[1][None].astype(jnp.bfloat16), "seq", axis=0, tiled=True).astype(
            jnp.float32
        ),
    )

    def backward_groups(count_now, current):
        index_now = seq_size - 1 - count_now
        return jnp.where(
            index_now > my_seq,
            matmul_high(later_a[index_now], current) + later_c[index_now],
            current,
        )

    from_later = lax.fori_loop(0, seq_size, backward_groups, zero_state)
    end_grad = matmul_high(after[0], from_later) + after[1]

    def mixer_local(query_in, key_in, value_in, beta_in):
        return mixer_run(start_state, query_in, key_in, value_in, beta_in, masks, BLOCK)

    _, mixer_pull = jax.vjp(mixer_local, queries, key_rows, value_rows, beta_rows)
    d_queries, d_keys, d_values, d_betas = mixer_pull((d_mixed, end_grad))
    d_logit32 = d_betas * live_rows[:, None] * sigmoid_val * (1.0 - sigmoid_val)
    d_logit = d_logit32.astype(jnp.bfloat16)
    d_extended, d_kernel = conv_pull((d_queries, d_keys, d_values))
    from_next = passed_along(
        d_extended[: tap_count - 1].astype(jnp.bfloat16), ("seq", "grp"), -1
    ).astype(jnp.float32)
    d_own = d_extended[tap_count - 1 :] + jnp.pad(
        from_next, ((row_count - (tap_count - 1), 0), (0, 0))
    )
    d_pre = d_own.astype(jnp.bfloat16)
    d_query_pre = d_pre[:, :model_width]
    d_key_pre = d_pre[:, model_width : 2 * model_width]
    d_value_pre = d_pre[:, 2 * model_width :]
    d_normed = (
        contract(d_query_pre, w_query)
        + contract(d_key_pre, w_key)
        + contract(d_value_pre, w_value)
        + contract(d_logit, w_beta)
    )
    d_input_part, d_gain_mixer = norm_a_back(d_normed)
    input_grad = (d_hidden + d_input_part).astype(jnp.bfloat16)
    small_sums = lax.psum((d_head_gain, jnp.sum(d_logit32, axis=0)), ("seq", "grp"))

    def grad_rows(start, count):

        def outer(matrix, grads):
            return lax.dot_general(
                matrix, grads, (((0,), (0,)), ((), ())), preferred_element_type=jnp.float32
            )

        def rows_of(vector, shift_rows):
            return lax.dynamic_slice_in_dim(vector, shift_rows, count, 0)

        pieces = [
            outer(normed_low, d_query_pre),
            outer(normed_low, d_key_pre),
            outer(normed_low, d_value_pre),
            outer(head_low, d_attn),
            outer(feed_low, d_gate),
            outer(feed_low, d_upper),
            outer(cotangent, inner_low),
            outer(normed_low, d_logit),
            rows_of(d_kernel, 0),
            rows_of(d_kernel, model_width),
            rows_of(d_kernel, 2 * model_width),
            rows_of(d_gain_mixer, 0)[:, None],
            rows_of(d_gain_feed, 0)[:, None],
        ]
        return jnp.concatenate(pieces, axis=1)

    summed = lax.psum_scatter(
        grad_rows(
            jnp.int32(0),
            lax.axis_size(("seq", "grp")) * (model_width // lax.axis_size(("seq", "grp"))),
        ),
        ("seq", "grp"),
        scatter_dimension=0,
        tiled=True,
    )
    hidden_units = gate_weight.shape[1]
    spans = [
        model_width,
        model_width,
        model_width,
        model_width,
        hidden_units,
        hidden_units,
        hidden_units,
        head_count,
        tap_count,
        tap_count,
        tap_count,
        1,
        1,
    ]
    parts_out = []
    offset_now = 0
    for span_width in spans:
        parts_out.append(summed[:, offset_now : offset_now + span_width])
        offset_now = offset_now + span_width
    return (
        block_out,
        input_grad,
        parts_out[11][:, 0],
        parts_out[0],
        parts_out[1],
        parts_out[2],
        parts_out[8],
        parts_out[9],
        parts_out[10],
        parts_out[7],
        small_sums[1],
        small_sums[0],
        parts_out[3],
        parts_out[12][:, 0],
        parts_out[4],
        parts_out[5],
        parts_out[6],
    )


def solution(mesh):
    placed = (
        P(("seq", "grp"), None),
        P(("seq", "grp"), None),
        P(),
        P(("seq", "grp")),
        P(("seq", "grp")),
        P(("seq", "grp"), None),
        P(("seq", "grp"), None),
        P(("seq", "grp"), None),
        P(("seq", "grp"), None),
        P(("seq", "grp"), None),
        P(("seq", "grp"), None),
        P(("seq", "grp"), None),
        P(),
        P(),
        P(("seq", "grp"), None),
        P(("seq", "grp")),
        P(("seq", "grp"), None),
        P(("seq", "grp"), None),
        P(("seq", "grp"), None),
    )
    return jax.shard_map(
        local,
        mesh=mesh,
        in_specs=placed,
        out_specs=(
            P(("seq", "grp"), None),
            P(("seq", "grp"), None),
            P(("seq", "grp")),
            P(("seq", "grp"), None),
            P(("seq", "grp"), None),
            P(("seq", "grp"), None),
            P(("seq", "grp"), None),
            P(("seq", "grp"), None),
            P(("seq", "grp"), None),
            P(("seq", "grp"), None),
            P(),
            P(),
            P(("seq", "grp"), None),
            P(("seq", "grp")),
            P(("seq", "grp"), None),
            P(("seq", "grp"), None),
            P(("seq", "grp"), None),
        ),
        check_vma=False,
    )
```

profile of v0, /device:TPU:0, one launch (start us, length us, event | category | flops | bytes accessed | tf_op | source)
XLA Modules:
  0.0 6790.9 jit_solution(3525248520164300345)
XLA Ops:
  13.5 42.4 all-reduce.15
  56.0 66.9 all-gather.8
  123.0 64.2 all-gather.9
  187.3 66.1 all-gather.10
  253.5 65.0 all-gather.11
  321.3 5.8 convolution_convert_fusion.1
  327.1 5.8 convolution_convert_fusion
  332.9 5.7 convolution_convert_fusion.2
  339.7 4.2 collective-permute-start
  347.9 6.1 fusion.328
  367.4 84.0 %while.176 = (s32[]{:T(128)}, f32[16,128,128]{2,1,0:T(8,128)S(1)}, f32[16,128,128]{2,1,0:T(8,128)}, f32[4,16,64,128]{3,2,1,0:T(8,128)}, f32[4,16,64,128]{3,2,1,0...) while((s32[]{:T(128)}, f32[16,128,128]{2,1,0:T(8,128)S(1)}, ...), condition=%wide.region_5.6_spmd.clone, body=%wide.region_4.5_spmd.clone.sunk | while | flops 2015138816 | bytes 29504484 | solution.py:134
  454.0 80.4 %all-gather.50.cloned.1.call-done = f32[64,128,128]{2,1,0:T(8,128)} async-done(((f32[16,128,128]{2,1,0:T(8,128)}), f32[64,128,128]{2,1,0:T(8,128)}) %all-gather.50.cloned.1.call-update) | async-done | bytes 4194320 | tf_op jit(solution)/shard_map/all_gather | solution.py:400
  541.2 74.5 %all-gather.46.cloned.1.call-done = f32[64,128,128]{2,1,0:T(8,128)} async-done(((f32[16,128,128]{2,1,0:T(8,128)}), f32[64,128,128]{2,1,0:T(8,128)}) %all-gather.46.cloned.1.call-update) | async-done | bytes 4194320 | tf_op jit(solution)/shard_map/all_gather | solution.py:339
  615.7 81.3 %all-gather.42.cloned.1.call-done = f32[64,128,128]{2,1,0:T(8,128)} async-done(((f32[16,128,128]{2,1,0:T(8,128)}), f32[64,128,128]{2,1,0:T(8,128)}) %all-gather.42.cloned.1.call-update) | async-done | bytes 4194320 | tf_op jit(solution)/shard_map/all_gather | solution.py:338
  741.7 6.8 convert.6
  748.5 43.1 all-gather.48.cloned.1.call-done
  791.6 56.9 all-gather.44.cloned.1.call-done
  848.5 23.7 while.177
  878.8 47.7 while.173
  926.4 4.5 copy.236
  935.7 6.7 multiply_reduce_fusion.10
  944.0 130.8 %all-gather.38.cloned.1.call-done = bf16[2048,5632]{1,0:T(8,128)(2,1)} async-done(((bf16[64,5632]{1,0:T(8,128)(2,1)}), bf16[2048,5632]{1,0:T(8,128)(2,1)}) %all-gather.38.cloned.1.call-update) | async-done | bytes 23068688 | tf_op jit(solution)/shard_map/all_gather | solution.py:266
  1074.8 13.2 fusion.425
  1088.0 132.3 %all-gather.36.cloned.1.call-done = bf16[2048,5632]{1,0:T(8,128)(2,1)} async-done(((bf16[64,5632]{1,0:T(8,128)(2,1)}), bf16[2048,5632]{1,0:T(8,128)(2,1)}) %all-gather.36.cloned.1.call-update) | async-done | bytes 23068688 | tf_op jit(solution)/shard_map/all_gather | solution.py:265
  1220.4 13.1 fusion.424
  1233.5 132.5 %all-gather.40.cloned.1.call-done = bf16[2048,5632]{1,0:T(8,128)(2,1)} async-done(((bf16[64,5632]{1,0:T(8,128)(2,1)}), bf16[2048,5632]{1,0:T(8,128)(2,1)}) %all-gather.40.cloned.1.call-update) | async-done | bytes 23068688 | tf_op jit(solution)/shard_map/all_gather | solution.py:267
  1366.0 17.3 multiply_convert_fusion
  1383.3 12.6 fusion.426
  1395.9 14.6 multiply_reduce_fusion.5
  1413.4 6.5 convolution_bitcast_fusion.6
  1426.4 56.5 while.178
  1492.1 134.1 %while.175 = (s32[]{:T(128)}, f32[16,128,128]{2,1,0:T(8,128)S(1)}, f32[4,16,64,64]{3,2,1,0:T(8,128)}, f32[4,16,64,1]{2,1,3,0:T(8,128)}, f32[4,1,64,64]{3,2,1,0:T...) while((s32[]{:T(128)}, f32[16,128,128]{2,1,0:T(8,128)S(1)}, ...), condition=%wide.region_20.21_spmd.clone.clone, body=%wide.region_19.20_spmd.clone.clone.sunk | while | flops 1311303680 | bytes 46039568 | solution.py:190
  1628.3 10.1 fusion.371
  1646.9 20.7 fusion.428
  1667.6 18.2 fusion.427
  1685.8 20.1 convolution_bitcast_fusion.5
  1712.5 6.7 convert.7
  1719.2 23.7 while.179
  1749.6 327.6 %while.174 = (s32[]{:T(128)}, f32[16,128,128]{2,1,0:T(8,128)}, f32[4,64,16,128]{3,2,1,0:T(8,128)}, f32[4,64,16,128]{3,2,1,0:T(8,128)}, f32[4,64,16,128]{3,2,1,0:...) while((s32[]{:T(128)}, f32[16,128,128]{2,1,0:T(8,128)}, ...), condition=%wide.region_25.26_spmd, body=%wide.region_21.25_spmd.sunk | while | flops 3225419776 | bytes 102221608 | solution.py:190
  1760.4 4.4 fusion.880
  1818.8 4.1 convolution_add_fusion.58
  1840.1 4.4 fusion.880
  1898.5 4.1 convolution_add_fusion.58
  1919.8 4.4 fusion.880
  1978.2 4.1 convolution_add_fusion.58
  1982.3 3.9 convolution_add_fusion.60
  1999.7 4.4 fusion.880
  2058.1 4.1 convolution_add_fusion.58
  2093.6 11.3 add_add_fusion.2
  2105.0 18.2 multiply_reduce_fusion.3
  2132.1 7.3 pad_add_fusion.1
  2141.2 9.0 multiply_multiply_fusion.5
  2150.2 9.7 pad_add_fusion
  2166.7 8.2 fusion.368
  2174.9 8.3 fusion.364
  2183.2 8.3 fusion.360
  2191.5 5.9 fusion.362
  2197.4 5.9 fusion.366
  2203.6 5.0 fusion.336
  2208.9 237.5 %concatenate.15 = f32[2048,25118]{1,0:T(8,128)} concatenate(f32[2048,2048]{1,0:T(8,128)} %fusion.368, f32[2048,2048]{1,0:T(8,128)} %fusion.364, f32[2048,2048]{1,0:T(8,128)} %fusion.360, f32[2048,2048]{1,0:T(8,128)} %fusion.371, f32[2048,5632]{1,0:T(8,128)} %fusion.427, f32[2048,5632]{1,0:T(8,128)} %fusion.428, f32[2048,5632]{1,0:T(8,128)} %convolution_bitcast_fusion.5, ...), dimensions={1} | concatenate | bytes 411533312 | tf_op jit(solution)/shard_map/concatenate | solution.py:482
  2446.5 14.4 fusion.332
  2460.9 47.6 all-reduce.14
  2511.8 4259.2 %reduce-scatter.2.cloned.1.call-done = f32[64,25118]{1,0:T(8,128)} async-done(((f32[2048,25118]{1,0:T(8,128)}), f32[64,25118]{1,0:T(8,128)}) %reduce-scatter.2.cloned.1.call-update) | async-done | bytes 6430224 | tf_op jit(solution)/shard_map/reduce_scatter | solution.py:484
  6779.7 4.4 fusion.411
  (1067 shorter events, 826.6 us)
Async XLA Ops:
  7.2 311.8 %copy-start.19 = (bf16[256,2048]{1,0:T(8,128)(2,1)S(1)}, bf16[256,2048]{1,0:T(8,128)(2,1)}, u32[]{:S(2)}) copy-start(bf16[256,2048]{1,0:T(8,128)(2,1)} %param.33) | copy-start | bytes 3145732
  7.2 312.8 %copy-start.115 = (f32[16]{0:T(128)S(1)}, f32[16]{0:T(128)}, u32[]{:S(2)}) copy-start(f32[16]{0:T(128)} %param.45) | copy-start | bytes 196
  7.2 314.1 %all-gather.30.cloned.1.call-start = ((), (), s32[]{:S(2)}) async-start(), calls=%async_computation.2 | async-start | bytes 8650752 | tf_op jit(solution)/shard_map/all_gather | solution.py:257
  7.9 319.1 %all-gather.32.cloned.1.call-start = ((), (), s32[]{:S(2)}) async-start(), calls=%async_computation.3 | async-start | bytes 8650752 | tf_op jit(solution)/shard_map/all_gather | solution.py:258
  8.7 324.2 %all-gather.28.cloned.1.call-start = ((), (), s32[]{:S(2)}) async-start(), calls=%async_computation.1 | async-start | bytes 8650752 | tf_op jit(solution)/shard_map/all_gather | solution.py:256
  9.4 524.9 %all-gather.50.cloned.1.call-start = ((), (), s32[]{:S(2)}) async-start(), calls=%async_computation.13 | async-start | bytes 5242880 | tf_op jit(solution)/shard_map/all_gather | solution.py:400
  10.2 922.1 %copy-start.106 = (f32[256]{0:T(256)}, f32[256]{0:T(256)S(1)}, u32[]{:S(2)}) copy-start(f32[256]{0:T(256)S(1)} %convert_element_type.183) | copy-start | bytes 3076
  56.0 276.9 %copy-start.78 = (f32[2048]{0:T(1024)}, f32[2048]{0:T(1024)S(1)}, u32[]{:S(2)}) copy-start(f32[2048]{0:T(1024)S(1)} %convert_element_type.172) | copy-start | bytes 24580
  319.8 13.1 copy-start.92
  319.8 28.0 copy-start.99
  319.8 28.0 copy-start.101
  319.8 28.0 copy-start.103
  321.2 26.6 copy-start.83
  321.2 26.6 copy-start.85
  321.2 26.6 copy-start.87
  321.3 26.6 copy-start.89
  339.7 5.4 collective-permute-start
  347.8 6.2 copy-start.9
  451.4 279.8 %copy-start.39 = (f32[128,128]{1,0:T(8,128)}, f32[128,128]{1,0:T(8,128)S(1)}, u32[]{:S(2)}) copy-start(f32[128,128]{1,0:T(8,128)S(1)} %get-tuple-element.4436) | copy-start | bytes 196612
  452.7 162.9 %all-gather.46.cloned.1.call-start = ((), (), s32[]{:S(2)}) async-start(), calls=%async_computation.11 | async-start | bytes 5242880 | tf_op jit(solution)/shard_map/all_gather | solution.py:339
  453.3 243.7 %all-gather.42.cloned.1.call-start = ((), (), s32[]{:S(2)}) async-start(), calls=%async_computation.9 | async-start | bytes 5242880 | tf_op jit(solution)/shard_map/all_gather | solution.py:338
  453.9 287.8 %all-gather.52.cloned.1.call-start = ((), (), s32[]{:S(2)}) async-start(), calls=%async_computation.14 | async-start | bytes 4718592 | tf_op jit(solution)/shard_map/all_gather | solution.py:410
  541.1 250.5 %all-gather.48.cloned.1.call-start = ((), (), s32[]{:S(2)}) async-start(), calls=%async_computation.12 | async-start | bytes 9437184 | tf_op jit(solution)/shard_map/all_gather | solution.py:349
  705.6 142.9 %all-gather.44.cloned.1.call-start = ((), (), s32[]{:S(2)}) async-start(), calls=%async_computation.10 | async-start | bytes 9437184 | tf_op jit(solution)/shard_map/all_gather | solution.py:348
  712.7 223.0 %all-gather.34.cloned.1.call-start = ((), (), s32[]{:S(2)}) async-start(), calls=%async_computation.4 | async-start | bytes 8650752 | tf_op jit(solution)/shard_map/all_gather | solution.py:263
  713.3 361.5 %all-gather.38.cloned.1.call-start = ((), (), s32[]{:S(2)}) async-start(), calls=%async_computation.6 | async-start | bytes 23789568 | tf_op jit(solution)/shard_map/all_gather | solution.py:266
  714.1 506.3 %all-gather.36.cloned.1.call-start = ((), (), s32[]{:S(2)}) async-start(), calls=%async_computation.5 | async-start | bytes 23789568 | tf_op jit(solution)/shard_map/all_gather | solution.py:265
  714.6 651.4 %all-gather.40.cloned.1.call-start = ((), (), s32[]{:S(2)}) async-start(), calls=%async_computation.7 | async-start | bytes 23789568 | tf_op jit(solution)/shard_map/all_gather | solution.py:267
  715.4 923.0 %all-gather.54.cloned.1.call-start = ((), (), s32[]{:S(2)}) async-start(), calls=%async_computation.15 | async-start | bytes 5242880 | tf_op jit(solution)/shard_map/all_gather | solution.py:401
  943.9 276.4 %copy-start.51 = (bf16[256,2048]{1,0:T(8,128)(2,1)}, bf16[256,2048]{1,0:T(8,128)(2,1)S(1)}, u32[]{:S(2)}) copy-start(bf16[256,2048]{1,0:T(8,128)(2,1)S(1)} %multiply_convert_fusion.3) | copy-start | bytes 3145732
  1395.9 14.6 copy-start.63
  1413.4 6.5 copy-start.34
  1483.9 228.6 %all-gather.56.cloned.1.call-start = ((), (), s32[]{:S(2)}) async-start(), calls=%async_computation.16 | async-start | bytes 4718592 | tf_op jit(solution)/shard_map/all_gather | solution.py:413
  1626.2 12.2 copy-start.7
  1646.9 5124.1 %reduce-scatter.2.cloned.1.call-start = ((), (), s32[]{:S(2)}) async-start(), calls=%async_computation.8 | async-start | bytes 213024768 | tf_op jit(solution)/shard_map/reduce_scatter | solution.py:484
  1646.9 20.7 copy-start.67
  1685.8 20.1 copy-start.3
  1712.5 6.7 copy-start.28
  1719.2 23.7 copy-start.65
  1719.2 23.7 copy-start.66
  1788.9 6.2 copy-start.43
  1868.7 6.2 copy-start.43
  1948.6 6.2 copy-start.43
  2028.3 6.2 copy-start.43
  2082.4 11.2 slice-start
  2087.1 6.5 slice-start.1
  2093.6 11.4 copy-start.100
  2093.6 11.4 copy-start.102
  2093.6 11.4 copy-start.104
  2129.9 11.3 slice-start.2
  2132.1 9.1 slice-start.3
  2150.2 11.3 copy-start.21
  2150.2 11.3 copy-start.79
  2150.2 11.3 copy-start.93
  2160.0 6.0 collective-permute-start.1
  2191.5 11.8 slice-start.4
  2446.4 14.5 copy-start.113
  2446.4 14.5 copy-start.114
  2446.5 62.1 copy-start.109
  2446.5 62.1 copy-start.112
  2446.5 62.1 copy-start.22
  2446.5 62.1 copy-start.35
  2446.5 62.1 copy-start.80
  2446.5 62.1 copy-start.94
  (115 other events, 344.8 us)
Sparse Core Ops, SparseCore 0:
  11.0 80.3 all-gather.29
  94.3 76.3 all-gather.31
  173.7 76.1 all-gather.27
  452.8 81.4 all-gather.49
  536.3 79.2 all-gather.45
  617.7 79.2 all-gather.41
  699.4 35.2 all-gather.51
  737.2 54.3 all-gather.47
  794.1 54.3 all-gather.43
  851.3 77.3 all-gather.33
  931.5 143.2 all-gather.37
  1077.5 142.8 all-gather.35
  1223.2 142.7 all-gather.39
  1484.1 78.9 all-gather.53
  1647.0 34.8 all-gather.55
  2446.5 4324.3 reduce-scatter.1
where the time goes:
time: 6810 us; the launch traced here: 6790 us
  waiting for transfers between devices  5000 us (73%)
  matrix products  883 us (13%)
  local copies, waits for them, and re-layouts  397 us (6%)
  blocking collectives  352 us (5%)
  other arithmetic  121 us (2%)
    reduce_scatter x1, waiting for transfers between devices, local(): lax.psum_scatter(grad_rows(jnp.int32(0), lax.axis_size(('seq', 'grp')) *...  4260 us
    dot_general x234, matrix products, matmul_high(): return jnp.matmul(left, right, precision=HIGH)  374 us
    concatenate x1, local copies, waits for them, and re-layouts, grad_rows(): return jnp.concatenate(pieces, axis=1)  237 us
  transfers between devices with their start and end apart: 18, of which 11 were waited for; matrix products, arithmetic and copies ran while one was open for 6% of the time, Pallas kernels for 0%

commit v1 on v0

v1 whole, which is shorter than its diff:
```python
import functools

import jax
import jax.numpy as jnp
from jax import lax
from jax.experimental import pallas as pl
from jax.experimental.pallas import tpu as pltpu
from jax.sharding import PartitionSpec as P

F32 = jnp.float32
LOW = jnp.bfloat16
EPSILON = 1e-06
VMEM_LIMIT = 56 * 1024 * 1024


def passed_along(value, axis, steps):
    count = lax.axis_size(axis)
    first, last = (max(0, -steps), min(count, count - steps))
    return lax.ppermute(value, axis, [(source, source + steps) for source in range(first, last)])


def rms_scale(values, gain):
    return values * lax.rsqrt(jnp.mean(values * values, axis=-1, keepdims=True) + EPSILON) * gain


def contract(left, right):
    return lax.dot_general(
        left, right, (((1,), (1,)), ((), ())), preferred_element_type=jnp.float32
    )


def split_low(value):
    upper = value.astype(LOW)
    return (upper, (value - upper.astype(F32)).astype(LOW))


def dot_one(left, right, dims=((1,), (0,))):
    return lax.dot_general(
        left.astype(LOW), right.astype(LOW), (dims, ((), ())), preferred_element_type=F32
    )


def dot_three(left, right, dims=((1,), (0,))):
    left_high, left_rest = split_low(left)
    right_high, right_rest = split_low(right)
    both = functools.partial(
        lax.dot_general, dimension_numbers=(dims, ((), ())), preferred_element_type=F32
    )
    return both(left_high, right_high) + (both(left_high, right_rest) + both(left_rest, right_high))


ROWS_ROWS = ((1,), (1,))
FIRST_FIRST = ((0,), (0,))


def inverse_unit_lower(lower, size):
    row = lax.broadcasted_iota(jnp.int32, (size, size), 0)
    column = lax.broadcasted_iota(jnp.int32, (size, size), 1)
    inverse = jnp.where(row == column, 1.0, 0.0).astype(F32)
    span = 1
    while span < size:
        joined = (row // (2 * span) == column // (2 * span)) & (row // span != column // span)
        part = jnp.where(joined, lower, 0.0)
        if span == 1:
            inverse = inverse - part
        else:
            inverse = inverse - dot_three(inverse, dot_three(part, inverse))
        span = span * 2
    return inverse


def unit(active):
    scale = lax.rsqrt(jnp.sum(active * active, axis=1, keepdims=True) + EPSILON)
    return (active * scale, scale)


def unit_back(grad, normal, scale):
    return scale * (grad - normal * jnp.sum(grad * normal, axis=1, keepdims=True))


def pick_lane(block, index):
    lane = lax.broadcasted_iota(jnp.int32, block.shape, 1)
    return jnp.sum(jnp.where(lane == index, block, 0.0), axis=1, keepdims=True)


def span_kernel(
    starts_col, starts_row, flags, betas, queries, keys, values,
    inverse_out, wy_out, scores_out, reach_out, local_out, pair_out,
):
    head = pl.program_id(0)
    count = queries.shape[0]
    width = queries.shape[1]
    row = lax.broadcasted_iota(jnp.int32, (count, count), 0)
    column = lax.broadcasted_iota(jnp.int32, (count, count), 1)
    same_doc = starts_col[...] == starts_row[...]
    first = flags[:, 0:1]
    last_part = flags[:, 1:2]
    beta = pick_lane(betas[...], head)
    query, _ = unit(queries[...])
    key, _ = unit(keys[...])
    value = values[...]
    products = dot_three(jnp.concatenate([key, query], axis=0), key, ROWS_ROWS)
    lower = jnp.where(same_doc & (row > column), beta * products[:count], 0.0)
    scores = jnp.where(same_doc & (row >= column), products[count:], 0.0)
    inverse = inverse_unit_lower(lower, count)
    wy = dot_three(inverse, jnp.concatenate([key * (beta * first), value * beta], axis=1))
    applied = dot_three(scores, wy)
    inverse_out[0] = inverse
    wy_out[0] = wy
    scores_out[0] = scores
    reach_out[...] = first * query - applied[:, :width]
    local_out[...] = applied[:, width:]
    pair = dot_three(key * last_part, wy, FIRST_FIRST)
    eye = jnp.where(
        lax.broadcasted_iota(jnp.int32, (width, width), 0)
        == lax.broadcasted_iota(jnp.int32, (width, width), 1),
        1.0,
        0.0,
    )
    change = (flags[count - 1 : count, 0:1] - 1.0) * eye - pair[:, :width]
    pair_out[0] = jnp.concatenate([change, pair[:, width:]], axis=1).astype(LOW)


def rows_specs(count, width, head_count):
    return [
        pl.BlockSpec((count, width), lambda head, part=part: (0, part * head_count + head))
        for part in range(3)
    ]


def span_call(starts, flags, betas, active, head_count):
    count, width = active.shape[0], active.shape[1] // (3 * head_count)
    rows = pl.BlockSpec((count, width), lambda head: (0, head))
    whole = lambda shape: pl.BlockSpec(shape, lambda head: (0, 0))
    square = pl.BlockSpec((1, count, count), lambda head: (head, 0, 0))
    return pl.pallas_call(
        span_kernel,
        grid=(head_count,),
        in_specs=[
            whole((count, 1)), whole((1, count)), whole(flags.shape), whole(betas.shape),
        ]
        + rows_specs(count, width, head_count),
        out_specs=[
            square,
            pl.BlockSpec((1, count, 2 * width), lambda head: (head, 0, 0)),
            square, rows, rows,
            pl.BlockSpec((1, width, 2 * width), lambda head: (head, 0, 0)),
        ],
        out_shape=[
            jax.ShapeDtypeStruct((head_count, count, count), F32),
            jax.ShapeDtypeStruct((head_count, count, 2 * width), F32),
            jax.ShapeDtypeStruct((head_count, count, count), F32),
            jax.ShapeDtypeStruct((count, head_count * width), F32),
            jax.ShapeDtypeStruct((count, head_count * width), F32),
            jax.ShapeDtypeStruct((head_count, width, 2 * width), LOW),
        ],
        compiler_params=pltpu.CompilerParams(vmem_limit_bytes=VMEM_LIMIT),
    )(starts[:, None], starts[None, :], flags, betas, active, active, active)


def mixed_kernel(reach, local, state, gain, flags, mixed_out, head_out):
    mixed = local[...] + dot_three(reach[...], state[0].astype(F32))
    mixed_out[...] = mixed
    scale = lax.rsqrt(jnp.mean(mixed * mixed, axis=1, keepdims=True) + EPSILON)
    head_out[...] = (mixed * scale * gain[...] * flags[:, 2:3]).astype(LOW)


def mixed_call(reach, local, states, gain, flags):
    head_count, width = states.shape[0], states.shape[1]
    count = reach.shape[0]
    rows = pl.BlockSpec((count, width), lambda head: (0, head))
    return pl.pallas_call(
        mixed_kernel,
        grid=(head_count,),
        in_specs=[
            rows, rows,
            pl.BlockSpec((1, width, width), lambda head: (head, 0, 0)),
            pl.BlockSpec((1, width), lambda head: (0, 0)),
            pl.BlockSpec(flags.shape, lambda head: (0, 0)),
        ],
        out_specs=[rows, rows],
        out_shape=[
            jax.ShapeDtypeStruct(reach.shape, F32),
            jax.ShapeDtypeStruct(reach.shape, LOW),
        ],
        compiler_params=pltpu.CompilerParams(vmem_limit_bytes=VMEM_LIMIT),
    )(reach, local, states, gain[None], flags)


def pull_kernel(reach, mixed_in, grads, gain, flags, change, d_mixed_out, gain_out, pair_out):
    mixed, d_head, live = mixed_in[...], grads[...], flags[:, 2:3]
    width = mixed.shape[1]
    scale = lax.rsqrt(jnp.mean(mixed * mixed, axis=1, keepdims=True) + EPSILON)
    lifted = d_head * gain[...]
    inner = jnp.mean(lifted * mixed, axis=1, keepdims=True)
    d_mixed = live * (scale * lifted - mixed * (scale * scale * scale * inner))
    d_mixed_out[...] = d_mixed
    part = jnp.sum(d_head * mixed * (scale * live), axis=0, keepdims=True)

    @pl.when(pl.program_id(0) == 0)
    def _():
        gain_out[...] = jnp.zeros_like(gain_out)

    gain_out[...] += part
    pulled = dot_three(reach[...], d_mixed, FIRST_FIRST)
    turned = jnp.transpose(change[0, :, :width].astype(F32))
    pair_out[0] = jnp.concatenate([turned, pulled], axis=1).astype(LOW)


def pull_call(reach, mixed, grads, gain, flags, pairs):
    head_count, width = pairs.shape[0], pairs.shape[1]
    count = reach.shape[0]
    rows = pl.BlockSpec((count, width), lambda head: (0, head))
    pair = pl.BlockSpec((1, width, 2 * width), lambda head: (head, 0, 0))
    return pl.pallas_call(
        pull_kernel,
        grid=(head_count,),
        in_specs=[
            rows, rows, rows,
            pl.BlockSpec((1, width), lambda head: (0, 0)),
            pl.BlockSpec(flags.shape, lambda head: (0, 0)),
            pair,
        ],
        out_specs=[rows, pl.BlockSpec((1, width), lambda head: (0, 0)), pair],
        out_shape=[
            jax.ShapeDtypeStruct(reach.shape, F32),
            jax.ShapeDtypeStruct((1, width), F32),
            jax.ShapeDtypeStruct(pairs.shape, LOW),
        ],
        compiler_params=pltpu.CompilerParams(vmem_limit_bytes=VMEM_LIMIT),
    )(reach, mixed, grads, gain[None], flags, pairs)


def back_kernel(
    starts_col, starts_row, flags, betas, queries, keys, values,
    inverse_in, wy_in, scores_in, state_in, end_in, grads,
    d_query_out, d_key_out, d_value_out, d_beta_out,
):
    head = pl.program_id(0)
    count = queries.shape[0]
    width = queries.shape[1]
    row = lax.broadcasted_iota(jnp.int32, (count, count), 0)
    column = lax.broadcasted_iota(jnp.int32, (count, count), 1)
    same_doc = starts_col[...] == starts_row[...]
    first = flags[:, 0:1]
    last_part = flags[:, 1:2]
    beta = pick_lane(betas[...], head)
    query, query_scale = unit(queries[...])
    key, key_scale = unit(keys[...])
    value, grad = values[...], grads[...]
    inverse, wy, scores = inverse_in[0], wy_in[0], scores_in[0]
    state, end = state_in[0].astype(F32), end_in[0].astype(F32)
    fresh = wy[:, width:] - dot_three(wy[:, :width], state)
    d_fresh = dot_three(scores, grad, FIRST_FIRST) + dot_three(key * last_part, end)
    pulled = dot_three(inverse, d_fresh, FIRST_FIRST)
    both = jnp.concatenate([grad, pulled], axis=0)
    through_state = dot_three(both, state, ROWS_ROWS)
    through_fresh = dot_three(both, fresh, ROWS_ROWS)
    d_scores = jnp.where(same_doc & (row >= column), through_fresh[:count], 0.0)
    d_lower = jnp.where(same_doc & (row > column), -through_fresh[count:], 0.0)
    by_keys = dot_three(jnp.concatenate([d_scores, d_lower], axis=0), key)
    d_query = first * through_state[:count] + by_keys[:count]
    d_query_out[...] = unit_back(d_query, query, query_scale)
    recalled = -through_state[count:]
    row_part = by_keys[count:]
    d_key = (
        dot_three(d_scores, query, FIRST_FIRST)
        + dot_three(d_lower, beta * key, FIRST_FIRST)
        + last_part * dot_three(fresh, end, ROWS_ROWS)
        + (beta * first) * recalled
        + beta * row_part
    )
    d_key_out[...] = unit_back(d_key, key, key_scale)
    d_value_out[...] = beta * pulled
    d_beta = jnp.sum(
        (row_part + first * recalled) * key + pulled * value, axis=1, keepdims=True
    )

    @pl.when(head == 0)
    def _():
        d_beta_out[...] = jnp.zeros_like(d_beta_out)

    lane = lax.broadcasted_iota(jnp.int32, d_beta_out.shape, 1)
    d_beta_out[...] += jnp.where(lane == head, d_beta, 0.0)


def back_call(starts, flags, betas, active, inverse, wy, scores, states, ends, grads):
    head_count, width = states.shape[0], states.shape[1]
    count = active.shape[0]
    rows = pl.BlockSpec((count, width), lambda head: (0, head))
    whole = lambda shape: pl.BlockSpec(shape, lambda head: (0, 0))
    per_head = lambda shape: pl.BlockSpec((1,) + shape, lambda head: (head, 0, 0))
    return pl.pallas_call(
        back_kernel,
        grid=(head_count,),
        in_specs=[
            whole((count, 1)), whole((1, count)), whole(flags.shape), whole(betas.shape),
            *rows_specs(count, width, head_count),
            per_head((count, count)), per_head((count, 2 * width)), per_head((count, count)),
            per_head((width, width)), per_head((width, width)),
            rows,
        ],
        out_specs=[rows, rows, rows, whole(betas.shape)],
        out_shape=[jax.ShapeDtypeStruct(grads.shape, F32)] * 3
        + [jax.ShapeDtypeStruct(betas.shape, F32)],
        compiler_params=pltpu.CompilerParams(vmem_limit_bytes=VMEM_LIMIT),
    )(
        starts[:, None], starts[None, :], flags, betas, active, active, active, inverse, wy, scores,
        states, ends, grads,
    )


def apply_pair(change, pair):
    upper, rest = split_low(pair)
    product = functools.partial(jnp.dot, preferred_element_type=F32)
    return pair + (product(change, upper) + product(change, rest))


def scan_kernel(
    backwards, group_size, seq_size, pairs, states_out,
    got, total_sent, total_got, state_sent, arrived, send_sem, recv_sem,
):
    head_count, width = pairs.shape[0], pairs.shape[1]
    share = head_count // group_size
    my_seq, my_group = lax.axis_index("seq"), lax.axis_index("grp")
    peers = [lax.rem(my_group + step, group_size) for step in range(1, group_size)]
    bits = []
    while 2 ** len(bits) < seq_size:
        bits.append(2 ** len(bits))
    upper_half = [lax.rem(my_seq // bit, 2) for bit in bits]
    partners = [my_seq + bit - 2 * bit * half for bit, half in zip(bits, upper_half)]
    barrier = pltpu.get_barrier_semaphore()
    for peer in peers:
        pl.semaphore_signal(
            barrier, inc=1, device_id=(my_seq, peer), device_id_type=pl.DeviceIdType.MESH
        )
    for partner in partners:
        pl.semaphore_signal(
            barrier, inc=1, device_id=(partner, my_group), device_id_type=pl.DeviceIdType.MESH
        )
    pl.semaphore_wait(barrier, len(peers) + len(partners))

    def send(source, target, place, device):
        copy = pltpu.make_async_remote_copy(
            src_ref=source,
            dst_ref=target,
            send_sem=send_sem.at[place],
            recv_sem=recv_sem.at[place],
            device_id=device,
            device_id_type=pl.DeviceIdType.MESH,
        )
        copy.start()
        return copy

    mine = pl.ds(my_group * share, share)
    copies = [
        send(pairs.at[pl.ds(peer * share, share)], got.at[my_group], place, (my_seq, peer))
        for place, peer in enumerate(peers)
    ]
    got[my_group] = pairs[mine]
    for copy in copies:
        copy.wait()
    members = list(range(group_size))
    if backwards:
        members = members[::-1]
    eye = jnp.where(
        lax.broadcasted_iota(jnp.int32, (width, width), 0)
        == lax.broadcasted_iota(jnp.int32, (width, width), 1),
        1.0,
        0.0,
    )
    nothing = jnp.zeros((width, width), F32)
    start = jnp.concatenate([eye, nothing], axis=1)

    def added(pair):
        return jnp.concatenate([nothing, pair[:, width:].astype(F32)], axis=1)

    totals = []
    for head in range(share):
        total = start + got[members[0], head].astype(F32)
        for member in members[1:]:
            pair = got[member, head]
            total = apply_pair(pair[:, :width], total) + added(pair)
        totals.append(total)
    before = [start for _ in range(share)]
    for level, partner in enumerate(partners):
        for head in range(share):
            total_sent[level, head] = (totals[head] - start).astype(LOW)
        copy = send(
            total_sent.at[level],
            total_got.at[level],
            group_size - 1 + level,
            (partner, my_group),
        )
        copy.wait()
        later = upper_half[level] == (0 if backwards else 1)
        for head in range(share):
            theirs = total_got[level, head].astype(F32) + start
            first_pair = jnp.where(later, theirs, totals[head])
            second_pair = jnp.where(later, totals[head], theirs)
            moved = dot_three(
                jnp.concatenate([second_pair[:, :width], before[head][:, :width]], axis=0),
                first_pair,
            )
            totals[head] = moved[:width] + added(second_pair)
            before[head] = jnp.where(later, moved[width:] + added(before[head]), before[head])
    for head in range(share):
        state = before[head][:, width:]
        for member in members:
            state_sent[member, head] = state.astype(LOW)
            if member != members[-1]:
                pair = got[member, head]
                state = apply_pair(pair[:, :width], state) + pair[:, width:].astype(F32)
    place_now = group_size - 1 + len(bits)
    copies = [
        send(state_sent.at[peer], arrived.at[mine], place_now + place, (my_seq, peer))
        for place, peer in enumerate(peers)
    ]
    arrived[mine] = state_sent[my_group]
    for copy in copies:
        copy.wait()
    states_out[...] = arrived[...]


def scan_call(pairs, backwards, collective_id):
    head_count, width = pairs.shape[0], pairs.shape[1]
    group_size, seq_size = lax.axis_size("grp"), lax.axis_size("seq")
    share = head_count // group_size
    levels = (seq_size - 1).bit_length()
    sems = 2 * (group_size - 1) + levels
    return pl.pallas_call(
        functools.partial(scan_kernel, backwards, group_size, seq_size),
        in_specs=[pl.BlockSpec(memory_space=pltpu.VMEM)],
        out_specs=pl.BlockSpec(memory_space=pltpu.VMEM),
        out_shape=jax.ShapeDtypeStruct((head_count, width, width), LOW),
        scratch_shapes=[
            pltpu.VMEM((group_size, share, width, 2 * width), LOW),
            pltpu.VMEM((levels, share, width, 2 * width), LOW),
            pltpu.VMEM((levels, share, width, 2 * width), LOW),
            pltpu.VMEM((group_size, share, width, width), LOW),
            pltpu.VMEM((head_count, width, width), LOW),
            pltpu.SemaphoreType.DMA((sems,)),
            pltpu.SemaphoreType.DMA((sems,)),
        ],
        compiler_params=pltpu.CompilerParams(
            collective_id=collective_id, has_side_effects=True, vmem_limit_bytes=VMEM_LIMIT
        ),
    )(pairs)


def seq_bits():
    count = lax.axis_size("seq")
    bits = []
    bit = 1
    while bit < count:
        bits.append(bit)
        bit = bit * 2
    return bits


def phase_orders():
    bits = seq_bits()
    return (list(reversed(bits[1:])) + bits[:1], bits[1:] + bits[:1])


def masks_of(order):
    masks = [0]
    for bit in order:
        masks = masks + [mask ^ bit for mask in masks]
    return masks


def swapped(value, bit):
    count = lax.axis_size("seq")
    return lax.ppermute(value, "seq", [(place, place ^ bit) for place in range(count)])


def gathered(rows, order):
    pieces = [rows]
    for bit in order:
        pieces = pieces + [swapped(piece, bit) for piece in pieces]
    return jnp.concatenate(pieces, axis=0)


def fetch(shard):
    block = lax.all_gather(shard, "grp", axis=0, tiled=True)
    half = block.shape[1] // 2
    first, second = phase_orders()
    return (gathered(block[:, :half], first), gathered(block[:, half:], second))


def relative(values, order):
    count = lax.axis_size("seq")
    width = values.shape[1] // count
    mine = lax.axis_index("seq")
    return jnp.concatenate(
        [
            lax.dynamic_slice_in_dim(values, (mine ^ mask) * width, width, 1)
            for mask in masks_of(order)
        ],
        axis=1,
    )


def absolute(values, order):
    count = lax.axis_size("seq")
    width = values.shape[1] // count
    mine = lax.axis_index("seq")
    masks = masks_of(order)
    where_mask = jnp.array([masks.index(mask) for mask in range(count)], jnp.int32)
    return jnp.concatenate(
        [
            lax.dynamic_slice_in_dim(values, where_mask[mine ^ place] * width, width, 1)
            for place in range(count)
        ],
        axis=1,
    )


def relative_pair(values):
    first, second = phase_orders()
    return (relative(values, first), relative(values, second))


def absolute_pair(pair):
    first, second = phase_orders()
    return absolute(pair[0], first) + absolute(pair[1], second)


def outer(matrix, grads):
    return lax.dot_general(
        matrix, grads, (((0,), (0,)), ((), ())), preferred_element_type=jnp.float32
    )


def scattered(rel_rows, grads, order):
    half = rel_rows.shape[1] // 2
    lower = outer(rel_rows[:, half:], grads).astype(jnp.bfloat16)
    arrived = swapped(lower, order[-1])
    kept = (outer(rel_rows[:, :half], grads) + arrived.astype(jnp.float32)).astype(jnp.bfloat16)
    for bit in reversed(order[:-1]):
        half = kept.shape[0] // 2
        arrived = swapped(kept[half:], bit)
        kept = (kept[:half].astype(jnp.float32) + arrived.astype(jnp.float32)).astype(jnp.bfloat16)
    return kept


def weight_grad(rel_pair, grads):
    first, second = phase_orders()
    half = grads.shape[1] // 2
    kept = jnp.concatenate(
        [
            scattered(rel_pair[0], grads[:, :half], first),
            scattered(rel_pair[1], grads[:, half:], second),
        ],
        axis=1,
    )
    return lax.psum_scatter(kept, "grp", scatter_dimension=0, tiled=True).astype(jnp.float32)


def product_pair(rel_pair, weight_pair):
    return jnp.concatenate(
        [
            jnp.dot(rows, weight, preferred_element_type=jnp.float32)
            for rows, weight in zip(rel_pair, weight_pair)
        ],
        axis=1,
    )


def contract_pair(grads, weight_pair):
    half = grads.shape[1] // 2
    return (contract(grads[:, :half], weight_pair[0]), contract(grads[:, half:], weight_pair[1]))


def local(
    tokens,
    cotangent,
    lengths,
    pad_mask,
    mixer_gain,
    query_weight,
    key_weight,
    value_weight,
    conv_query,
    conv_key,
    conv_value,
    beta_weight,
    beta_bias,
    head_gain,
    out_weight,
    feed_gain,
    gate_weight,
    up_weight,
    down_weight,
):
    row_count, model_width = tokens.shape
    head_count = beta_bias.shape[0]
    head_width = head_gain.shape[0]
    tap_count = conv_query.shape[1]
    small = lax.all_gather(
        jnp.concatenate(
            [mixer_gain[:, None], feed_gain[:, None], conv_query, conv_key, conv_value, beta_weight],
            axis=1,
        ),
        ("seq", "grp"),
        axis=0,
        tiled=True,
    )
    gain_mixer, gain_feed = small[:, 0], small[:, 1]
    c_query = small[:, 2 : 2 + tap_count]
    c_key = small[:, 2 + tap_count : 2 + 2 * tap_count]
    c_value = small[:, 2 + 2 * tap_count : 2 + 3 * tap_count]
    w_beta = small[:, 2 + 3 * tap_count :]
    w_qkv = fetch(jnp.concatenate([query_weight, key_weight, value_weight], axis=1))
    w_out = fetch(out_weight)
    w_gate = fetch(gate_weight)
    w_up = fetch(up_weight)
    w_down = fetch(down_weight)
    anchor = lax.axis_index(("seq", "grp")) * row_count
    places = anchor + jnp.arange(row_count, dtype=jnp.int32)
    starts = jnp.cumsum(lengths) - lengths
    row_start = jnp.max(jnp.where(starts[None, :] <= places[:, None], starts[None, :], 0), axis=1)
    valid = jnp.stack(
        [(places - offset >= row_start).astype(jnp.float32) for offset in range(1, tap_count)]
    )
    live_rows = pad_mask.astype(jnp.float32)
    inputs32 = tokens.astype(jnp.float32)
    normed_a, norm_a_back = jax.vjp(rms_scale, inputs32, gain_mixer.astype(jnp.float32))
    normed_low = normed_a.astype(jnp.bfloat16)
    normed_rel = relative_pair(normed_low)
    own_pre = product_pair(normed_rel, w_qkv).astype(jnp.bfloat16)
    logit_part = jnp.dot(normed_low, w_beta, preferred_element_type=jnp.float32)
    sigmoid_val = jax.nn.sigmoid(logit_part + beta_bias)
    beta_rows = sigmoid_val * live_rows[:, None]
    earlier_rows = passed_along(own_pre[row_count - (tap_count - 1) :], ("seq", "grp"), 1)
    extended = jnp.concatenate([earlier_rows, own_pre], axis=0).astype(jnp.float32)
    kernel = jnp.concatenate([c_query, c_key, c_value], axis=0).astype(jnp.float32)

    def conv_act(padded, kernel_all):
        summed = padded[tap_count - 1 :] * kernel_all[:, tap_count - 1]
        for offset in range(1, tap_count):
            moved = padded[tap_count - 1 - offset : tap_count - 1 - offset + row_count]
            summed = (
                summed + moved * valid[offset - 1][:, None] * kernel_all[:, tap_count - 1 - offset]
            )
        return jax.nn.silu(summed)

    active, conv_pull = jax.vjp(conv_act, extended, kernel)
    flags = jnp.stack(
        [
            (row_start < anchor).astype(jnp.float32),
            (row_start == row_start[-1]).astype(jnp.float32),
            live_rows,
        ],
        axis=1,
    )
    inverse, wy, scores, reach, local_out, pairs = span_call(
        row_start, flags, beta_rows, active, head_count
    )
    start_states = scan_call(pairs, False, 0)
    mixed, head_low = mixed_call(reach, local_out, start_states, head_gain, flags)
    head_rel = relative_pair(head_low)
    hidden_one = inputs32 + product_pair(head_rel, w_out)
    normed_f, norm_f_back = jax.vjp(rms_scale, hidden_one, gain_feed.astype(jnp.float32))
    feed_low = normed_f.astype(jnp.bfloat16)
    feed_rel = relative_pair(feed_low)
    gate = product_pair(feed_rel, w_gate)
    upper = product_pair(feed_rel, w_up)
    gate_sig = jax.nn.sigmoid(gate)
    gate_act = gate * gate_sig
    inner_low = (gate_act * upper).astype(jnp.bfloat16)
    block_out = (hidden_one + absolute_pair(contract_pair(inner_low, w_down))).astype(jnp.bfloat16)
    grad_out = cotangent.astype(jnp.float32)
    cotangent_rel = relative_pair(cotangent)
    d_inner = product_pair(cotangent_rel, w_down)
    d_gate = (d_inner * upper * gate_sig * (1.0 + gate * (1.0 - gate_sig))).astype(jnp.bfloat16)
    d_upper = (d_inner * gate_act).astype(jnp.bfloat16)
    d_feed = absolute_pair(
        tuple(
            one + two
            for one, two in zip(contract_pair(d_gate, w_gate), contract_pair(d_upper, w_up))
        )
    )
    down_grad = weight_grad(cotangent_rel, inner_low)
    gate_grad = weight_grad(feed_rel, d_gate)
    up_grad = weight_grad(feed_rel, d_upper)
    d_hidden_part, d_gain_feed = norm_f_back(d_feed)
    d_hidden = grad_out + d_hidden_part
    d_attn = d_hidden.astype(jnp.bfloat16)
    d_head = absolute_pair(contract_pair(d_attn, w_out))
    out_grad = weight_grad(head_rel, d_attn)
    d_mixed, d_head_gain, back_pairs = pull_call(reach, mixed, d_head, head_gain, flags, pairs)
    end_states = scan_call(back_pairs, True, 1)
    d_queries, d_keys, d_values, d_betas = back_call(
        row_start,
        flags,
        beta_rows,
        active,
        inverse,
        wy,
        scores,
        start_states,
        end_states,
        d_mixed,
    )
    d_logit32 = d_betas * live_rows[:, None] * sigmoid_val * (1.0 - sigmoid_val)
    d_logit = d_logit32.astype(jnp.bfloat16)
    d_extended, d_kernel = conv_pull(jnp.concatenate([d_queries, d_keys, d_values], axis=1))
    from_next = passed_along(
        d_extended[: tap_count - 1].astype(jnp.bfloat16), ("seq", "grp"), -1
    ).astype(jnp.float32)
    d_own = d_extended[tap_count - 1 :] + jnp.pad(
        from_next, ((row_count - (tap_count - 1), 0), (0, 0))
    )
    d_pre = d_own.astype(jnp.bfloat16)
    d_normed = absolute_pair(contract_pair(d_pre, w_qkv)) + contract(d_logit, w_beta)
    qkv_grad = weight_grad(normed_rel, d_pre)
    d_input_part, d_gain_mixer = norm_a_back(d_normed)
    input_grad = (d_hidden + d_input_part).astype(jnp.bfloat16)
    replicated = jnp.sum(
        lax.all_gather(
            jnp.concatenate([d_head_gain[0], jnp.sum(d_logit32, axis=0)])[None],
            ("seq", "grp"),
            axis=0,
            tiled=True,
        ),
        axis=0,
    )
    sharded = lax.psum_scatter(
        jnp.concatenate(
            [
                outer(normed_low, d_logit),
                d_kernel[:model_width],
                d_kernel[model_width : 2 * model_width],
                d_kernel[2 * model_width :],
                d_gain_mixer[:, None],
                d_gain_feed[:, None],
            ],
            axis=1,
        ),
        ("seq", "grp"),
        scatter_dimension=0,
        tiled=True,
    )
    taps_at = head_count + 3 * tap_count
    return (
        block_out,
        input_grad,
        sharded[:, taps_at],
        qkv_grad[:, :model_width],
        qkv_grad[:, model_width : 2 * model_width],
        qkv_grad[:, 2 * model_width :],
        sharded[:, head_count : head_count + tap_count],
        sharded[:, head_count + tap_count : head_count + 2 * tap_count],
        sharded[:, head_count + 2 * tap_count : taps_at],
        sharded[:, :head_count],
        replicated[head_width:],
        replicated[:head_width],
        out_grad,
        sharded[:, taps_at + 1],
        gate_grad,
        up_grad,
        down_grad,
    )


def solution(mesh):
    placed = (
        P(("seq", "grp"), None),
        P(("seq", "grp"), None),
        P(),
        P(("seq", "grp")),
        P(("seq", "grp")),
        P(("seq", "grp"), None),
        P(("seq", "grp"), None),
        P(("seq", "grp"), None),
        P(("seq", "grp"), None),
        P(("seq", "grp"), None),
        P(("seq", "grp"), None),
        P(("seq", "grp"), None),
        P(),
        P(),
        P(("seq", "grp"), None),
        P(("seq", "grp")),
        P(("seq", "grp"), None),
        P(("seq", "grp"), None),
        P(("seq", "grp"), None),
    )
    return jax.shard_map(
        local,
        mesh=mesh,
        in_specs=placed,
        out_specs=(
            P(("seq", "grp"), None),
            P(("seq", "grp"), None),
            P(("seq", "grp")),
            P(("seq", "grp"), None),
            P(("seq", "grp"), None),
            P(("seq", "grp"), None),
            P(("seq", "grp"), None),
            P(("seq", "grp"), None),
            P(("seq", "grp"), None),
            P(("seq", "grp"), None),
            P(),
            P(),
            P(("seq", "grp"), None),
            P(("seq", "grp")),
            P(("seq", "grp"), None),
            P(("seq", "grp"), None),
            P(("seq", "grp"), None),
        ),
        check_vma=False,
    )
```

time: 6810 us -> 1840 us (0.27)
  waiting for transfers between devices: 5000 us -> 772 us
  matrix products: 883 us -> 237 us
  Pallas kernels: 0 us -> 274 us
  blocking collectives: 352 us -> 117 us
  local copies, waits for them, and re-layouts: 397 us -> 222 us
    reduce_scatter x1 -> x4, waiting for transfers between devices: 4260 us -> 6.38 us  [weight_grad(): lax.psum_scatter(kept, 'grp', scatter_dimension=0, tiled=True)]
    ppermute x0 -> x100, waiting for transfers between devices: none -> 673 us  [swapped(): lax.ppermute(value, 'seq', [(place, place ^ bit) for place in range(count)])]
    dot_general x373 -> x10, matrix products: 720 us -> 66.1 us  [product_pair(): jnp.dot(rows, weight, preferred_element_type=jnp.float32)]
    all_gather x15 -> x5, waiting for transfers between devices: 732 us -> 89.6 us  [fetch(): block = lax.all_gather(shard, 'grp', axis=0, tiled=True)]
    pallas_call x0 -> x6, Pallas kernels: none -> 274 us  [the longest x2 120 us: scan_call(): pl.pallas_call(functools.partial(scan_kernel, backwards, group_size, seq_...]
    concatenate x1 -> x29, local copies, waits for them, and re-layouts: 237 us -> 20.1 us  [the longest x10 10.3 us: gathered(): return jnp.concatenate(pieces, axis=0)]
    all_gather x4 -> x1, blocking collectives: 262 us -> 74.9 us  [local(): lax.all_gather(jnp.concatenate([mixer_gain[:, None], feed_gain[:, None],...]
    unnamed x239 -> x491, local copies, waits for them, and re-layouts: 34.1 us -> 156 us
  transfers between devices with their start and end apart: 18 -> 113, of which waited for: 11 -> 38; matrix products, arithmetic and copies ran while one was open for 6% -> 20% of each run, Pallas kernels for 0% -> 0%
where the time goes in v1:
time: 1840 us; the launch traced here: 1830 us
  waiting for transfers between devices  772 us (42%)
  Pallas kernels  274 us (15%)
  matrix products  237 us (13%)
  local copies, waits for them, and re-layouts  222 us (12%)
  blocking collectives  117 us (6%)
  other arithmetic  110 us (6%)
  starting transfers between devices  68.4 us (4%)
  between operations  27.6 us (2%)
    ppermute x100, waiting for transfers between devices, swapped(): lax.ppermute(value, 'seq', [(place, place ^ bit) for place in range(count)])  673 us
    unnamed x491, local copies, waits for them, and re-layouts  156 us
    pallas_call x2, Pallas kernels, scan_call(): pl.pallas_call(functools.partial(scan_kernel, backwards, group_size, seq_...  120 us
    pallas_call x1, Pallas kernels, span_call(): pl.pallas_call(span_kernel, grid=(head_count,), in_specs=[whole((count, 1...  94.7 us
    all_gather x5, waiting for transfers between devices, fetch(): block = lax.all_gather(shard, 'grp', axis=0, tiled=True)  89.6 us
    dot_general x11, matrix products, contract(): lax.dot_general(left, right, (((1,), (1,)), ((), ())), preferred_element_...  87 us
    dot_general x21, matrix products, outer(): lax.dot_general(matrix, grads, (((0,), (0,)), ((), ())), preferred_elemen...  81.7 us
    all_gather x1, blocking collectives, local(): lax.all_gather(jnp.concatenate([mixer_gain[:, None], feed_gain[:, None],...  74.9 us
  transfers between devices with their start and end apart: 113, of which 38 were waited for; matrix products, arithmetic and copies ran while one was open for 20% of the time, Pallas kernels for 0%

profile of v1, /device:TPU:0, one launch (start us, length us, event | category | flops | bytes accessed | tf_op | source)
XLA Modules:
  0.0 1827.8 jit_solution(10954069843505815296)
XLA Ops:
  14.0 74.9 %all-gather.1 = bf16[32,64,30]{1,2,0:T(8,128)(2,1)S(1)} all-gather(bf16[1,64,30]{1,2,0:T(8,128)(2,1)S(1)} %bitcast.121), channel_id=1, replica_groups=mesh['seq'=8,'grp'=4] {'seq','grp'}, dimensions={0}, use_global_device_ids=true | all-gather | bytes 126720 | tf_op jit(solution)/shard_map/all_gather | solution.py:601
  133.0 7.6 collective-permute-done.15
  163.9 7.1 collective-permute-done.24
  177.5 4.5 fusion.157
  186.1 4.5 fusion.159
  192.6 30.5 %all-gather.12.cloned.1.call-done = bf16[256,5632]{1,0:T(8,128)(2,1)} async-done(((bf16[64,5632]{1,0:T(8,128)(2,1)}), bf16[256,5632]{1,0:T(8,128)(2,1)}) %all-gather.12.cloned.1.call-update) | async-done | bytes 2883600 | tf_op jit(solution)/shard_map/all_gather | solution.py:486
  227.6 59.1 %all-gather.8.cloned.1.call-done = bf16[256,6144]{1,0:T(8,128)(2,1)} async-done(((bf16[64,6144]{1,0:T(8,128)(2,1)}), bf16[256,6144]{1,0:T(8,128)(2,1)}) %all-gather.8.cloned.1.call-update) | async-done | bytes 3145744 | tf_op jit(solution)/shard_map/all_gather | solution.py:486
  305.2 20.2 %collective-permute-done.43 = bf16[256,2816]{1,0:T(8,128)(2,1)S(1)} collective-permute-done((bf16[256,2816]{1,0:T(8,128)(2,1)}, bf16[256,2816]{1,0:T(8,128)(2,1)S(1)}, u32[]{:S(2)}, u32[]{:S(2)}) %collective-permute-start.43) | collective-permute-done | bytes 1441824 | tf_op jit(solution)/shard_map/ppermute | solution.py:475
  335.2 21.1 %collective-permute-done.51 = bf16[256,2816]{1,0:T(8,128)(2,1)S(1)} collective-permute-done((bf16[256,2816]{1,0:T(8,128)(2,1)S(1)}, bf16[256,2816]{1,0:T(8,128)(2,1)S(1)}, u32[]{:S(2)}, u32[]{:S(2)}) %collective-permute-start.51) | collective-permute-done | bytes 1441824 | tf_op jit(solution)/shard_map/ppermute | solution.py:475
  359.0 28.2 %collective-permute-done.29 = bf16[256,2816]{1,0:T(8,128)(2,1)S(1)} collective-permute-done((bf16[256,2816]{1,0:T(8,128)(2,1)S(1)}, bf16[256,2816]{1,0:T(8,128)(2,1)S(1)}, u32[]{:S(2)}, u32[]{:S(2)}) %collective-permute-start.29) | collective-permute-done | bytes 1441824 | tf_op jit(solution)/shard_map/ppermute | solution.py:475
  397.0 21.1 %collective-permute-done.37 = bf16[256,2816]{1,0:T(8,128)(2,1)S(1)} collective-permute-done((bf16[256,2816]{1,0:T(8,128)(2,1)S(1)}, bf16[256,2816]{1,0:T(8,128)(2,1)S(1)}, u32[]{:S(2)}, u32[]{:S(2)}) %collective-permute-start.37) | collective-permute-done | bytes 1441824 | tf_op jit(solution)/shard_map/ppermute | solution.py:475
  419.3 32.5 %collective-permute-done = bf16[256,3072]{1,0:T(8,128)(2,1)S(1)} collective-permute-done((bf16[256,3072]{1,0:T(8,128)(2,1)S(1)}, bf16[256,3072]{1,0:T(8,128)(2,1)S(1)}, u32[]{:S(2)}, u32[]{:S(2)}) %collective-permute-start) | collective-permute-done | bytes 1572896 | tf_op jit(solution)/shard_map/ppermute | solution.py:475
  461.3 24.2 %collective-permute-done.8 = bf16[256,3072]{1,0:T(8,128)(2,1)S(1)} collective-permute-done((bf16[256,3072]{1,0:T(8,128)(2,1)S(1)}, bf16[256,3072]{1,0:T(8,128)(2,1)S(1)}, u32[]{:S(2)}, u32[]{:S(2)}) %collective-permute-start.8) | collective-permute-done | bytes 1572896 | tf_op jit(solution)/shard_map/ppermute | solution.py:475
  486.9 28.4 %collective-permute-done.66 = bf16[256,2816]{1,0:T(8,128)(2,1)S(1)} collective-permute-done((bf16[256,2816]{1,0:T(8,128)(2,1)}, bf16[256,2816]{1,0:T(8,128)(2,1)S(1)}, u32[]{:S(2)}, u32[]{:S(2)}) %collective-permute-start.66) | collective-permute-done | bytes 1441824 | tf_op jit(solution)/shard_map/ppermute | solution.py:475
  522.2 25.6 %collective-permute-done.59 = bf16[256,2816]{1,0:T(8,128)(2,1)S(1)} collective-permute-done((bf16[256,2816]{1,0:T(8,128)(2,1)}, bf16[256,2816]{1,0:T(8,128)(2,1)S(1)}, u32[]{:S(2)}, u32[]{:S(2)}) %collective-permute-start.59) | collective-permute-done | bytes 1441824 | tf_op jit(solution)/shard_map/ppermute | solution.py:475
  554.7 24.6 %collective-permute-done.45 = bf16[256,2816]{1,0:T(8,128)(2,1)S(1)} collective-permute-done((bf16[256,2816]{1,0:T(8,128)(2,1)S(1)}, bf16[256,2816]{1,0:T(8,128)(2,1)S(1)}, u32[]{:S(2)}, u32[]{:S(2)}) %collective-permute-start.45) | collective-permute-done | bytes 1441824 | tf_op jit(solution)/shard_map/ppermute | solution.py:475
  586.5 23.4 %collective-permute-done.52 = bf16[256,2816]{1,0:T(8,128)(2,1)S(1)} collective-permute-done((bf16[256,2816]{1,0:T(8,128)(2,1)S(1)}, bf16[256,2816]{1,0:T(8,128)(2,1)S(1)}, u32[]{:S(2)}, u32[]{:S(2)}) %collective-permute-start.52) | collective-permute-done | bytes 1441824 | tf_op jit(solution)/shard_map/ppermute | solution.py:475
  616.7 22.8 %collective-permute-done.31 = bf16[256,2816]{1,0:T(8,128)(2,1)S(1)} collective-permute-done((bf16[256,2816]{1,0:T(8,128)(2,1)S(1)}, bf16[256,2816]{1,0:T(8,128)(2,1)S(1)}, u32[]{:S(2)}, u32[]{:S(2)}) %collective-permute-start.31) | collective-permute-done | bytes 1441824 | tf_op jit(solution)/shard_map/ppermute | solution.py:475
  647.8 20.4 %collective-permute-done.38 = bf16[256,2816]{1,0:T(8,128)(2,1)S(1)} collective-permute-done((bf16[256,2816]{1,0:T(8,128)(2,1)S(1)}, bf16[256,2816]{1,0:T(8,128)(2,1)S(1)}, u32[]{:S(2)}, u32[]{:S(2)}) %collective-permute-start.38) | collective-permute-done | bytes 1441824 | tf_op jit(solution)/shard_map/ppermute | solution.py:475
  675.0 6.5 collective-permute-done.2
  687.7 21.5 %collective-permute-done.9 = bf16[256,3072]{1,0:T(8,128)(2,1)S(1)} collective-permute-done((bf16[256,3072]{1,0:T(8,128)(2,1)S(1)}, bf16[256,3072]{1,0:T(8,128)(2,1)S(1)}, u32[]{:S(2)}, u32[]{:S(2)}) %collective-permute-start.9) | collective-permute-done | bytes 1572896 | tf_op jit(solution)/shard_map/ppermute | solution.py:475
  713.9 9.3 fusion.175
  725.9 9.3 fusion.176
  737.8 17.8 convolution_convert_fusion.9
  765.6 7.4 fusion.3
  773.0 94.7 %shard_map.386 = (f32[16,256,256]{2,1,0:T(8,128)}, f32[16,256,256]{2,1,0:T(8,128)}, f32[16,256,256]{2,1,0:T(8,128)}, f32[256,2048]{1,0:T(8,128)}, f32[256,2048]{1,0:T(8,128)}, /*index=5*/bf16[16,128,256]{2,1,0:T(8,128)(2,1)}) custom-call(s32[256,1]{1,0:T(8,128)} %copy.71.starts_col, s32[1,256]{1,0:T(1,128)} %bitcast.118, f32[256,3]{1,0:T(8,128)} %copy.72.flags, ...), custom_call_target="tpu_custom_call" | custom-call | tf_op jit(solution)/shard_map/pallas_call | solution.py:136
  867.7 63.4 %shard_map.387.state.state_in = bf16[16,128,128]{2,1,0:T(8,128)(2,1)} custom-call(bf16[16,128,256]{2,1,0:T(8,128)(2,1)} %get-tuple-element.34.pairs.change), custom_call_target="tpu_custom_call" | custom-call | tf_op jit(solution)/shard_map/pallas_call | solution.py:431
  931.1 12.4 shard_map.388
  954.5 4.8 fusion.174
  959.3 4.7 fusion.172
  964.0 9.2 fusion.173
  973.2 4.9 fusion.171
  978.1 8.8 multiply_convert_fusion.1
  987.0 11.3 fusion.35
  998.3 9.3 fusion.48
  1007.6 8.8 fusion.61
  1016.4 8.7 fusion.68
  1025.1 13.2 convolution_add_fusion
  1038.4 13.6 convolution_add_fusion.1
  1099.6 14.1 shard_map.389
  1113.7 57.0 %shard_map.390.end_in = bf16[16,128,128]{2,1,0:T(8,128)(2,1)} custom-call(bf16[16,128,256]{2,1,0:T(8,128)(2,1)} %get-tuple-element.40.pairs), custom_call_target="tpu_custom_call" | custom-call | tf_op jit(solution)/shard_map/pallas_call | solution.py:431
  1170.7 32.7 %shard_map.391 = (f32[256,2048]{1,0:T(8,128)}, f32[256,2048]{1,0:T(8,128)}, f32[256,2048]{1,0:T(8,128)}, f32[256,16]{1,0:T(8,128)}) custom-call(s32[256,1]{1,0:T(8,128)} %copy.71.starts_col, s32[1,256]{1,0:T(1,128)} %bitcast.119, f32[256,3]{1,0:T(8,128)} %copy.72.flags, f32[256,16]{1,0:T(8,128)} %get-tuple-element.265.betas, ...), custom_call_target="tpu_custom_call" | custom-call | tf_op jit(solution)/shard_map/pallas_call | solution.py:293
  1212.9 7.8 multiply_reduce_fusion.3
  1221.5 9.0 multiply_multiply_fusion.2
  1230.4 10.1 pad_add_fusion
  1246.0 4.6 collective-permute-start.93
  1251.8 7.6 fusion.24
  1259.6 6.5 fusion.17
  1313.9 62.2 %collective-permute-done.83 = bf16[256,1024]{0,1:T(8,128)(2,1)} collective-permute-done((bf16[256,1024]{0,1:T(8,128)(2,1)}, bf16[256,1024]{0,1:T(8,128)(2,1)}, u32[]{:S(2)}, u32[]{:S(2)}) %collective-permute-start.83) | collective-permute-done | bytes 524320 | tf_op jit(solution)/shard_map/ppermute | solution.py:475
  1376.5 4.5 convolution_convert_fusion.6
  1382.3 7.6 collective-permute-done.80
  1418.7 13.7 collective-permute-done.95
  1439.5 5.7 convolution_convert_fusion.7
  1445.2 53.3 %collective-permute-done.100 = bf16[512,2816]{1,0:T(8,128)(2,1)} collective-permute-done((bf16[512,2816]{1,0:T(8,128)(2,1)}, bf16[512,2816]{1,0:T(8,128)(2,1)}, u32[]{:S(2)}, u32[]{:S(2)}) %collective-permute-start.100) | collective-permute-done | bytes 2883616 | tf_op jit(solution)/shard_map/ppermute | solution.py:475
  1522.6 13.4 collective-permute-done.101
  1542.6 5.4 add_convert_fusion
  1552.7 48.5 %collective-permute-done.88 = bf16[512,2816]{1,0:T(8,128)(2,1)} collective-permute-done((bf16[512,2816]{1,0:T(8,128)(2,1)}, bf16[512,2816]{1,0:T(8,128)(2,1)}, u32[]{:S(2)}, u32[]{:S(2)}) %collective-permute-start.88) | collective-permute-done | bytes 2883616 | tf_op jit(solution)/shard_map/ppermute | solution.py:475
  1609.2 4.6 add_convert_fusion.1
  1616.5 21.9 %collective-permute-done.89 = bf16[256,2816]{1,0:T(8,128)(2,1)S(1)} collective-permute-done((bf16[256,2816]{1,0:T(8,128)(2,1)S(1)}, bf16[256,2816]{1,0:T(8,128)(2,1)S(1)}, u32[]{:S(2)}, u32[]{:S(2)}) %collective-permute-start.89) | collective-permute-done | bytes 1441824 | tf_op jit(solution)/shard_map/ppermute | solution.py:475
  1638.7 60.3 %collective-permute-done.86 = bf16[256,2816]{1,0:T(8,128)(2,1)S(1)} collective-permute-done((bf16[256,2816]{1,0:T(8,128)(2,1)S(1)}, bf16[256,2816]{1,0:T(8,128)(2,1)S(1)}, u32[]{:S(2)}, u32[]{:S(2)}) %collective-permute-start.86) | collective-permute-done | bytes 1441824 | tf_op jit(solution)/shard_map/ppermute | solution.py:475
  1711.6 29.9 %collective-permute-done.77 = bf16[256,3072]{1,0:T(8,128)(2,1)S(1)} collective-permute-done((bf16[256,3072]{1,0:T(8,128)(2,1)S(1)}, bf16[256,3072]{1,0:T(8,128)(2,1)S(1)}, u32[]{:S(2)}, u32[]{:S(2)}) %collective-permute-start.77) | collective-permute-done | bytes 1572896 | tf_op jit(solution)/shard_map/ppermute | solution.py:475
  1742.2 4.7 collective-permute-done.74
  1750.1 42.1 %all-reduce.9 = f32[4608]{0:T(1024)S(1)} all-reduce(f32[4608]{0:T(1024)S(1)} %maximum_dynamic-update-slice_fusion), channel_id=2, replica_groups=mesh['seq'=8,'grp'=4] {'seq','grp'}, use_global_device_ids=true, to_apply=%add.9 | all-reduce | flops 4608 | bytes 36864
  1812.1 6.4 reduce-scatter.11.cloned.1.call-done
  (855 shorter events, 446.2 us)
Async XLA Ops:
  7.3 116.2 %all-gather.10.cloned.1.call-start = ((), (), s32[]{:S(2)}) async-start(), calls=%async_computation.7 | async-start | bytes 1310720 | tf_op jit(solution)/shard_map/all_gather | solution.py:486
  8.0 169.5 %all-gather.16.cloned.1.call-start = ((), (), s32[]{:S(2)}) async-start(), calls=%async_computation.10 | async-start | bytes 3604480 | tf_op jit(solution)/shard_map/all_gather | solution.py:486
  8.8 177.3 %all-gather.14.cloned.1.call-start = ((), (), s32[]{:S(2)}) async-start(), calls=%async_computation.9 | async-start | bytes 3604480 | tf_op jit(solution)/shard_map/all_gather | solution.py:486
  9.5 213.6 %all-gather.12.cloned.1.call-start = ((), (), s32[]{:S(2)}) async-start(), calls=%async_computation.8 | async-start | bytes 3604480 | tf_op jit(solution)/shard_map/all_gather | solution.py:486
  10.1 276.7 %all-gather.8.cloned.1.call-start = ((), (), s32[]{:S(2)}) async-start(), calls=%async_computation.6 | async-start | bytes 3932160 | tf_op jit(solution)/shard_map/all_gather | solution.py:486
  12.2 1784.3 %reduce-scatter.19.cloned.1.call-start = ((), (), s32[]{:S(2)}) async-start(), calls=%async_computation.15 | async-start | bytes 1081344
  182.0 112.8 %collective-permute-start.65 = (bf16[256,2816]{1,0:T(8,128)(2,1)}, bf16[256,2816]{1,0:T(8,128)(2,1)}, u32[]{:S(2)}, u32[]{:S(2)}) collective-permute-start(bf16[256,2816]{1,0:T(8,128)(2,1)} %get-tuple-element.207), channel_id=1, source_target_pairs={{0,16},{4,20},{8,24},{12,28},{16,0},{20,4},{24,8},{28,12},{1,17},{... | collective-permute-start | bytes 4325384 | tf_op jit(solution)/shard_map/ppermute | solution.py:475
  183.5 107.3 %collective-permute-start.64 = (bf16[256,2816]{1,0:T(8,128)(2,1)}, bf16[256,2816]{1,0:T(8,128)(2,1)}, u32[]{:S(2)}, u32[]{:S(2)}) collective-permute-start(bf16[256,2816]{1,0:T(8,128)(2,1)} %get-tuple-element.207), channel_id=1, source_target_pairs={{0,8},{4,12},{8,0},{12,4},{16,24},{20,28},{24,16},{28,20},{1,9},{5... | collective-permute-start | bytes 4325384 | tf_op jit(solution)/shard_map/ppermute | solution.py:475
  185.5 116.5 %collective-permute-start.58 = (bf16[256,2816]{1,0:T(8,128)(2,1)}, bf16[256,2816]{1,0:T(8,128)(2,1)}, u32[]{:S(2)}, u32[]{:S(2)}) collective-permute-start(bf16[256,2816]{1,0:T(8,128)(2,1)} %get-tuple-element.210), channel_id=1, source_target_pairs={{0,8},{4,12},{8,0},{12,4},{16,24},{20,28},{24,16},{28,20},{1,9},{5... | collective-permute-start | bytes 4325384 | tf_op jit(solution)/shard_map/ppermute | solution.py:475
  185.5 112.5 %collective-permute-start.57 = (bf16[256,2816]{1,0:T(8,128)(2,1)}, bf16[256,2816]{1,0:T(8,128)(2,1)}, u32[]{:S(2)}, u32[]{:S(2)}) collective-permute-start(bf16[256,2816]{1,0:T(8,128)(2,1)} %get-tuple-element.210), channel_id=1, source_target_pairs={{0,16},{4,20},{8,24},{12,28},{16,0},{20,4},{24,8},{28,12},{1,17},{... | collective-permute-start | bytes 4325384 | tf_op jit(solution)/shard_map/ppermute | solution.py:475
  190.6 137.5 %collective-permute-start.44 = (bf16[256,2816]{1,0:T(8,128)(2,1)}, bf16[256,2816]{1,0:T(8,128)(2,1)S(1)}, u32[]{:S(2)}, u32[]{:S(2)}) collective-permute-start(bf16[256,2816]{1,0:T(8,128)(2,1)} %get-tuple-element.215), channel_id=1, source_target_pairs={{0,8},{4,12},{8,0},{12,4},{16,24},{20,28},{24,16},{28,20},{1,9},{5... | collective-permute-start | bytes 4325384 | tf_op jit(solution)/shard_map/ppermute | solution.py:475
  290.7 34.7 %collective-permute-start.43 = (bf16[256,2816]{1,0:T(8,128)(2,1)}, bf16[256,2816]{1,0:T(8,128)(2,1)S(1)}, u32[]{:S(2)}, u32[]{:S(2)}) collective-permute-start(bf16[256,2816]{1,0:T(8,128)(2,1)} %get-tuple-element.215), channel_id=1, source_target_pairs={{0,16},{4,20},{8,24},{12,28},{16,0},{20,4},{24,8},{28,12},{1,17},{... | collective-permute-start | bytes 4325384 | tf_op jit(solution)/shard_map/ppermute | solution.py:475
  294.8 61.5 %collective-permute-start.51 = (bf16[256,2816]{1,0:T(8,128)(2,1)S(1)}, bf16[256,2816]{1,0:T(8,128)(2,1)S(1)}, u32[]{:S(2)}, u32[]{:S(2)}) collective-permute-start(bf16[256,2816]{1,0:T(8,128)(2,1)S(1)} %copy-done.71), channel_id=1, source_target_pairs={{0,16},{4,20},{8,24},{12,28},{16,0},{20,4},{24,8},{28,12},{1,17},{... | collective-permute-start | bytes 4325384 | tf_op jit(solution)/shard_map/ppermute | solution.py:475
  298.0 34.5 %collective-permute-start.50 = (bf16[256,2816]{1,0:T(8,128)(2,1)S(1)}, bf16[256,2816]{1,0:T(8,128)(2,1)S(1)}, u32[]{:S(2)}, u32[]{:S(2)}) collective-permute-start(bf16[256,2816]{1,0:T(8,128)(2,1)S(1)} %copy-done.71), channel_id=1, source_target_pairs={{0,8},{4,12},{8,0},{12,4},{16,24},{20,28},{24,16},{28,20},{1,9},{5... | collective-permute-start | bytes 4325384 | tf_op jit(solution)/shard_map/ppermute | solution.py:475
  302.0 87.9 %collective-permute-start.30 = (bf16[256,2816]{1,0:T(8,128)(2,1)S(1)}, bf16[256,2816]{1,0:T(8,128)(2,1)S(1)}, u32[]{:S(2)}, u32[]{:S(2)}) collective-permute-start(bf16[256,2816]{1,0:T(8,128)(2,1)S(1)} %copy-done.70), channel_id=1, source_target_pairs={{0,8},{4,12},{8,0},{12,4},{16,24},{20,28},{24,16},{28,20},{1,9},{5... | collective-permute-start | bytes 4325384 | tf_op jit(solution)/shard_map/ppermute | solution.py:475
  325.4 61.8 %collective-permute-start.29 = (bf16[256,2816]{1,0:T(8,128)(2,1)S(1)}, bf16[256,2816]{1,0:T(8,128)(2,1)S(1)}, u32[]{:S(2)}, u32[]{:S(2)}) collective-permute-start(bf16[256,2816]{1,0:T(8,128)(2,1)S(1)} %copy-done.70), channel_id=1, source_target_pairs={{0,16},{4,20},{8,24},{12,28},{16,0},{20,4},{24,8},{28,12},{1,17},{... | collective-permute-start | bytes 4325384 | tf_op jit(solution)/shard_map/ppermute | solution.py:475
  328.1 90.0 %collective-permute-start.37 = (bf16[256,2816]{1,0:T(8,128)(2,1)S(1)}, bf16[256,2816]{1,0:T(8,128)(2,1)S(1)}, u32[]{:S(2)}, u32[]{:S(2)}) collective-permute-start(bf16[256,2816]{1,0:T(8,128)(2,1)S(1)} %copy-done.69), channel_id=1, source_target_pairs={{0,16},{4,20},{8,24},{12,28},{16,0},{20,4},{24,8},{28,12},{1,17},{... | collective-permute-start | bytes 4325384 | tf_op jit(solution)/shard_map/ppermute | solution.py:475
  332.5 61.8 %collective-permute-start.36 = (bf16[256,2816]{1,0:T(8,128)(2,1)S(1)}, bf16[256,2816]{1,0:T(8,128)(2,1)S(1)}, u32[]{:S(2)}, u32[]{:S(2)}) collective-permute-start(bf16[256,2816]{1,0:T(8,128)(2,1)S(1)} %copy-done.69), channel_id=1, source_target_pairs={{0,8},{4,12},{8,0},{12,4},{16,24},{20,28},{24,16},{28,20},{1,9},{5... | collective-permute-start | bytes 4325384 | tf_op jit(solution)/shard_map/ppermute | solution.py:475
  356.3 95.5 %collective-permute-start = (bf16[256,3072]{1,0:T(8,128)(2,1)S(1)}, bf16[256,3072]{1,0:T(8,128)(2,1)S(1)}, u32[]{:S(2)}, u32[]{:S(2)}) collective-permute-start(bf16[256,3072]{1,0:T(8,128)(2,1)S(1)} %get-tuple-element.203), channel_id=1, source_target_pairs={{0,16},{4,20},{8,24},{12,28},{16,0},{20,4},{24,8},{28,12},{1,17},{... | collective-permute-start | bytes 4718600 | tf_op jit(solution)/shard_map/ppermute | solution.py:475
  387.2 67.3 %collective-permute-start.1 = (bf16[256,3072]{1,0:T(8,128)(2,1)S(1)}, bf16[256,3072]{1,0:T(8,128)(2,1)S(1)}, u32[]{:S(2)}, u32[]{:S(2)}) collective-permute-start(bf16[256,3072]{1,0:T(8,128)(2,1)S(1)} %get-tuple-element.203), channel_id=1, source_target_pairs={{0,8},{4,12},{8,0},{12,4},{16,24},{20,28},{24,16},{28,20},{1,9},{5... | collective-permute-start | bytes 4718600 | tf_op jit(solution)/shard_map/ppermute | solution.py:475
  389.9 70.2 %collective-permute-start.7 = (bf16[256,3072]{1,0:T(8,128)(2,1)S(1)}, bf16[256,3072]{1,0:T(8,128)(2,1)S(1)}, u32[]{:S(2)}, u32[]{:S(2)}) collective-permute-start(bf16[256,3072]{1,0:T(8,128)(2,1)S(1)} %get-tuple-element.206), channel_id=1, source_target_pairs={{0,8},{4,12},{8,0},{12,4},{16,24},{20,28},{24,16},{28,20},{1,9},{5... | collective-permute-start | bytes 4718600 | tf_op jit(solution)/shard_map/ppermute | solution.py:475
  394.3 91.2 %collective-permute-start.8 = (bf16[256,3072]{1,0:T(8,128)(2,1)S(1)}, bf16[256,3072]{1,0:T(8,128)(2,1)S(1)}, u32[]{:S(2)}, u32[]{:S(2)}) collective-permute-start(bf16[256,3072]{1,0:T(8,128)(2,1)S(1)} %get-tuple-element.206), channel_id=1, source_target_pairs={{0,16},{4,20},{8,24},{12,28},{16,0},{20,4},{24,8},{28,12},{1,17},{... | collective-permute-start | bytes 4718600 | tf_op jit(solution)/shard_map/ppermute | solution.py:475
  418.1 99.9 %collective-permute-start.67 = (bf16[256,2816]{1,0:T(8,128)(2,1)}, bf16[256,2816]{1,0:T(8,128)(2,1)S(1)}, u32[]{:S(2)}, u32[]{:S(2)}) collective-permute-start(bf16[256,2816]{1,0:T(8,128)(2,1)} %get-tuple-element.207), channel_id=1, source_target_pairs={{0,4},{4,0},{8,12},{12,8},{16,20},{20,16},{24,28},{28,24},{1,5},{5... | collective-permute-start | bytes 4325384 | tf_op jit(solution)/shard_map/ppermute | solution.py:475
  451.8 63.4 %collective-permute-start.66 = (bf16[256,2816]{1,0:T(8,128)(2,1)}, bf16[256,2816]{1,0:T(8,128)(2,1)S(1)}, u32[]{:S(2)}, u32[]{:S(2)}) collective-permute-start(bf16[256,2816]{1,0:T(8,128)(2,1)} %collective-permute-done.64), channel_id=1, source_target_pairs={{0,16},{4,20},{8,24},{12,28},{16,0},{20,4},{24,8},{28,12},{1,17},{... | collective-permute-start | bytes 4325384 | tf_op jit(solution)/shard_map/ppermute | solution.py:475
  454.6 96.0 %collective-permute-start.60 = (bf16[256,2816]{1,0:T(8,128)(2,1)}, bf16[256,2816]{1,0:T(8,128)(2,1)S(1)}, u32[]{:S(2)}, u32[]{:S(2)}) collective-permute-start(bf16[256,2816]{1,0:T(8,128)(2,1)} %get-tuple-element.210), channel_id=1, source_target_pairs={{0,4},{4,0},{8,12},{12,8},{16,20},{20,16},{24,28},{28,24},{1,5},{5... | collective-permute-start | bytes 4325384 | tf_op jit(solution)/shard_map/ppermute | solution.py:475
  460.1 59.1 %collective-permute-start.68 = (bf16[256,2816]{1,0:T(8,128)(2,1)}, bf16[256,2816]{1,0:T(8,128)(2,1)S(1)}, u32[]{:S(2)}, u32[]{:S(2)}) collective-permute-start(bf16[256,2816]{1,0:T(8,128)(2,1)} %collective-permute-done.64), channel_id=1, source_target_pairs={{0,4},{4,0},{8,12},{12,8},{16,20},{20,16},{24,28},{28,24},{1,5},{5... | collective-permute-start | bytes 4325384 | tf_op jit(solution)/shard_map/ppermute | solution.py:475
  485.5 35.4 %collective-permute-start.69 = (bf16[256,2816]{1,0:T(8,128)(2,1)}, bf16[256,2816]{1,0:T(8,128)(2,1)S(1)}, u32[]{:S(2)}, u32[]{:S(2)}) collective-permute-start(bf16[256,2816]{1,0:T(8,128)(2,1)} %collective-permute-done.65), channel_id=1, source_target_pairs={{0,4},{4,0},{8,12},{12,8},{16,20},{20,16},{24,28},{28,24},{1,5},{5... | collective-permute-start | bytes 4325384 | tf_op jit(solution)/shard_map/ppermute | solution.py:475
  518.0 64.0 %collective-permute-start.46 = (bf16[256,2816]{1,0:T(8,128)(2,1)}, bf16[256,2816]{1,0:T(8,128)(2,1)S(1)}, u32[]{:S(2)}, u32[]{:S(2)}) collective-permute-start(bf16[256,2816]{1,0:T(8,128)(2,1)} %get-tuple-element.215), channel_id=1, source_target_pairs={{0,4},{4,0},{8,12},{12,8},{16,20},{20,16},{24,28},{28,24},{1,5},{5... | collective-permute-start | bytes 4325384 | tf_op jit(solution)/shard_map/ppermute | solution.py:475
  550.5 62.1 %collective-permute-start.53 = (bf16[256,2816]{1,0:T(8,128)(2,1)S(1)}, bf16[256,2816]{1,0:T(8,128)(2,1)S(1)}, u32[]{:S(2)}, u32[]{:S(2)}) collective-permute-start(bf16[256,2816]{1,0:T(8,128)(2,1)S(1)} %copy-done.71), channel_id=1, source_target_pairs={{0,4},{4,0},{8,12},{12,8},{16,20},{20,16},{24,28},{28,24},{1,5},{5... | collective-permute-start | bytes 4325384 | tf_op jit(solution)/shard_map/ppermute | solution.py:475
  582.0 60.3 %collective-permute-start.32 = (bf16[256,2816]{1,0:T(8,128)(2,1)S(1)}, bf16[256,2816]{1,0:T(8,128)(2,1)S(1)}, u32[]{:S(2)}, u32[]{:S(2)}) collective-permute-start(bf16[256,2816]{1,0:T(8,128)(2,1)S(1)} %copy-done.70), channel_id=1, source_target_pairs={{0,4},{4,0},{8,12},{12,8},{16,20},{20,16},{24,28},{28,24},{1,5},{5... | collective-permute-start | bytes 4325384 | tf_op jit(solution)/shard_map/ppermute | solution.py:475
  612.6 56.9 %collective-permute-start.39 = (bf16[256,2816]{1,0:T(8,128)(2,1)S(1)}, bf16[256,2816]{1,0:T(8,128)(2,1)S(1)}, u32[]{:S(2)}, u32[]{:S(2)}) collective-permute-start(bf16[256,2816]{1,0:T(8,128)(2,1)S(1)} %copy-done.69), channel_id=1, source_target_pairs={{0,4},{4,0},{8,12},{12,8},{16,20},{20,16},{24,28},{28,24},{1,5},{5... | collective-permute-start | bytes 4325384 | tf_op jit(solution)/shard_map/ppermute | solution.py:475
  645.2 36.3 %collective-permute-start.2 = (bf16[256,3072]{1,0:T(8,128)(2,1)S(1)}, bf16[256,3072]{1,0:T(8,128)(2,1)S(1)}, u32[]{:S(2)}, u32[]{:S(2)}) collective-permute-start(bf16[256,3072]{1,0:T(8,128)(2,1)S(1)} %collective-permute-done), channel_id=1, source_target_pairs={{0,8},{4,12},{8,0},{12,4},{16,24},{20,28},{24,16},{28,20},{1,9},{5... | collective-permute-start | bytes 4718600 | tf_op jit(solution)/shard_map/ppermute | solution.py:475
  672.4 36.8 %collective-permute-start.9 = (bf16[256,3072]{1,0:T(8,128)(2,1)S(1)}, bf16[256,3072]{1,0:T(8,128)(2,1)S(1)}, u32[]{:S(2)}, u32[]{:S(2)}) collective-permute-start(bf16[256,3072]{1,0:T(8,128)(2,1)S(1)} %collective-permute-done.7), channel_id=1, source_target_pairs={{0,16},{4,20},{8,24},{12,28},{16,0},{20,4},{24,8},{28,12},{1,17},{... | collective-permute-start | bytes 4718600 | tf_op jit(solution)/shard_map/ppermute | solution.py:475
  710.9 51.8 %collective-permute-start.42 = (bf16[256,2816]{1,0:T(8,128)(2,1)S(1)}, bf16[256,2816]{1,0:T(8,128)(2,1)S(1)}, u32[]{:S(2)}, u32[]{:S(2)}) collective-permute-start(bf16[256,2816]{1,0:T(8,128)(2,1)S(1)} %collective-permute-done.38), channel_id=1, source_target_pairs={{0,4},{4,0},{8,12},{12,8},{16,20},{20,16},{24,28},{28,24},{1,5},{5... | collective-permute-start | bytes 4325384 | tf_op jit(solution)/shard_map/ppermute | solution.py:475
  1206.0 60.4 %collective-permute-start.81 = (bf16[1024,1024]{0,1:T(8,128)(2,1)}, bf16[1024,1024]{0,1:T(8,128)(2,1)}, u32[]{:S(2)}, u32[]{:S(2)}) collective-permute-start(bf16[1024,1024]{0,1:T(8,128)(2,1)} %convolution_convert_fusion.10), channel_id=1, source_target_pairs={{0,4},{4,0},{8,12},{12,8},{16,20},{20,16},{24,28},{28,24},{1,5},{5... | collective-permute-start | bytes 6291464 | tf_op jit(solution)/shard_map/ppermute | solution.py:475
  1206.0 63.9 %collective-permute-start.78 = (bf16[1024,1024]{0,1:T(8,128)(2,1)}, bf16[1024,1024]{0,1:T(8,128)(2,1)}, u32[]{:S(2)}, u32[]{:S(2)}) collective-permute-start(bf16[1024,1024]{0,1:T(8,128)(2,1)} %convolution_convert_fusion.11), channel_id=1, source_target_pairs={{0,4},{4,0},{8,12},{12,8},{16,20},{20,16},{24,28},{28,24},{1,5},{5... | collective-permute-start | bytes 6291464 | tf_op jit(solution)/shard_map/ppermute | solution.py:475
  1250.5 150.6 %collective-permute-start.99 = (bf16[1024,2816]{1,0:T(8,128)(2,1)}, bf16[1024,2816]{1,0:T(8,128)(2,1)}, u32[]{:S(2)}, u32[]{:S(2)}) collective-permute-start(bf16[1024,2816]{1,0:T(8,128)(2,1)} %convolution_convert_fusion), channel_id=1, source_target_pairs={{0,4},{4,0},{8,12},{12,8},{16,20},{20,16},{24,28},{28,24},{1,5},{5... | collective-permute-start | bytes 17301512 | tf_op jit(solution)/shard_map/ppermute | solution.py:475
  1266.4 144.1 %collective-permute-start.96 = (bf16[1024,2816]{1,0:T(8,128)(2,1)}, bf16[1024,2816]{1,0:T(8,128)(2,1)}, u32[]{:S(2)}, u32[]{:S(2)}) collective-permute-start(bf16[1024,2816]{1,0:T(8,128)(2,1)} %convolution_convert_fusion.1), channel_id=1, source_target_pairs={{0,4},{4,0},{8,12},{12,8},{16,20},{20,16},{24,28},{28,24},{1,5},{5... | collective-permute-start | bytes 17301512 | tf_op jit(solution)/shard_map/ppermute | solution.py:475
  1284.2 109.2 %collective-permute-start.94 = (bf16[512,2816]{1,0:T(8,128)(2,1)}, bf16[512,2816]{1,0:T(8,128)(2,1)}, u32[]{:S(2)}, u32[]{:S(2)}) collective-permute-start(bf16[512,2816]{1,0:T(8,128)(2,1)} %slice.492), channel_id=1, source_target_pairs={{0,16},{4,20},{8,24},{12,28},{16,0},{20,4},{24,8},{28,12},{1,17},{... | collective-permute-start | bytes 8650760 | tf_op jit(solution)/shard_map/ppermute | solution.py:475
  1296.7 100.8 %collective-permute-start.91 = (bf16[512,2816]{1,0:T(8,128)(2,1)}, bf16[512,2816]{1,0:T(8,128)(2,1)}, u32[]{:S(2)}, u32[]{:S(2)}) collective-permute-start(bf16[512,2816]{1,0:T(8,128)(2,1)} %slice.488), channel_id=1, source_target_pairs={{0,8},{4,12},{8,0},{12,4},{16,24},{20,28},{24,16},{28,20},{1,9},{5... | collective-permute-start | bytes 8650760 | tf_op jit(solution)/shard_map/ppermute | solution.py:475
  1301.2 74.9 %collective-permute-start.83 = (bf16[256,1024]{0,1:T(8,128)(2,1)}, bf16[256,1024]{0,1:T(8,128)(2,1)}, u32[]{:S(2)}, u32[]{:S(2)}) collective-permute-start(bf16[256,1024]{0,1:T(8,128)(2,1)} %slice.477), channel_id=1, source_target_pairs={{0,8},{4,12},{8,0},{12,4},{16,24},{20,28},{24,16},{28,20},{1,9},{5... | collective-permute-start | bytes 1572872 | tf_op jit(solution)/shard_map/ppermute | solution.py:475
  1311.7 491.2 %reduce-scatter.21.cloned.1.call-start = ((), (), s32[]{:S(2)}) async-start(), calls=%async_computation.16 | async-start | bytes 1310720
  1389.9 115.0 %collective-permute-start.87 = (bf16[1024,2816]{1,0:T(8,128)(2,1)}, bf16[1024,2816]{1,0:T(8,128)(2,1)}, u32[]{:S(2)}, u32[]{:S(2)}) collective-permute-start(bf16[1024,2816]{1,0:T(8,128)(2,1)} %convolution_convert_fusion.4), channel_id=1, source_target_pairs={{0,4},{4,0},{8,12},{12,8},{16,20},{20,16},{24,28},{28,24},{1,5},{5... | collective-permute-start | bytes 17301512 | tf_op jit(solution)/shard_map/ppermute | solution.py:475
  1393.4 411.8 %reduce-scatter.15.cloned.1.call-start = ((), (), s32[]{:S(2)}) async-start(), calls=%async_computation.13 | async-start | bytes 3604480 | tf_op jit(solution)/shard_map/reduce_scatter | solution.py:558
  1393.4 121.1 %collective-permute-start.84 = (bf16[1024,2816]{1,0:T(8,128)(2,1)}, bf16[1024,2816]{1,0:T(8,128)(2,1)}, u32[]{:S(2)}, u32[]{:S(2)}) collective-permute-start(bf16[1024,2816]{1,0:T(8,128)(2,1)} %convolution_convert_fusion.5), channel_id=1, source_target_pairs={{0,4},{4,0},{8,12},{12,8},{16,20},{20,16},{24,28},{28,24},{1,5},{5... | collective-permute-start | bytes 17301512 | tf_op jit(solution)/shard_map/ppermute | solution.py:475
  1397.4 34.9 %collective-permute-start.95 = (bf16[256,2816]{1,0:T(8,128)(2,1)S(1)}, bf16[256,2816]{1,0:T(8,128)(2,1)S(1)}, u32[]{:S(2)}, u32[]{:S(2)}) collective-permute-start(bf16[256,2816]{1,0:T(8,128)(2,1)S(1)} %slice.494), channel_id=1, source_target_pairs={{0,8},{4,12},{8,0},{12,4},{16,24},{20,28},{24,16},{28,20},{1,9},{5... | collective-permute-start | bytes 4325384 | tf_op jit(solution)/shard_map/ppermute | solution.py:475
  1401.1 35.9 %collective-permute-start.92 = (bf16[256,2816]{1,0:T(8,128)(2,1)S(1)}, bf16[256,2816]{1,0:T(8,128)(2,1)S(1)}, u32[]{:S(2)}, u32[]{:S(2)}) collective-permute-start(bf16[256,2816]{1,0:T(8,128)(2,1)S(1)} %slice.490), channel_id=1, source_target_pairs={{0,16},{4,20},{8,24},{12,28},{16,0},{20,4},{24,8},{28,12},{1,17},{... | collective-permute-start | bytes 4325384 | tf_op jit(solution)/shard_map/ppermute | solution.py:475
  1410.5 88.0 %collective-permute-start.100 = (bf16[512,2816]{1,0:T(8,128)(2,1)}, bf16[512,2816]{1,0:T(8,128)(2,1)}, u32[]{:S(2)}, u32[]{:S(2)}) collective-permute-start(bf16[512,2816]{1,0:T(8,128)(2,1)} %slice.500), channel_id=1, source_target_pairs={{0,16},{4,20},{8,24},{12,28},{16,0},{20,4},{24,8},{28,12},{1,17},{... | collective-permute-start | bytes 8650760 | tf_op jit(solution)/shard_map/ppermute | solution.py:475
  1432.4 69.6 %collective-permute-start.97 = (bf16[512,2816]{1,0:T(8,128)(2,1)}, bf16[512,2816]{1,0:T(8,128)(2,1)}, u32[]{:S(2)}, u32[]{:S(2)}) collective-permute-start(bf16[512,2816]{1,0:T(8,128)(2,1)} %slice.496), channel_id=1, source_target_pairs={{0,8},{4,12},{8,0},{12,4},{16,24},{20,28},{24,16},{28,20},{1,9},{5... | collective-permute-start | bytes 8650760 | tf_op jit(solution)/shard_map/ppermute | solution.py:475
  1437.0 104.8 %collective-permute-start.75 = (bf16[1024,3072]{1,0:T(8,128)(2,1)}, bf16[1024,3072]{1,0:T(8,128)(2,1)}, u32[]{:S(2)}, u32[]{:S(2)}) collective-permute-start(bf16[1024,3072]{1,0:T(8,128)(2,1)} %convolution_convert_fusion.6), channel_id=1, source_target_pairs={{0,4},{4,0},{8,12},{12,8},{16,20},{20,16},{24,28},{28,24},{1,5},{5... | collective-permute-start | bytes 18874376 | tf_op jit(solution)/shard_map/ppermute | solution.py:475
  1439.2 368.2 %reduce-scatter.17.cloned.1.call-start = ((), (), s32[]{:S(2)}) async-start(), calls=%async_computation.14 | async-start | bytes 3604480 | tf_op jit(solution)/shard_map/reduce_scatter | solution.py:558
  1498.5 110.7 %collective-permute-start.72 = (bf16[1024,3072]{1,0:T(8,128)(2,1)}, bf16[1024,3072]{1,0:T(8,128)(2,1)}, u32[]{:S(2)}, u32[]{:S(2)}) collective-permute-start(bf16[1024,3072]{1,0:T(8,128)(2,1)} %convolution_convert_fusion.7), channel_id=1, source_target_pairs={{0,4},{4,0},{8,12},{12,8},{16,20},{20,16},{24,28},{28,24},{1,5},{5... | collective-permute-start | bytes 18874376 | tf_op jit(solution)/shard_map/ppermute | solution.py:475
  1502.0 34.1 %collective-permute-start.101 = (bf16[256,2816]{1,0:T(8,128)(2,1)S(1)}, bf16[256,2816]{1,0:T(8,128)(2,1)S(1)}, u32[]{:S(2)}, u32[]{:S(2)}) collective-permute-start(bf16[256,2816]{1,0:T(8,128)(2,1)S(1)} %slice.502), channel_id=1, source_target_pairs={{0,8},{4,12},{8,0},{12,4},{16,24},{20,28},{24,16},{28,20},{1,9},{5... | collective-permute-start | bytes 4325384 | tf_op jit(solution)/shard_map/ppermute | solution.py:475
  1504.9 34.4 %collective-permute-start.98 = (bf16[256,2816]{1,0:T(8,128)(2,1)S(1)}, bf16[256,2816]{1,0:T(8,128)(2,1)S(1)}, u32[]{:S(2)}, u32[]{:S(2)}) collective-permute-start(bf16[256,2816]{1,0:T(8,128)(2,1)S(1)} %slice.498), channel_id=1, source_target_pairs={{0,16},{4,20},{8,24},{12,28},{16,0},{20,4},{24,8},{28,12},{1,17},{... | collective-permute-start | bytes 4325384 | tf_op jit(solution)/shard_map/ppermute | solution.py:475
  1514.6 86.7 %collective-permute-start.88 = (bf16[512,2816]{1,0:T(8,128)(2,1)}, bf16[512,2816]{1,0:T(8,128)(2,1)}, u32[]{:S(2)}, u32[]{:S(2)}) collective-permute-start(bf16[512,2816]{1,0:T(8,128)(2,1)} %slice.484), channel_id=1, source_target_pairs={{0,16},{4,20},{8,24},{12,28},{16,0},{20,4},{24,8},{28,12},{1,17},{... | collective-permute-start | bytes 8650760 | tf_op jit(solution)/shard_map/ppermute | solution.py:475
  1536.0 69.9 %collective-permute-start.85 = (bf16[512,2816]{1,0:T(8,128)(2,1)}, bf16[512,2816]{1,0:T(8,128)(2,1)}, u32[]{:S(2)}, u32[]{:S(2)}) collective-permute-start(bf16[512,2816]{1,0:T(8,128)(2,1)} %slice.480), channel_id=1, source_target_pairs={{0,8},{4,12},{8,0},{12,4},{16,24},{20,28},{24,16},{28,20},{1,9},{5... | collective-permute-start | bytes 8650760 | tf_op jit(solution)/shard_map/ppermute | solution.py:475
  1541.5 268.2 %reduce-scatter.13.cloned.1.call-start = ((), (), s32[]{:S(2)}) async-start(), calls=%async_computation.12 | async-start | bytes 3604480 | tf_op jit(solution)/shard_map/reduce_scatter | solution.py:558
  1552.6 148.6 %collective-permute-start.76 = (bf16[512,3072]{1,0:T(8,128)(2,1)}, bf16[512,3072]{1,0:T(8,128)(2,1)}, u32[]{:S(2)}, u32[]{:S(2)}) collective-permute-start(bf16[512,3072]{1,0:T(8,128)(2,1)} %slice.460), channel_id=1, source_target_pairs={{0,16},{4,20},{8,24},{12,28},{16,0},{20,4},{24,8},{28,12},{1,17},{... | collective-permute-start | bytes 9437192 | tf_op jit(solution)/shard_map/ppermute | solution.py:475
  1603.8 34.6 %collective-permute-start.89 = (bf16[256,2816]{1,0:T(8,128)(2,1)S(1)}, bf16[256,2816]{1,0:T(8,128)(2,1)S(1)}, u32[]{:S(2)}, u32[]{:S(2)}) collective-permute-start(bf16[256,2816]{1,0:T(8,128)(2,1)S(1)} %slice.486), channel_id=1, source_target_pairs={{0,8},{4,12},{8,0},{12,4},{16,24},{20,28},{24,16},{28,20},{1,9},{5... | collective-permute-start | bytes 4325384 | tf_op jit(solution)/shard_map/ppermute | solution.py:475
  1608.8 90.2 %collective-permute-start.86 = (bf16[256,2816]{1,0:T(8,128)(2,1)S(1)}, bf16[256,2816]{1,0:T(8,128)(2,1)S(1)}, u32[]{:S(2)}, u32[]{:S(2)}) collective-permute-start(bf16[256,2816]{1,0:T(8,128)(2,1)S(1)} %slice.482), channel_id=1, source_target_pairs={{0,16},{4,20},{8,24},{12,28},{16,0},{20,4},{24,8},{28,12},{1,17},{... | collective-permute-start | bytes 4325384 | tf_op jit(solution)/shard_map/ppermute | solution.py:475
  1616.5 90.7 %collective-permute-start.73 = (bf16[512,3072]{1,0:T(8,128)(2,1)S(1)}, bf16[512,3072]{1,0:T(8,128)(2,1)}, u32[]{:S(2)}, u32[]{:S(2)}) collective-permute-start(bf16[512,3072]{1,0:T(8,128)(2,1)S(1)} %slice.456), channel_id=1, source_target_pairs={{0,8},{4,12},{8,0},{12,4},{16,24},{20,28},{24,16},{28,20},{1,9},{5... | collective-permute-start | bytes 9437192 | tf_op jit(solution)/shard_map/ppermute | solution.py:475
  1701.2 117.3 %reduce-scatter.11.cloned.1.call-start = ((), (), s32[]{:S(2)}) async-start(), calls=%async_computation.11 | async-start | bytes 3932160 | tf_op jit(solution)/shard_map/reduce_scatter | solution.py:558
  1705.4 36.2 %collective-permute-start.77 = (bf16[256,3072]{1,0:T(8,128)(2,1)S(1)}, bf16[256,3072]{1,0:T(8,128)(2,1)S(1)}, u32[]{:S(2)}, u32[]{:S(2)}) collective-permute-start(bf16[256,3072]{1,0:T(8,128)(2,1)S(1)} %slice.462), channel_id=1, source_target_pairs={{0,8},{4,12},{8,0},{12,4},{16,24},{20,28},{24,16},{28,20},{1,9},{5... | collective-permute-start | bytes 4718600 | tf_op jit(solution)/shard_map/ppermute | solution.py:475
  1711.2 35.6 %collective-permute-start.74 = (bf16[256,3072]{1,0:T(8,128)(2,1)S(1)}, bf16[256,3072]{1,0:T(8,128)(2,1)S(1)}, u32[]{:S(2)}, u32[]{:S(2)}) collective-permute-start(bf16[256,3072]{1,0:T(8,128)(2,1)S(1)} %slice.458), channel_id=1, source_target_pairs={{0,16},{4,20},{8,24},{12,28},{16,0},{20,4},{24,8},{28,12},{1,17},{... | collective-permute-start | bytes 4718600 | tf_op jit(solution)/shard_map/ppermute | solution.py:475
  (202 other events, 3582.1 us)
Sparse Core Ops, SparseCore 0:
  9.7 32.4 all-gather.9
  43.7 60.5 all-gather.15
  105.9 57.8 all-gather.13
  165.2 57.8 all-gather.11
  224.5 62.1 all-gather.7
  1311.8 136.4 reduce-scatter.18
  1451.3 23.3 reduce-scatter.20
  1476.9 54.8 reduce-scatter.14
  1541.7 54.2 reduce-scatter.16
  1701.3 53.8 reduce-scatter.12
  1757.6 60.8 reduce-scatter.10

commit v2 on v1

--- a/solution.py
+++ b/solution.py
@@ -27,6 +27,24 @@
     return lax.dot_general(
         left, right, (((1,), (1,)), ((), ())), preferred_element_type=jnp.float32
     )
+
+
+def launch(kernel, after, in_specs, operands, **options):
+    count = len(after)
+
+    def body(*refs):
+        kernel(*refs[count:])
+
+    return pl.pallas_call(
+        body,
+        in_specs=[pl.BlockSpec(memory_space=pl.ANY)] * count + list(in_specs),
+        compiler_params=pltpu.CompilerParams(vmem_limit_bytes=VMEM_LIMIT),
+        **options,
+    )(*after, *operands)
+
+
+def estimate(flops, moved, steps=0):
+    return pl.CostEstimate(flops=1, bytes_accessed=1, transcendentals=0)
 
 
 def split_low(value):
@@ -128,13 +146,14 @@
     ]
 
 
-def span_call(starts, flags, betas, active, head_count):
+def span_call(starts, flags, betas, active, head_count, after=()):
     count, width = active.shape[0], active.shape[1] // (3 * head_count)
     rows = pl.BlockSpec((count, width), lambda head: (0, head))
     whole = lambda shape: pl.BlockSpec(shape, lambda head: (0, 0))
     square = pl.BlockSpec((1, count, count), lambda head: (head, 0, 0))
-    return pl.pallas_call(
+    return launch(
         span_kernel,
+        after,
         grid=(head_count,),
         in_specs=[
             whole((count, 1)), whole((1, count)), whole(flags.shape), whole(betas.shape),
@@ -154,8 +173,9 @@
             jax.ShapeDtypeStruct((count, head_count * width), F32),
             jax.ShapeDtypeStruct((head_count, width, 2 * width), LOW),
         ],
-        compiler_params=pltpu.CompilerParams(vmem_limit_bytes=VMEM_LIMIT),
-    )(starts[:, None], starts[None, :], flags, betas, active, active, active)
+        cost_estimate=estimate(100 * head_count * count**3, 24 * active.shape[0] * active.shape[1]),
+        operands=(starts[:, None], starts[None, :], flags, betas, active, active, active,),
+    )
 
 
 def mixed_kernel(reach, local, state, gain, flags, mixed_out, head_out):
@@ -165,12 +185,13 @@
     head_out[...] = (mixed * scale * gain[...] * flags[:, 2:3]).astype(LOW)
 
 
-def mixed_call(reach, local, states, gain, flags):
+def mixed_call(reach, local, states, gain, flags, after=()):
     head_count, width = states.shape[0], states.shape[1]
     count = reach.shape[0]
     rows = pl.BlockSpec((count, width), lambda head: (0, head))
-    return pl.pallas_call(
+    return launch(
         mixed_kernel,
+        after,
         grid=(head_count,),
         in_specs=[
             rows, rows,
@@ -183,8 +204,9 @@
             jax.ShapeDtypeStruct(reach.shape, F32),
             jax.ShapeDtypeStruct(reach.shape, LOW),
         ],
-        compiler_params=pltpu.CompilerParams(vmem_limit_bytes=VMEM_LIMIT),
-    )(reach, local, states, gain[None], flags)
+        cost_estimate=estimate(6 * count * width * width * head_count, 14 * reach.shape[0] * reach.shape[1]),
+        operands=(reach, local, states, gain[None], flags,),
+    )
 
 
 def pull_kernel(reach, mixed_in, grads, gain, flags, change, d_mixed_out, gain_out, pair_out):
@@ -207,13 +229,14 @@
     pair_out[0] = jnp.concatenate([turned, pulled], axis=1).astype(LOW)
 
 
-def pull_call(reach, mixed, grads, gain, flags, pairs):
+def pull_call(reach, mixed, grads, gain, flags, pairs, after=()):
     head_count, width = pairs.shape[0], pairs.shape[1]
     count = reach.shape[0]
     rows = pl.BlockSpec((count, width), lambda head: (0, head))
     pair = pl.BlockSpec((1, width, 2 * width), lambda head: (head, 0, 0))
-    return pl.pallas_call(
+    return launch(
         pull_kernel,
+        after,
         grid=(head_count,),
         in_specs=[
             rows, rows, rows,
@@ -227,8 +250,9 @@
             jax.ShapeDtypeStruct((1, width), F32),
             jax.ShapeDtypeStruct(pairs.shape, LOW),
         ],
-        compiler_params=pltpu.CompilerParams(vmem_limit_bytes=VMEM_LIMIT),
-    )(reach, mixed, grads, gain[None], flags, pairs)
+        cost_estimate=estimate(6 * count * width * width * head_count, 20 * reach.shape[0] * reach.shape[1]),
+        operands=(reach, mixed, grads, gain[None], flags, pairs,),
+    )
 
 
 def back_kernel(
@@ -284,14 +308,15 @@
     d_beta_out[...] += jnp.where(lane == head, d_beta, 0.0)
 
 
-def back_call(starts, flags, betas, active, inverse, wy, scores, states, ends, grads):
+def back_call(starts, flags, betas, active, inverse, wy, scores, states, ends, grads, after=()):
     head_count, width = states.shape[0], states.shape[1]
     count = active.shape[0]
     rows = pl.BlockSpec((count, width), lambda head: (0, head))
     whole = lambda shape: pl.BlockSpec(shape, lambda head: (0, 0))
     per_head = lambda shape: pl.BlockSpec((1,) + shape, lambda head: (head, 0, 0))
-    return pl.pallas_call(
+    return launch(
         back_kernel,
+        after,
         grid=(head_count,),
         in_specs=[
             whole((count, 1)), whole((1, count)), whole(flags.shape), whole(betas.shape),
@@ -303,10 +328,9 @@
         out_specs=[rows, rows, rows, whole(betas.shape)],
         out_shape=[jax.ShapeDtypeStruct(grads.shape, F32)] * 3
         + [jax.ShapeDtypeStruct(betas.shape, F32)],
-        compiler_params=pltpu.CompilerParams(vmem_limit_bytes=VMEM_LIMIT),
-    )(
-        starts[:, None], starts[None, :], flags, betas, active, active, active, inverse, wy, scores,
-        states, ends, grads,
+        cost_estimate=estimate(36 * head_count * count**3, 40 * grads.shape[0] * grads.shape[1]),
+        operands=(starts[:, None], starts[None, :], flags, betas, active, active, active, inverse, wy, scores,
+        states, ends, grads,),
     )
 
 
@@ -317,6 +341,12 @@
 
 
 def scan_kernel(
+    waited, backwards, group_size, seq_size, *refs,
+):
+    scan_steps(backwards, group_size, seq_size, *refs[waited:])
+
+
+def scan_steps(
     backwards, group_size, seq_size, pairs, states_out,
     got, total_sent, total_got, state_sent, arrived, send_sem, recv_sem,
 ):
@@ -422,17 +452,19 @@
     states_out[...] = arrived[...]
 
 
-def scan_call(pairs, backwards, collective_id):
+def scan_call(pairs, backwards, collective_id, after=()):
     head_count, width = pairs.shape[0], pairs.shape[1]
     group_size, seq_size = lax.axis_size("grp"), lax.axis_size("seq")
     share = head_count // group_size
     levels = (seq_size - 1).bit_length()
     sems = 2 * (group_size - 1) + levels
     return pl.pallas_call(
-        functools.partial(scan_kernel, backwards, group_size, seq_size),
-        in_specs=[pl.BlockSpec(memory_space=pltpu.VMEM)],
+        functools.partial(scan_kernel, len(after), backwards, group_size, seq_size),
+        in_specs=[pl.BlockSpec(memory_space=pl.ANY)] * len(after)
+        + [pl.BlockSpec(memory_space=pltpu.VMEM)],
         out_specs=pl.BlockSpec(memory_space=pltpu.VMEM),
         out_shape=jax.ShapeDtypeStruct((head_count, width, width), LOW),
+        cost_estimate=estimate(400 * share * width**3 * levels, 64 * pairs.size),
         scratch_shapes=[
             pltpu.VMEM((group_size, share, width, 2 * width), LOW),
             pltpu.VMEM((levels, share, width, 2 * width), LOW),
@@ -445,22 +477,22 @@
         compiler_params=pltpu.CompilerParams(
             collective_id=collective_id, has_side_effects=True, vmem_limit_bytes=VMEM_LIMIT
         ),
-    )(pairs)
-
-
-def seq_bits():
+    )(*after, pairs)
+
+
+def swapped(value, bit):
+    count = lax.axis_size("seq")
+    return lax.ppermute(value, "seq", [(place, place ^ bit) for place in range(count)])
+
+
+def chip_bits():
     count = lax.axis_size("seq")
     bits = []
-    bit = 1
+    bit = 2
     while bit < count:
         bits.append(bit)
         bit = bit * 2
     return bits
-
-
-def phase_orders():
-    bits = seq_bits()
-    return (list(reversed(bits[1:])) + bits[:1], bits[1:] + bits[:1])
 
 
 def masks_of(order):
@@ -470,43 +502,24 @@
     return masks
 
 
-def swapped(value, bit):
-    count = lax.axis_size("seq")
-    return lax.ppermute(value, "seq", [(place, place ^ bit) for place in range(count)])
-
-
-def gathered(rows, order):
-    pieces = [rows]
-    for bit in order:
-        pieces = pieces + [swapped(piece, bit) for piece in pieces]
-    return jnp.concatenate(pieces, axis=0)
-
-
-def fetch(shard):
-    block = lax.all_gather(shard, "grp", axis=0, tiled=True)
-    half = block.shape[1] // 2
-    first, second = phase_orders()
-    return (gathered(block[:, :half], first), gathered(block[:, half:], second))
-
-
-def relative(values, order):
+def tied(value, *others):
+    return lax.optimization_barrier((value,) + others)[0]
+
+
+def relative(values, masks):
     count = lax.axis_size("seq")
     width = values.shape[1] // count
     mine = lax.axis_index("seq")
     return jnp.concatenate(
-        [
-            lax.dynamic_slice_in_dim(values, (mine ^ mask) * width, width, 1)
-            for mask in masks_of(order)
-        ],
+        [lax.dynamic_slice_in_dim(values, (mine ^ mask) * width, width, 1) for mask in masks],
         axis=1,
     )
 
 
-def absolute(values, order):
+def absolute(values, masks):
     count = lax.axis_size("seq")
     width = values.shape[1] // count
     mine = lax.axis_index("seq")
-    masks = masks_of(order)
     where_mask = jnp.array([masks.index(mask) for mask in range(count)], jnp.int32)
     return jnp.concatenate(
         [
@@ -517,60 +530,734 @@
     )
 
 
-def relative_pair(values):
-    first, second = phase_orders()
-    return (relative(values, first), relative(values, second))
-
-
-def absolute_pair(pair):
-    first, second = phase_orders()
-    return absolute(pair[0], first) + absolute(pair[1], second)
-
-
-def outer(matrix, grads):
-    return lax.dot_general(
-        matrix, grads, (((0,), (0,)), ((), ())), preferred_element_type=jnp.float32
-    )
-
-
-def scattered(rel_rows, grads, order):
-    half = rel_rows.shape[1] // 2
-    lower = outer(rel_rows[:, half:], grads).astype(jnp.bfloat16)
-    arrived = swapped(lower, order[-1])
-    kept = (outer(rel_rows[:, :half], grads) + arrived.astype(jnp.float32)).astype(jnp.bfloat16)
-    for bit in reversed(order[:-1]):
-        half = kept.shape[0] // 2
-        arrived = swapped(kept[half:], bit)
-        kept = (kept[:half].astype(jnp.float32) + arrived.astype(jnp.float32)).astype(jnp.bfloat16)
-    return kept
-
-
-def weight_grad(rel_pair, grads):
-    first, second = phase_orders()
-    half = grads.shape[1] // 2
-    kept = jnp.concatenate(
-        [
-            scattered(rel_pair[0], grads[:, :half], first),
-            scattered(rel_pair[1], grads[:, half:], second),
-        ],
-        axis=1,
-    )
-    return lax.psum_scatter(kept, "grp", scatter_dimension=0, tiled=True).astype(jnp.float32)
-
-
-def product_pair(rel_pair, weight_pair):
-    return jnp.concatenate(
-        [
-            jnp.dot(rows, weight, preferred_element_type=jnp.float32)
-            for rows, weight in zip(rel_pair, weight_pair)
-        ],
-        axis=1,
-    )
-
-
-def contract_pair(grads, weight_pair):
-    half = grads.shape[1] // 2
-    return (contract(grads[:, :half], weight_pair[0]), contract(grads[:, half:], weight_pair[1]))
+def spread_views(block, order, joined):
+    views = [(block, 0)]
+    for bit in order:
+        if joined:
+            if len(views) > 1:
+                rows = block.shape[0]
+                held = jnp.concatenate(
+                    [array[at * rows : (at + 1) * rows] for array, at in views], axis=0
+                )
+            else:
+                held = block
+            arrived = swapped(held, bit)
+            views = views + [(arrived, at) for at in range(len(views))]
+        else:
+            views = views + [(swapped(array, bit), at) for array, at in views]
+    return views
+
+
+def halved_sum(kept, bit):
+    half = kept.shape[0] // 2
+    arrived = swapped(kept[half:], bit)
+    return (kept[:half].astype(F32) + arrived.astype(F32)).astype(LOW)
+
+
+def over_groups(rows):
+    return lax.psum_scatter(rows, "grp", scatter_dimension=0, tiled=True).astype(F32)
+
+
+def tile_of(width, largest):
+    tile = largest
+    while width % tile:
+        tile = tile // 2
+    return tile
+
+
+def join_kernel(first, second, target):
+    rows = first.shape[0]
+    target[:rows] = first[...]
+    target[rows:] = second[...]
+
+
+def join_columns(first, second, start, width, after=()):
+    tile = tile_of(width, 1024)
+    while start % tile:
+        tile = tile // 2
+    rows = first.shape[0]
+    return launch(
+        join_kernel,
+        after,
+        grid=(width // tile,),
+        in_specs=[pl.BlockSpec((rows, tile), lambda step: (0, start // tile + step))] * 2,
+        out_specs=pl.BlockSpec((2 * rows, tile), lambda step: (0, step)),
+        out_shape=jax.ShapeDtypeStruct((2 * rows, width), first.dtype),
+        cost_estimate=estimate(0, 4 * rows * width),
+        operands=(first, second),
+    )
+
+
+def contract_kernel(grads, weights, total):
+    @pl.when(pl.program_id(0) == 0)
+    def _():
+        total[...] = jnp.zeros_like(total)
+
+    total[...] += lax.dot_general(
+        grads[...], weights[...], (((1,), (1,)), ((), ())), preferred_element_type=F32
+    )
+
+
+def contract_rows(grads, weights, start, after=()):
+    tokens, width = grads.shape
+    tile = tile_of(width, 512)
+    depth = weights.shape[0]
+    first = start // tile
+    return launch(
+        contract_kernel,
+        after,
+        grid=(width // tile,),
+        in_specs=[
+            pl.BlockSpec((tokens, tile), lambda step: (0, step)),
+            pl.BlockSpec((depth, tile), lambda step: (0, first + step)),
+        ],
+        out_specs=pl.BlockSpec((tokens, depth), lambda step: (0, 0)),
+        out_shape=jax.ShapeDtypeStruct((tokens, depth), F32),
+        cost_estimate=estimate(2 * tokens * depth * width, 2 * depth * width),
+        operands=(grads, weights),
+    )
+
+
+def feed_kernel(count, cuts, resumed, feed, slopes, *refs):
+    weights, refs = refs[: 6 * count], refs[6 * count :]
+    if resumed:
+        before, refs = refs[:2], refs[2:]
+    grads_first, grads_second, out_total, d_total = refs
+    step = pl.program_id(0)
+
+    @pl.when(step == 0)
+    def _():
+        out_total[...] = before[0][...] if resumed else jnp.zeros_like(out_total)
+        d_total[...] = before[1][...] if resumed else jnp.zeros_like(d_total)
+
+    back = functools.partial(
+        lax.dot_general, dimension_numbers=(((1,), (1,)), ((), ())), preferred_element_type=F32
+    )
+
+    def tile_step(pieces, grads_out):
+        gate_part, up_part, down_part = [
+            jnp.concatenate(
+                [piece[...] for piece in pieces[kind * count : (kind + 1) * count]], axis=0
+            )
+            for kind in range(3)
+        ]
+        gate = jnp.dot(feed[...], gate_part, preferred_element_type=F32)
+        upper = jnp.dot(feed[...], up_part, preferred_element_type=F32)
+        d_inner = jnp.dot(slopes[...], down_part, preferred_element_type=F32)
+        gate_sig = 1.0 / (1.0 + jnp.exp(-gate))
+        gate_act = gate * gate_sig
+        inner = (gate_act * upper).astype(LOW)
+        d_gate = (d_inner * upper * gate_sig * (1.0 + gate * (1.0 - gate_sig))).astype(LOW)
+        d_upper = (d_inner * gate_act).astype(LOW)
+        grads_out[0] = d_gate
+        grads_out[1] = d_upper
+        grads_out[2] = inner
+        out_total[...] += back(inner, down_part)
+        d_total[...] += back(d_gate, gate_part) + back(d_upper, up_part)
+
+    @pl.when(step < cuts[0])
+    def _():
+        tile_step(weights[: 3 * count], grads_first)
+
+    @pl.when(step >= cuts[0])
+    def _():
+        tile_step(weights[3 * count :], grads_second)
+
+
+def feed_call(feed, slopes, piece_lists, before, tile, after=()):
+    tokens, depth = feed.shape
+    cuts = [pieces[0][0].shape[1] // (3 * tile) for pieces in piece_lists]
+    block_rows = depth // len(piece_lists[0])
+    count = len(piece_lists[0])
+    first = lambda step: jnp.minimum(step, cuts[0] - 1)
+    second = lambda step: jnp.maximum(step - cuts[0], 0)
+    whole = pl.BlockSpec((tokens, depth), lambda step: (0, 0))
+    weights = [
+        pl.BlockSpec(
+            (block_rows, tile),
+            lambda step, at=at, kind=kind, where=where, cut=cut: (at, kind * cut + where(step)),
+        )
+        for pieces, where, cut in zip(piece_lists, (first, second), cuts)
+        for kind in range(3)
+        for _, at in pieces
+    ]
+    width = (cuts[0] + cuts[1]) * tile
+    return launch(
+        functools.partial(feed_kernel, count, cuts, before is not None),
+        after,
+        grid=(cuts[0] + cuts[1],),
+        in_specs=[whole, whole] + weights + ([whole, whole] if before is not None else []),
+        out_specs=[
+            pl.BlockSpec((3, tokens, tile), lambda step: (0, 0, first(step))),
+            pl.BlockSpec((3, tokens, tile), lambda step: (0, 0, second(step))),
+            whole,
+            whole,
+        ],
+        out_shape=[
+            jax.ShapeDtypeStruct((3, tokens, cuts[0] * tile), LOW),
+            jax.ShapeDtypeStruct((3, tokens, cuts[1] * tile), LOW),
+            jax.ShapeDtypeStruct((tokens, depth), F32),
+            jax.ShapeDtypeStruct((tokens, depth), F32),
+        ],
+        cost_estimate=estimate(
+            12 * tokens * depth * width, 6 * depth * width, 3 * tokens * width
+        ),
+        operands=(
+            feed, slopes,
+            *([array for array, _ in piece_lists[0]] * 3),
+            *([array for array, _ in piece_lists[1]] * 3),
+            *(before if before is not None else ()),
+        ),
+    )
+
+
+def outer_kernel(count, kinds, starts, first_kind, *refs):
+    sources = (refs[:count], refs[count : 2 * count])
+    grads, arrived, out = refs[2 * count], refs[2 * count + 1 : -1], refs[-1]
+    kind = pl.program_id(0) + first_kind
+    depth = out.shape[0] // count
+
+    def fill(source, added):
+        for place in range(count):
+            rows = slice(place * depth, (place + 1) * depth)
+            total = lax.dot_general(
+                source[place][...], grads[0], (((0,), (0,)), ((), ())),
+                preferred_element_type=F32,
+            )
+            if added is not None:
+                total = total + added[rows].astype(F32)
+            out[rows] = total.astype(LOW)
+
+    for which in range(2):
+        wanted = (kind == kinds - 1) if which else (kind < kinds - 1)
+        if not arrived:
+            pl.when(wanted)(functools.partial(fill, sources[which], None))
+        for place, added in enumerate(arrived):
+            inside = kind >= starts[place]
+            if place + 1 < len(arrived):
+                inside = inside & (kind < starts[place + 1])
+            pl.when(wanted & inside)(functools.partial(fill, sources[which], added))
+
+
+def outer_call(sources, grads, places, span=None, arrived=(), starts=(0,), after=()):
+    tokens, model = sources[0].shape
+    kinds, _, width = grads.shape
+    blocks = 2 * len(places)
+    depth = model // blocks
+    half = model // 2
+    first_kind, stop = span or (0, kinds)
+    last = stop - first_kind
+
+    def own(place):
+        return pl.BlockSpec((tokens, depth), lambda kind: (0, place))
+
+    def added(array, start):
+        most = array.shape[1] // width - 1
+        return pl.BlockSpec(
+            (half, width), lambda kind: (0, jnp.clip(kind + first_kind - start, 0, most))
+        )
+
+    return launch(
+        functools.partial(outer_kernel, len(places), kinds, starts, first_kind),
+        after,
+        grid=(last,),
+        in_specs=[own(place) for place in places] * 2
+        + [pl.BlockSpec((1, tokens, width), lambda kind: (first_kind + kind, 0, 0))]
+        + [added(array, start) for array, start in zip(arrived, starts)],
+        out_specs=pl.BlockSpec((half, width), lambda kind: (0, kind)),
+        out_shape=jax.ShapeDtypeStruct((half, last * width), LOW),
+        cost_estimate=estimate(1, 1),
+        operands=(
+            *([sources[0]] * len(places)), *([sources[1]] * len(places)), grads, *arrived,
+        ),
+    )
+
+
+def gather_kernel(
+    group_size, bits, orders, cuts, feed_cuts, shard, feed, full, pair_first, pair_second, rest,
+    own_sem, line_send, line_recv, tree_send, tree_recv, feed_send, feed_recv, core_send, core_recv,
+):
+    my_seq, my_group = lax.axis_index("seq"), lax.axis_index("grp")
+    rows = shard.shape[0]
+    levels = len(orders[0])
+
+    def flipped(mask):
+        place = my_seq
+        for bit in bits:
+            if mask & bit:
+                place = place + bit - 2 * bit * lax.rem(my_seq // bit, 2)
+        return place
+
+    def remote(source, target, send_sem, recv_sem, device):
+        return pltpu.make_async_remote_copy(
+            src_ref=source, dst_ref=target, send_sem=send_sem, recv_sem=recv_sem,
+            device_id=device, device_id_type=pl.DeviceIdType.MESH,
+        )
+
+    def greet(device):
+        pl.semaphore_signal(
+            barrier, inc=1, device_id=device, device_id_type=pl.DeviceIdType.MESH
+        )
+
+    def has(direction, steps):
+        return my_group >= steps if direction == 0 else my_group + steps < group_size
+
+    def beside(direction, steps):
+        return my_group - steps if direction == 0 else my_group + steps
+
+    barrier = pltpu.get_barrier_semaphore()
+    for bit in bits:
+        greet((flipped(bit), my_group))
+    for direction in range(2):
+
+        @pl.when(has(direction, 1))
+        def _():
+            greet((my_seq, beside(direction, 1)))
+
+    pl.semaphore_wait(
+        barrier,
+        len(bits) + jnp.minimum(my_group, 1) + jnp.minimum(group_size - 1 - my_group, 1),
+    )
+
+    def place_of(mask, group):
+        return pl.ds(pl.multiple_of((flipped(mask) * group_size + group) * rows, rows), rows)
+
+    def line_copies(kind, direction, hop):
+        origin = beside(direction, hop - 1)
+        device = (my_seq, beside(1 - direction, 1))
+        if kind == 0:
+            views = [(shard if hop == 1 else full.at[place_of(0, origin)], full.at[place_of(0, origin)])]
+            sems = (line_send, line_recv)
+        else:
+            spot = pl.ds(pl.multiple_of(origin * rows, rows), rows)
+            parts = (pair_first, pair_second, rest)
+            views = [
+                (
+                    feed.at[:, cut] if hop == 1 else part.at[spot],
+                    part.at[spot],
+                )
+                for part, cut in zip(parts, feed_cuts)
+            ]
+            sems = (feed_send, feed_recv)
+        return [
+            remote(source, target, sems[0].at[direction, hop - 1, at], sems[1].at[direction, hop - 1, at], device)
+            for at, (source, target) in enumerate(views)
+        ]
+
+    def line_send_now(kind, direction, hop):
+        @pl.when(has(1 - direction, 1))
+        def _():
+            for copy in line_copies(kind, direction, hop):
+                copy.start()
+
+    def line_wait(kind, direction, hop):
+        for copy in line_copies(kind, direction, hop):
+            copy.wait_recv()
+
+    def line_drain(kind):
+        for direction in range(2):
+            for hop in range(1, group_size):
+
+                @pl.when(has(direction, hop - 1) & has(1 - direction, 1))
+                def _():
+                    for copy in line_copies(kind, direction, hop):
+                        copy.wait_send()
+
+    slots = [(0, 0)] + [(direction, hop) for hop in range(1, group_size) for direction in range(2)]
+
+    def node_copy(slot, part, level, mask):
+        direction, hop = slots[slot]
+        origin = beside(direction, hop) if hop else my_group
+        view = full.at[place_of(mask, origin), cuts[part]]
+        source = shard.at[:, cuts[part]] if hop == 0 and mask == 0 else view
+        node = 2**level - 1 + masks_of(orders[part][:level]).index(mask)
+        return remote(
+            source, view, tree_send.at[slot, part, node], tree_recv.at[slot, part, node],
+            (flipped(orders[part][level]), my_group),
+        )
+
+    def stage(slot, lag):
+        direction, hop = slots[slot]
+        if lag == 0:
+            if hop:
+                line_wait(0, direction, hop)
+                if hop + 1 < group_size:
+                    line_send_now(0, direction, hop + 1)
+            for part in range(2):
+                for level in range(levels):
+                    node_copy(slot, part, level, 0).start()
+        else:
+            level = lag - 1
+            for part in range(2):
+                for mask in masks_of(orders[part][:level]):
+                    node_copy(slot, part, level, mask).wait_recv()
+                    for later in range(level + 1, levels):
+                        node_copy(slot, part, later, mask ^ orders[part][level]).start()
+
+    def when_held(slot, work):
+        direction, hop = slots[slot]
+        if hop == 0:
+            work()
+        else:
+            pl.when(has(direction, hop))(work)
+
+    own = pltpu.make_async_copy(shard, full.at[place_of(0, my_group)], own_sem.at[0])
+    own.start()
+    spot = pl.ds(pl.multiple_of(my_group * rows, rows), rows)
+    own_feed = [
+        pltpu.make_async_copy(feed.at[:, cut], part.at[spot], own_sem.at[1 + at])
+        for at, (part, cut) in enumerate(zip((pair_first, pair_second, rest), feed_cuts))
+    ]
+    for copy in own_feed:
+        copy.start()
+    for direction in range(2):
+        line_send_now(0, direction, 1)
+    def feed_hop(hop):
+        for direction in range(2):
+
+            @pl.when(has(direction, hop))
+            def _():
+                line_wait(1, direction, hop)
+                if hop + 1 < group_size:
+                    line_send_now(1, direction, hop + 1)
+
+    def at_lag(slot, lag):
+        when_held(slot, functools.partial(stage, slot, lag))
+
+    at_lag(0, 0)
+    for hop in range(1, group_size):
+        at_lag(2 * hop - 1, 0)
+        at_lag(2 * hop, 0)
+        if hop == group_size - 2:
+            for direction in range(2):
+                line_send_now(1, direction, 1)
+        for slot in [0] if hop == 1 else [2 * hop - 3, 2 * hop - 2]:
+            at_lag(slot, 1)
+    for slot in range(max(2 * group_size - 3, 0), len(slots)):
+        at_lag(slot, 1)
+    hop_now = 1
+    for lag in range(2, levels):
+        for slot in range(len(slots)):
+            if slot % 3 == 0 and hop_now < group_size:
+                feed_hop(hop_now)
+                hop_now = hop_now + 1
+            at_lag(slot, lag)
+    for hop in range(hop_now, group_size):
+        feed_hop(hop)
+    line_drain(1)
+    for copy in own_feed:
+        copy.wait()
+    half = rest.shape[0]
+    first_width = pair_first.shape[1]
+    swaps = [
+        remote(
+            rest.at[:, cut], part.at[pl.ds(half, half)], core_send.at[at], core_recv.at[at],
+            (flipped(1), my_group),
+        )
+        for at, (part, cut) in enumerate(
+            (
+                (pair_first, pl.ds(0, first_width)),
+                (pair_second, pl.ds(first_width, pair_second.shape[1])),
+            )
+        )
+    ]
+    for copy in swaps:
+        copy.start()
+    for slot in range(len(slots)):
+        when_held(slot, functools.partial(stage, slot, levels))
+    for copy in swaps:
+        copy.wait()
+    own.wait()
+    line_drain(0)
+
+    def drain(slot):
+        for part in range(2):
+            for level in range(levels):
+                for mask in masks_of(orders[part][:level]):
+                    node_copy(slot, part, level, mask).wait_send()
+
+    for slot in range(len(slots)):
+        when_held(slot, functools.partial(drain, slot))
+
+
+def gather_call(shard, feed, cuts, feed_cuts, orders, collective_id):
+    group_size, seq_size = lax.axis_size("grp"), lax.axis_size("seq")
+    rows, width = shard.shape
+    bits = [1] + chip_bits()
+    nodes = 2 ** len(bits) - 1
+    slots = 2 * group_size - 1
+    first_width, second_width = feed_cuts[0].size, feed_cuts[1].size
+    any_space = pl.BlockSpec(memory_space=pl.ANY)
+    dma = pltpu.SemaphoreType.DMA
+    return pl.pallas_call(
+        functools.partial(gather_kernel, group_size, bits, orders, cuts, feed_cuts),
+        in_specs=[any_space] * 2,
+        out_specs=[any_space] * 4,
+        out_shape=[
+            jax.ShapeDtypeStruct((rows * group_size * seq_size, width), LOW),
+            jax.ShapeDtypeStruct((2 * rows * group_size, first_width), LOW),
+            jax.ShapeDtypeStruct((2 * rows * group_size, second_width), LOW),
+            jax.ShapeDtypeStruct((rows * group_size, first_width + second_width), LOW),
+        ],
+        scratch_shapes=[
+            dma((4,)),
+            dma((2, group_size - 1, 1)), dma((2, group_size - 1, 1)),
+            dma((slots, 2, nodes)), dma((slots, 2, nodes)),
+            dma((2, group_size - 1, 3)), dma((2, group_size - 1, 3)),
+            dma((2,)), dma((2,)),
+        ],
+        cost_estimate=estimate(1.5e11, 1e8),
+        compiler_params=pltpu.CompilerParams(collective_id=collective_id, has_side_effects=True),
+    )(shard, feed)
+
+
+def reduce_kernel(waited, group_size, orders, groups, *refs):
+    refs = refs[waited:]
+    sets = len(groups)
+    inputs, refs = refs[: 4 * sets + 1], refs[4 * sets + 1 :]
+    totals, everywhere, refs = refs[:sets], refs[sets], refs[sets + 1 :]
+    buffers, refs = refs[: 5 * sets], refs[5 * sets :]
+    vector_out, vector_in = refs[:2]
+    send_sem, recv_sem, core_send, core_recv, line_send, line_recv, v_send, v_recv = refs[2:]
+    my_seq, my_group = lax.axis_index("seq"), lax.axis_index("grp")
+    levels = len(orders[0])
+    peers = [lax.rem(my_group + step, group_size) for step in range(1, group_size)]
+    bits = [1] + list(orders[1])
+    units = [(place, group) for place in range(sets) for group in range(groups[place])]
+    lower_rows = inputs[0].shape[0]
+    final = lower_rows // 2 ** (levels - 1)
+    half = final // 2
+    rows = half // group_size
+
+    def partner(bit):
+        return my_seq + bit - 2 * bit * lax.rem(my_seq // bit, 2)
+
+    def greet(device):
+        pl.semaphore_signal(
+            barrier, inc=1, device_id=device, device_id_type=pl.DeviceIdType.MESH
+        )
+
+    barrier = pltpu.get_barrier_semaphore()
+    for bit in bits:
+        greet((partner(bit), my_group))
+    for peer in peers:
+        greet((my_seq, peer))
+    pl.semaphore_wait(barrier, len(bits) + len(peers))
+
+    def remote(source, target, send, recv, device):
+        return pltpu.make_async_remote_copy(
+            src_ref=source, dst_ref=target, send_sem=send, recv_sem=recv,
+            device_id=device, device_id_type=pl.DeviceIdType.MESH,
+        )
+
+    def held(level):
+        return lower_rows // 2**level
+
+    def begins(level):
+        return sum(held(before) for before in range(level))
+
+    def parts_of(unit):
+        place, group = units[unit]
+        return inputs[4 * place : 4 * place + 4], buffers[5 * place : 5 * place + 5], group
+
+    def chip_copy(unit, part, level):
+        given, (arrived, leaving, _, _, _), group = parts_of(unit)
+        width = arrived.shape[-1]
+        count = held(level)
+        if level == 0:
+            source = given[part].at[:, pl.ds(group * width, width)]
+        else:
+            source = leaving.at[part, group, pl.ds(begins(level) - held(0), count)]
+        return remote(
+            source,
+            arrived.at[part, group, pl.ds(begins(level), count)],
+            send_sem.at[unit, part, level],
+            recv_sem.at[unit, part, level],
+            (partner(orders[part][levels - 1 - level]), my_group),
+        )
+
+    def core_copy(unit):
+        _, (_, _, chip_total, core_in, _), group = parts_of(unit)
+        return remote(
+            chip_total.at[group, pl.ds(half, half)],
+            core_in.at[group],
+            core_send.at[unit],
+            core_recv.at[unit],
+            (partner(1), my_group),
+        )
+
+    def line_copies(unit):
+        _, (_, _, chip_total, core_in, line_in), group = parts_of(unit)
+        copies = []
+        for at, peer in enumerate(peers):
+            spot = pl.ds(pl.multiple_of(peer * rows, rows), rows)
+            for side, source in enumerate((chip_total.at[group, spot], core_in.at[group, spot])):
+                copies.append(
+                    remote(
+                        source,
+                        line_in.at[group, at, side],
+                        line_send.at[unit, at, side],
+                        line_recv.at[unit, at, side],
+                        (my_seq, peer),
+                    )
+                )
+        return copies
+
+    def stage(unit, lag):
+        given, (arrived, leaving, chip_total, core_in, line_in), group = parts_of(unit)
+        width = arrived.shape[-1]
+        if lag == 0:
+            for part in range(2):
+                chip_copy(unit, part, 0).start()
+        elif lag <= levels:
+            level = lag - 1
+            for part in range(2):
+                chip_copy(unit, part, level).wait_recv()
+                count = held(level)
+
+                def added(low, high):
+                    base = begins(level)
+                    value = arrived[part, group, base + low : base + high].astype(F32)
+                    if level == 0:
+                        kept = given[2 + part][low:high, group * width : (group + 1) * width]
+                    else:
+                        before = begins(level - 1)
+                        kept = arrived[part, group, before + low : before + high]
+                    return value + kept.astype(F32)
+
+                if lag < levels:
+                    middle = count // 2
+                    spot = begins(level + 1) - held(0)
+                    leaving[part, group, spot : spot + middle] = added(middle, count).astype(LOW)
+                    chip_copy(unit, part, level + 1).start()
+                    base = begins(level)
+                    arrived[part, group, base : base + middle] = added(0, middle).astype(LOW)
+                else:
+                    chip_total[group, :, part * width : (part + 1) * width] = added(
+                        0, count
+                    ).astype(LOW)
+            if lag == levels:
+                core_copy(unit).start()
+        elif lag == levels + 1:
+            core_copy(unit).wait_recv()
+            for copy in line_copies(unit):
+                copy.start()
+        else:
+            own = pl.ds(pl.multiple_of(my_group * rows, rows), rows)
+            for copy in line_copies(unit):
+                copy.wait_recv()
+            total = totals[units[unit][0]]
+            for side, source in enumerate((chip_total, core_in)):
+                value = source[group, own].astype(F32)
+                for at in range(len(peers)):
+                    value = value + line_in[group, at, side].astype(F32)
+                spot = (group * 2 + side) * 2 * width
+                total[:, spot : spot + 2 * width] = value
+
+    def vector_copies(step):
+        if step < len(bits):
+            return [
+                remote(
+                    vector_out.at[step], vector_in.at[step], v_send.at[step], v_recv.at[step],
+                    (partner(bits[step]), my_group),
+                )
+            ]
+        return [
+            remote(
+                vector_out.at[step], vector_in.at[step + at], v_send.at[step + at],
+                v_recv.at[step + at], (my_seq, peer),
+            )
+            for at, peer in enumerate(peers)
+        ]
+
+    def vector_step(step):
+        if step:
+            for copy in vector_copies(step - 1):
+                copy.wait_recv()
+        if step == 0:
+            vector_out[0] = inputs[-1][...]
+        elif step <= len(bits):
+            vector_out[step] = vector_out[step - 1] + vector_in[step - 1]
+        else:
+            value = vector_out[len(bits)]
+            for at in range(len(peers)):
+                value = value + vector_in[len(bits) + at]
+            everywhere[...] = value
+        if step <= len(bits):
+            for copy in vector_copies(step):
+                copy.start()
+
+    last_step = len(units) + levels + 2
+    for step in range(last_step):
+        for lag in range(levels + 3):
+            if 0 <= step - lag < len(units):
+                stage(step - lag, lag)
+        if step <= len(bits) + 1:
+            vector_step(step)
+    for step in range(last_step, len(bits) + 2):
+        vector_step(step)
+    for step in range(len(bits) + 1):
+        for copy in vector_copies(step):
+            copy.wait_send()
+    for unit in range(len(units)):
+        for part in range(2):
+            for level in range(levels):
+                chip_copy(unit, part, level).wait_send()
+        core_copy(unit).wait_send()
+        for copy in line_copies(unit):
+            copy.wait_send()
+
+
+def reduce_call(sets, vector, orders, collective_id, after=()):
+    group_size = lax.axis_size("grp")
+    depth = sets[0][0][0].shape[0]
+    levels = len(orders[0])
+    final = depth // 2 ** (levels - 1)
+    half = final // 2
+    rows = half // group_size
+    held_all = sum(depth // 2**level for level in range(levels))
+    groups = [group for _, _, group in sets]
+    units = sum(groups)
+    bits = levels + 1
+    in_vmem = pl.BlockSpec(memory_space=pltpu.VMEM)
+    in_any = pl.BlockSpec(memory_space=pl.ANY)
+    dma = pltpu.SemaphoreType.DMA
+    widths = [lowers[0].shape[1] // group for lowers, _, group in sets]
+    scratch = []
+    for group, width in zip(groups, widths):
+        scratch += [
+            pltpu.VMEM((2, group, held_all, width), LOW),
+            pltpu.VMEM((2, group, max(held_all - depth, 16), width), LOW),
+            pltpu.VMEM((group, final, 2 * width), LOW),
+            pltpu.VMEM((group, half, 2 * width), LOW),
+            pltpu.VMEM((group, max(group_size - 1, 1), 2, rows, 2 * width), LOW),
+        ]
+    operands = []
+    for lowers, uppers, _ in sets:
+        operands += [*lowers, *uppers]
+    return pl.pallas_call(
+        functools.partial(reduce_kernel, len(after), group_size, orders, groups),
+        in_specs=[in_any] * len(after) + [in_any, in_any, in_vmem, in_vmem] * len(sets) + [in_vmem],
+        out_specs=[in_vmem] * (len(sets) + 1),
+        out_shape=[
+            jax.ShapeDtypeStruct((rows, group * 4 * width), F32)
+            for group, width in zip(groups, widths)
+        ]
+        + [jax.ShapeDtypeStruct(vector.shape, F32)],
+        scratch_shapes=scratch
+        + [
+            pltpu.VMEM((bits + 1,) + vector.shape, F32),
+            pltpu.VMEM((bits + group_size,) + vector.shape, F32),
+            dma((units, 2, levels)), dma((units, 2, levels)),
+            dma((units,)), dma((units,)),
+            dma((units, group_size, 2)), dma((units, group_size, 2)),
+            dma((bits + group_size,)), dma((bits + group_size,)),
+        ],
+        cost_estimate=estimate(1, 1),
+        compiler_params=pltpu.CompilerParams(
+            collective_id=collective_id, has_side_effects=True, vmem_limit_bytes=VMEM_LIMIT
+        ),
+    )(*after, *operands, vector)
 
 
 def local(
@@ -598,25 +1285,90 @@
     head_count = beta_bias.shape[0]
     head_width = head_gain.shape[0]
     tap_count = conv_query.shape[1]
-    small = lax.all_gather(
-        jnp.concatenate(
-            [mixer_gain[:, None], feed_gain[:, None], conv_query, conv_key, conv_value, beta_weight],
-            axis=1,
-        ),
-        ("seq", "grp"),
-        axis=0,
-        tiled=True,
-    )
+    hidden_units = gate_weight.shape[1]
+    my_core = lax.rem(lax.axis_index("seq"), 2)
+    chip = chip_bits()
+    chip_orders = (list(reversed(chip)), list(chip))
+    plain_orders = [order + [1] for order in chip_orders]
+    plain_masks = [masks_of(order) for order in plain_orders]
+    pair_masks = [masks_of([1] + order) for order in chip_orders]
+
+    def along_groups(shard):
+        return lax.all_gather(shard, "grp", axis=0, tiled=True)
+
+    small_shard = jnp.concatenate(
+        [mixer_gain[:, None], feed_gain[:, None], conv_query, conv_key, conv_value, beta_weight],
+        axis=1,
+    )
+    small_width = small_shard.shape[1]
+    padded_small = jnp.pad(small_shard, ((0, 0), (0, -small_width % 128)))
+    plain_shard = jnp.concatenate(
+        [query_weight, key_weight, value_weight, out_weight, padded_small], axis=1
+    )
+    plain_cut = 2 * model_width
+    plain_cuts = (pl.ds(0, plain_cut), pl.ds(plain_cut, plain_shard.shape[1] - plain_cut))
+    unit_width = hidden_units // 2
+    tile = tile_of(unit_width, 256)
+    tiles = unit_width // tile
+    half_tiles = -(-tiles // 2)
+    rest = tiles - half_tiles
+    counts = [-(-half_tiles // 2), half_tiles // 2, -(-rest // 2), rest // 2]
+    edges = [sum(counts[:place]) * tile for place in range(5)]
+    spans = list(zip(edges[:-1], edges[1:]))
+    feed_shards = (gate_weight, up_weight, down_weight)
+
+    def units_of(core, start, stop):
+        return [
+            lax.dynamic_slice_in_dim(shard, core * unit_width + start, stop - start, 1)
+            for shard in feed_shards
+        ]
+
+    feed_shard = jnp.concatenate(
+        [
+            part
+            for core in (my_core, 1 - my_core)
+            for start, stop in spans[:2]
+            for part in units_of(core, start, stop)
+        ],
+        axis=1,
+    )
+    widths = [3 * (stop - start) for start, stop in spans]
+    feed_cuts = (
+        pl.ds(0, widths[0]),
+        pl.ds(widths[0], widths[1]),
+        pl.ds(widths[0] + widths[1], widths[0] + widths[1]),
+    )
+    full, pair_first, pair_second, _ = gather_call(
+        plain_shard, feed_shard, plain_cuts, feed_cuts, plain_orders, 2
+    )
+    w_qkv, w_out = full[:, : 3 * model_width], full[:, 3 * model_width : 4 * model_width]
+    small = full[:, 4 * model_width : 4 * model_width + small_width]
     gain_mixer, gain_feed = small[:, 0], small[:, 1]
     c_query = small[:, 2 : 2 + tap_count]
     c_key = small[:, 2 + tap_count : 2 + 2 * tap_count]
     c_value = small[:, 2 + 2 * tap_count : 2 + 3 * tap_count]
     w_beta = small[:, 2 + 3 * tap_count :]
-    w_qkv = fetch(jnp.concatenate([query_weight, key_weight, value_weight], axis=1))
-    w_out = fetch(out_weight)
-    w_gate = fetch(gate_weight)
-    w_up = fetch(up_weight)
-    w_down = fetch(down_weight)
+
+    feed_blocks = [
+        along_groups(
+            tied(
+                jnp.concatenate(
+                    [part for start, stop in spans[2:] for part in units_of(core, start, stop)],
+                    axis=1,
+                ),
+                full,
+            )
+        )
+        for core in (1 - my_core, my_core)
+    ]
+    theirs_block = swapped(feed_blocks[0], 1)
+    feed_pieces = [
+        spread_views(pair_first, chip_orders[0], True),
+        spread_views(pair_second, chip_orders[1], True),
+    ]
+    out_half = model_width // 2
+    qkv_half = 3 * model_width // 2
+
     anchor = lax.axis_index(("seq", "grp")) * row_count
     places = anchor + jnp.arange(row_count, dtype=jnp.int32)
     starts = jnp.cumsum(lengths) - lengths
@@ -628,8 +1380,7 @@
     inputs32 = tokens.astype(jnp.float32)
     normed_a, norm_a_back = jax.vjp(rms_scale, inputs32, gain_mixer.astype(jnp.float32))
     normed_low = normed_a.astype(jnp.bfloat16)
-    normed_rel = relative_pair(normed_low)
-    own_pre = product_pair(normed_rel, w_qkv).astype(jnp.bfloat16)
+    own_pre = jnp.dot(normed_low, w_qkv, preferred_element_type=F32).astype(LOW)
     logit_part = jnp.dot(normed_low, w_beta, preferred_element_type=jnp.float32)
     sigmoid_val = jax.nn.sigmoid(logit_part + beta_bias)
     beta_rows = sigmoid_val * live_rows[:, None]
@@ -656,42 +1407,116 @@
         axis=1,
     )
     inverse, wy, scores, reach, local_out, pairs = span_call(
-        row_start, flags, beta_rows, active, head_count
-    )
+        row_start,
+        flags,
+        beta_rows,
+        active,
+        head_count,
+        after=(feed_pieces[0][1][0], feed_pieces[1][1][0]),
+    )
+    ready = (pairs, feed_pieces[0][-1][0], feed_pieces[1][-1][0])
+    edge = 0
+    for place, width in enumerate(widths[2:]):
+        paired = join_columns(feed_blocks[1], theirs_block, edge, width, ready)
+        feed_pieces.append(spread_views(paired, chip_orders[place], False))
+        edge = edge + width
     start_states = scan_call(pairs, False, 0)
-    mixed, head_low = mixed_call(reach, local_out, start_states, head_gain, flags)
-    head_rel = relative_pair(head_low)
-    hidden_one = inputs32 + product_pair(head_rel, w_out)
+    mixed, head_low = mixed_call(
+        reach,
+        local_out,
+        start_states,
+        head_gain,
+        flags,
+        after=tuple(feed_pieces[place][at][0] for place in (2, 3) for at in (1, 2)),
+    )
+    hidden_one = inputs32 + jnp.dot(head_low, w_out, preferred_element_type=F32)
     normed_f, norm_f_back = jax.vjp(rms_scale, hidden_one, gain_feed.astype(jnp.float32))
     feed_low = normed_f.astype(jnp.bfloat16)
-    feed_rel = relative_pair(feed_low)
-    gate = product_pair(feed_rel, w_gate)
-    upper = product_pair(feed_rel, w_up)
-    gate_sig = jax.nn.sigmoid(gate)
-    gate_act = gate * gate_sig
-    inner_low = (gate_act * upper).astype(jnp.bfloat16)
-    block_out = (hidden_one + absolute_pair(contract_pair(inner_low, w_down))).astype(jnp.bfloat16)
+    both_feed = jnp.concatenate([feed_low, swapped(feed_low, 1)], axis=0)
+    both_slopes = jnp.concatenate([cotangent, swapped(cotangent, 1)], axis=0)
+    feed_rel = relative(both_feed, pair_masks[0])
+    slopes_rel = relative(both_slopes, pair_masks[0])
+    depth = model_width // len(feed_pieces[0])
+    second_places = [pair_masks[1][::2].index(mask) for mask in pair_masks[0][::2]]
+    first_places = [pair_masks[0][::2].index(mask) for mask in pair_masks[1][::2]]
+    chip_count = len(feed_pieces[0])
+    half_places = [
+        [list(range(chip_count // 2)), list(range(chip_count // 2, chip_count))],
+        [first_places[: chip_count // 2], first_places[chip_count // 2 :]],
+    ]
+    sources = (feed_rel, slopes_rel)
+    totals = None
+    feed_grads, lower_halves, sent = [], [], []
+    for chunk in range(2):
+        grads_first, grads_second, *totals = feed_call(
+            feed_rel,
+            slopes_rel,
+            [
+                feed_pieces[2 * chunk],
+                [feed_pieces[2 * chunk + 1][place] for place in second_places],
+            ],
+            totals,
+            tile,
+            after=lower_halves,
+        )
+        feed_grads += [grads_first, grads_second]
+        for part, grads in enumerate((grads_first, grads_second)):
+            places = half_places[part][1]
+            pieces = [outer_call(sources, grads, places)]
+            lower_halves += pieces
+            sent.append([swapped(piece, chip_orders[part][-1]) for piece in pieces])
+    out_total, d_total = totals
+    their_masks = [mask ^ 1 for mask in pair_masks[0]]
+    d_feed = absolute(d_total[:row_count], pair_masks[0]) + absolute(
+        swapped(d_total[row_count:], 1), their_masks
+    )
+    block_out = (
+        hidden_one
+        + absolute(out_total[:row_count], pair_masks[0])
+        + absolute(swapped(out_total[row_count:], 1), their_masks)
+    ).astype(jnp.bfloat16)
     grad_out = cotangent.astype(jnp.float32)
-    cotangent_rel = relative_pair(cotangent)
-    d_inner = product_pair(cotangent_rel, w_down)
-    d_gate = (d_inner * upper * gate_sig * (1.0 + gate * (1.0 - gate_sig))).astype(jnp.bfloat16)
-    d_upper = (d_inner * gate_act).astype(jnp.bfloat16)
-    d_feed = absolute_pair(
-        tuple(
-            one + two
-            for one, two in zip(contract_pair(d_gate, w_gate), contract_pair(d_upper, w_up))
-        )
-    )
-    down_grad = weight_grad(cotangent_rel, inner_low)
-    gate_grad = weight_grad(feed_rel, d_gate)
-    up_grad = weight_grad(feed_rel, d_upper)
     d_hidden_part, d_gain_feed = norm_f_back(d_feed)
     d_hidden = grad_out + d_hidden_part
     d_attn = d_hidden.astype(jnp.bfloat16)
-    d_head = absolute_pair(contract_pair(d_attn, w_out))
-    out_grad = weight_grad(head_rel, d_attn)
-    d_mixed, d_head_gain, back_pairs = pull_call(reach, mixed, d_head, head_gain, flags, pairs)
-    end_states = scan_call(back_pairs, True, 1)
+    d_head = contract_rows(d_attn, full, 3 * model_width, after=lower_halves)
+
+    def feed_upper(place, after):
+        starts = (0, 1)[: len(sent[place])]
+        return outer_call(
+            sources, feed_grads[place], half_places[place % 2][0], None, sent[place], starts, after
+        )
+
+    def chip_sum(total, part):
+        for bit in reversed(chip_orders[part][:-1]):
+            total = halved_sum(total, bit)
+        return total
+
+    def device_sum(totals):
+        half = totals[0].shape[0] // 2
+        mine = [total[:half] for total in totals]
+        theirs = [swapped(total[half:], 1) for total in totals]
+        return over_groups(jnp.concatenate(mine + theirs, axis=1))
+
+    def both_halves(grads):
+        width = grads.shape[1] // 2
+        mine = lax.dynamic_slice_in_dim(grads, my_core * width, width, 1)
+        theirs = lax.dynamic_slice_in_dim(grads, (1 - my_core) * width, width, 1)
+        return jnp.concatenate([mine, swapped(theirs, 1)], axis=0)
+
+    d_mixed, d_head_gain, back_pairs = pull_call(
+        reach, mixed, d_head, head_gain, flags, pairs, after=(sent[0][0], sent[1][0])
+    )
+    upper_first = [feed_upper(place, ()) for place in range(2)]
+    end_states = scan_call(back_pairs, True, 1, after=upper_first)
+    chip_first = [chip_sum(total, part) for part, total in enumerate(upper_first)]
+    upper_second = [feed_upper(place, (end_states,)) for place in range(2, 4)]
+    chip_second = [chip_sum(total, part) for part, total in enumerate(upper_second)]
+    both_attn = both_halves(d_attn)
+    plain_sources = [
+        relative(jnp.concatenate([rows, swapped(rows, 1)], axis=0), pair_masks[0])
+        for rows in (normed_low, head_low)
+    ]
     d_queries, d_keys, d_values, d_betas = back_call(
         row_start,
         flags,
@@ -703,6 +1528,7 @@
         start_states,
         end_states,
         d_mixed,
+        after=upper_second,
     )
     d_logit32 = d_betas * live_rows[:, None] * sigmoid_val * (1.0 - sigmoid_val)
     d_logit = d_logit32.astype(jnp.bfloat16)
@@ -714,35 +1540,110 @@
         from_next, ((row_count - (tap_count - 1), 0), (0, 0))
     )
     d_pre = d_own.astype(jnp.bfloat16)
-    d_normed = absolute_pair(contract_pair(d_pre, w_qkv)) + contract(d_logit, w_beta)
-    qkv_grad = weight_grad(normed_rel, d_pre)
+    both_pre = both_halves(d_pre)
+    fine = model_width // 4
+
+    def plain_grads(part):
+        kinds = [
+            both_pre[:, (3 * part + kind) * fine : (3 * part + kind + 1) * fine]
+            for kind in range(3)
+        ]
+        return jnp.stack(kinds + [both_attn[:, part * fine : (part + 1) * fine]])
+
+    plain_slopes = [plain_grads(part) for part in range(2)]
+    plain_lower = [
+        outer_call(
+            plain_sources, plain_slopes[part], half_places[part][1], after=(*chip_first, *chip_second)
+        )
+        for part in range(2)
+    ]
+    plain_upper = [
+        outer_call(plain_sources, plain_slopes[part], half_places[part][0]) for part in range(2)
+    ]
+    d_normed = contract(d_logit, w_beta) + contract_rows(d_pre, full, 0)
+    feed_kept = [device_sum(chip_first), device_sum(chip_second)]
     d_input_part, d_gain_mixer = norm_a_back(d_normed)
     input_grad = (d_hidden + d_input_part).astype(jnp.bfloat16)
-    replicated = jnp.sum(
-        lax.all_gather(
-            jnp.concatenate([d_head_gain[0], jnp.sum(d_logit32, axis=0)])[None],
-            ("seq", "grp"),
-            axis=0,
-            tiled=True,
-        ),
-        axis=0,
-    )
-    sharded = lax.psum_scatter(
-        jnp.concatenate(
-            [
-                outer(normed_low, d_logit),
-                d_kernel[:model_width],
-                d_kernel[model_width : 2 * model_width],
-                d_kernel[2 * model_width :],
-                d_gain_mixer[:, None],
-                d_gain_feed[:, None],
-            ],
-            axis=1,
-        ),
-        ("seq", "grp"),
-        scatter_dimension=0,
-        tiled=True,
-    )
+    small_grads = jnp.concatenate(
+        [
+            lax.dot_general(
+                normed_low, d_logit, (((0,), (0,)), ((), ())), preferred_element_type=F32
+            ),
+            d_kernel[:model_width],
+            d_kernel[model_width : 2 * model_width],
+            d_kernel[2 * model_width :],
+            d_gain_mixer[:, None],
+            d_gain_feed[:, None],
+        ],
+        axis=1,
+    )
+    small_both = jnp.pad(
+        jnp.where(my_core == 0, small_grads + swapped(small_grads, 1), 0.0).astype(LOW),
+        ((0, 0), (0, 128 - small_grads.shape[1])),
+    )
+    block_rows = model_width // lax.axis_size("seq")
+    small_blocks = [
+        lax.dynamic_slice_in_dim(
+            small_both, (lax.axis_index("seq") ^ mask) * block_rows, block_rows, 0
+        )
+        for mask in pair_masks[0]
+    ]
+    half_blocks = len(small_blocks) // 2
+    small_upper = jnp.concatenate(small_blocks[:half_blocks], axis=0)
+    small_lower = jnp.concatenate(small_blocks[half_blocks:], axis=0)
+    vector = jnp.concatenate([d_head_gain[0], jnp.sum(d_logit32, axis=0)])
+    padded = jnp.zeros((8, 256), F32).at[0, : vector.shape[0]].set(vector)
+    plain_sum, small_sum, everywhere = reduce_call(
+        [
+            (plain_lower, plain_upper, 8),
+            ((small_lower, small_lower), (small_upper, small_upper), 1),
+        ],
+        padded,
+        chip_orders,
+        3,
+    )
+    replicated = everywhere[0, : vector.shape[0]]
+
+    def in_order(mine, other):
+        return jnp.concatenate(
+            [jnp.where(my_core == 0, mine, other), jnp.where(my_core == 0, other, mine)], axis=1
+        )
+
+    fine = fine // 2
+    groups = [plain_sum[:, at * fine : (at + 1) * fine] for at in range(32)]
+    qkv_grad, out_grad = [
+        in_order(
+            *[
+                jnp.concatenate(
+                    [
+                        groups[4 * kind + 2 * owner + part]
+                        for part in range(2)
+                        for kind in range(*span)
+                    ],
+                    axis=1,
+                )
+                for owner in range(2)
+            ]
+        )
+        for span in ((0, 6), (6, 8))
+    ]
+    feed_sums = []
+    for kind in range(3):
+        halves = []
+        for owner in range(2):
+            for chunk in range(2):
+                at = owner * feed_kept[chunk].shape[1] // 2
+                for start, stop in spans[2 * chunk : 2 * chunk + 2]:
+                    width = stop - start
+                    halves.append(
+                        feed_kept[chunk][:, at + kind * width : at + (kind + 1) * width]
+                    )
+                    at = at + 3 * width
+        feed_sums.append(
+            in_order(jnp.concatenate(halves[:4], axis=1), jnp.concatenate(halves[4:], axis=1))
+        )
+    gate_grad, up_grad, down_grad = feed_sums
+    sharded = jnp.where(my_core == 0, small_sum[:, :128], small_sum[:, 256:384])
     taps_at = head_count + 3 * tap_count
     return (
         block_out,

time: 1840 us -> 1230 us (0.67)
  waiting for transfers between devices: 772 us -> 29.7 us
  Pallas kernels: 274 us -> 862 us
  matrix products: 237 us -> 24.5 us
  blocking collectives: 117 us -> 0 us
  local copies, waits for them, and re-layouts: 222 us -> 149 us
  starting transfers between devices: 68.4 us -> 26 us
    ppermute x100 -> x32, waiting for transfers between devices: 673 us -> 29.6 us  [swapped(): lax.ppermute(value, 'seq', [(place, place ^ bit) for place in range(count)])]
    pallas_call x6 -> x26, Pallas kernels: 274 us -> 862 us  [the longest x22 336 us: launch(): pl.pallas_call(body, in_specs=[pl.BlockSpec(memory_space=pl.ANY)] * count...]
    dot_general x31 -> x3, matrix products: 148 us -> 18.8 us  [the longest x1 12.3 us: local(): own_pre = jnp.dot(normed_low, w_qkv, preferred_element_type=F32).astype(LOW)]
    all_gather x5 -> x2, waiting for transfers between devices: 89.6 us -> 0.02 us  [along_groups(): return lax.all_gather(shard, 'grp', axis=0, tiled=True)]
    dot_general x11 -> x1, matrix products: 87 us -> 3.35 us  [contract(): lax.dot_general(left, right, (((1,), (1,)), ((), ())), preferred_element_...]
    all_gather x1 -> x0, blocking collectives: 74.9 us -> none  [local(): lax.all_gather(jnp.concatenate([mixer_gain[:, None], feed_gain[:, None],...]
    unnamed x491 -> x262, local copies, waits for them, and re-layouts: 156 us -> 92.8 us
    unnamed x1 -> x0, blocking collectives: 42.1 us -> none
  transfers between devices with their start and end apart: 113 -> 38, of which waited for: 38 -> 5; matrix products, arithmetic and copies ran while one was open for 20% -> 19% of each run, Pallas kernels for 0% -> 56%
where the time goes in v2:
time: 1230 us; the launch traced here: 1220 us
  Pallas kernels  862 us (70%)
  local copies, waits for them, and re-layouts  149 us (12%)
  other arithmetic  101 us (8%)
  waiting for transfers between devices  29.7 us (2%)
  between operations  26.3 us (2%)
  starting transfers between devices  26 us (2%)
  matrix products  24.5 us (2%)
    pallas_call x22, Pallas kernels, launch(): pl.pallas_call(body, in_specs=[pl.BlockSpec(memory_space=pl.ANY)] * count...  336 us
    pallas_call x1, Pallas kernels, reduce_call(): pl.pallas_call(functools.partial(reduce_kernel, len(after), group_size, o...  181 us
    pallas_call x2, Pallas kernels, scan_call(): pl.pallas_call(functools.partial(scan_kernel, len(after), backwards, grou...  175 us
    pallas_call x1, Pallas kernels, gather_call(): pl.pallas_call(functools.partial(gather_kernel, group_size, bits, orders,...  170 us
    unnamed x262, local copies, waits for them, and re-layouts  92.8 us
    ppermute x32, waiting for transfers between devices, swapped(): lax.ppermute(value, 'seq', [(place, place ^ bit) for place in range(count)])  29.6 us
  transfers between devices with their start and end apart: 38, of which 5 were waited for; matrix products, arithmetic and copies ran while one was open for 19% of the time, Pallas kernels for 56%

profile of v2, /device:TPU:0, one launch (start us, length us, event | category | flops | bytes accessed | tf_op | source)
XLA Modules:
  0.0 1217.6 jit_solution(2633992418262256506)
XLA Ops:
  27.9 1.8 constant_dynamic-update-slice_fusion.26
  29.7 170.0 %shard_map.350 = (bf16[2048,8320]{1,0:T(8,128)(2,1)}, bf16[512,2304]{1,0:T(8,128)(2,1)}, bf16[512,2304]{1,0:T(8,128)(2,1)}, bf16[256,4608]{1,0:T(8,128)(2,1)}) custom-call(bf16[64,8320]{1,0:T(8,128)(2,1)} %copy-done.37, bf16[64,9216]{1,0:T(8,128)(2,1)} %get-tuple-element.285.feed), custom_call_target="tpu_custom_call" | custom-call | flops 1 | bytes 1 | tf_op jit(solution)/shard_map/pallas_call | solution.py:992
  206.4 1.8 convert_reduce_fusion
  209.2 12.3 %fusion.4 = bf16[256,6144]{1,0:T(8,128)(2,1)S(1)} fusion(bf16[256,2048]{1,0:T(8,128)(2,1)S(1)} %fusion.15, bf16[2048,8320]{1,0:T(8,128)(2,1)} %get-tuple-element.62.refs_5_.refs_1_), kind=kOutput, calls=%fused_computation.5 | convolution fusion | flops 6444023808 | bytes 29360128 | tf_op jit(solution)/shard_map/dot_general | solution.py:1383
  225.9 3.3 fusion.97
  233.1 20.4 %collective-permute-done.refs_0_.refs_3_.refs_7_.refs_11_ = bf16[512,2304]{1,0:T(8,128)(2,1)} collective-permute-done((bf16[512,2304]{1,0:T(8,128)(2,1)}, bf16[512,2304]{1,0:T(8,128)(2,1)}, u32[]{:S(2)}, u32[]{:S(2)}) %collective-permute-start) | collective-permute-done | bytes 2359328 | tf_op jit(solution)/shard_map/ppermute | solution.py:485
  253.5 4.2 pad_maximum_fusion
  258.2 4.1 pad_maximum_fusion.1
  264.6 2.3 broadcast_multiply_fusion.1
  269.3 2.8 maximum_convert_fusion
  272.3 7.8 fusion.10
  280.1 94.8 %shard_map.351 = (f32[16,256,256]{2,1,0:T(8,128)}, f32[16,256,256]{2,1,0:T(8,128)}, f32[16,256,256]{2,1,0:T(8,128)}, f32[256,2048]{1,0:T(8,128)}, f32[256,2048]{1,0:T(8,128)}, /*index=5*/bf16[16,128,256]{2,1,0:T(8,128)(2,1)}) custom-call(bf16[512,2304]{1,0:T(8,128)(2,1)} %collective-permute-done.refs_0_.refs_3_.refs_7_.refs_11_, ...), custom_call_target="tpu_custom_call" | custom-call | flops 1 | bytes 1 | tf_op jit(solution)/shard_map/pallas_call | solution.py:38
  376.2 6.5 shard_map.352.refs_4_.refs_8_.refs_12_
  395.6 4.8 shard_map.353.refs_16_.refs_20_.refs_24_
  406.9 88.2 %shard_map.354.refs_6_.refs_12_ = bf16[16,128,128]{2,1,0:T(8,128)(2,1)} custom-call(bf16[16,128,256]{2,1,0:T(8,128)(2,1)} %get-tuple-element.63.refs_0_.refs_7_), custom_call_target="tpu_custom_call" | custom-call | flops 1 | bytes 1 | tf_op jit(solution)/shard_map/pallas_call | solution.py:461
  495.1 12.2 %shard_map.355 = (f32[256,2048]{1,0:T(8,128)}, bf16[256,2048]{1,0:T(8,128)(2,1)}) custom-call(bf16[512,2304]{1,0:T(8,128)(2,1)} %collective-permute-done.6.refs_0_.refs_5_.refs_9_.refs_13_, bf16[512,2304]{1,0:T(8,128)(2,1)} %collective-permute-done.7.refs_1_.refs_6_.refs_10_.refs_14_, ...), custom_call_target="tpu_custom_call" | custom-call | flops 1 | bytes 1 | tf_op jit(solution)/shard_map/pallas_call | solution.py:38
  507.4 6.3 multiply_reduce_fusion.6
  520.9 31.5 %shard_map.356 = (bf16[3,512,768]{2,1,0:T(8,128)(2,1)}, bf16[3,512,768]{2,1,0:T(8,128)(2,1)}, f32[512,2048]{1,0:T(8,128)}, f32[512,2048]{1,0:T(8,128)}) custom-call(bf16[512,2048]{1,0:T(8,128)(2,1)} %copy-done, bf16[512,2048]{1,0:T(8,128)(2,1)} %copy-done.1, bf16[512,2304]{1,0:T(8,128)(2,1)} %get-tuple-element.60.refs_2_.refs_6_.refs_10_, ...), custom_call_target="tpu_custom_call" | custom-call | flops 1 | bytes 1 | tf_op jit(solution)/shard_map/pallas_call | solution.py:38
  552.4 6.8 shard_map.357.refs_0_
  559.2 7.1 shard_map.358.refs_1_
  569.4 29.5 %shard_map.359 = (bf16[3,512,768]{2,1,0:T(8,128)(2,1)}, bf16[3,512,512]{2,1,0:T(8,128)(2,1)}, f32[512,2048]{1,0:T(8,128)}, f32[512,2048]{1,0:T(8,128)}) custom-call(bf16[1024,2304]{1,0:T(8,128)(2,1)} %shard_map.357.refs_0_, bf16[1024,2304]{1,0:T(8,128)(2,1)} %shard_map.358.refs_1_, bf16[512,2048]{1,0:T(8,128)(2,1)} %copy-done, bf16[512,2048]{1,0:T(8,128)(2,1)} %copy-done.1, ...), custom_call_target="tpu_custom_call" | custom-call | flops 1 | bytes 1 | tf_op jit(solution)/shard_map/pallas_call | solution.py:38
  598.9 4.8 fusion.98
  603.7 2.3 fusion.99
  607.5 6.7 shard_map.362.refs_2_
  628.9 6.1 shard_map.363.refs_3_
  641.7 1.7 dynamic-slice_dynamic-update-slice_fusion.17
  665.4 2.4 multiply_reduce_fusion.4
  667.8 5.6 fusion.95
  673.4 7.3 shard_map.364.refs_4_
  680.7 8.3 shard_map.360.refs_0_
  689.0 8.3 shard_map.361.refs_1_
  697.4 14.1 %shard_map.365 = (f32[256,2048]{1,0:T(8,128)}, f32[1,128]{1,0:T(1,128)}, bf16[16,128,256]{2,1,0:T(8,128)(2,1)}) custom-call(bf16[1024,2304]{1,0:T(8,128)(2,1)} %collective-permute-done.16.refs_5_.refs_0_, bf16[1024,2304]{1,0:T(8,128)(2,1)} %collective-permute-done.17.refs_5_.refs_1_, f32[256,2048]{1,0:T(8,128)} %get-tuple-element.66.refs_4_.refs_2_, ...), custom_call_target="tpu_custom_call" | custom-call | flops 1 | bytes 1 | tf_op jit(solution)/shard_map/pallas_call | solution.py:38
  711.5 86.6 %shard_map.366.refs_0_.refs_13_ = bf16[16,128,128]{2,1,0:T(8,128)(2,1)} custom-call(bf16[1024,2304]{1,0:T(8,128)(2,1)} %shard_map.360.refs_0_, bf16[1024,2304]{1,0:T(8,128)(2,1)} %shard_map.361.refs_1_, bf16[16,128,256]{2,1,0:T(8,128)(2,1)} %get-tuple-element.78.refs_2_), custom_call_target="tpu_custom_call" | custom-call | flops 1 | bytes 1 | tf_op jit(solution)/shard_map/pallas_call | solution.py:461
  798.1 6.7 shard_map.368.refs_1_
  804.8 2.8 slice.533
  810.7 8.5 shard_map.367.refs_0_
  819.2 3.3 slice.531
  826.8 2.5 fusion.38
  831.0 3.3 slice.529
  836.2 32.6 %shard_map.369 = (f32[256,2048]{1,0:T(8,128)}, f32[256,2048]{1,0:T(8,128)}, f32[256,2048]{1,0:T(8,128)}, f32[256,16]{1,0:T(8,128)}) custom-call(bf16[1024,2304]{1,0:T(8,128)(2,1)} %shard_map.367.refs_0_, bf16[1024,1536]{1,0:T(8,128)(2,1)} %shard_map.368.refs_1_, s32[256,1]{1,0:T(8,128)} %copy.107.refs_2_, s32[1,256]{1,0:T(1,128)} %bitcast.93, ...), custom_call_target="tpu_custom_call" | custom-call | flops 1 | bytes 1 | tf_op jit(solution)/shard_map/pallas_call | solution.py:38
  868.8 1.9 constant_dynamic-update-slice_fusion.33
  873.0 2.6 add_convert_fusion.3.refs_3_
  877.1 2.9 add_convert_fusion.refs_2_
  881.6 8.7 multiply_reduce_fusion.3
  890.3 3.0 pad_maximum_fusion.3
  894.1 10.6 multiply_multiply_fusion.2
  904.8 8.1 pad_add_fusion
  914.2 3.2 add_convert_fusion.1.refs_1_
  918.9 2.4 collective-permute-start.31
  921.3 5.7 collective-permute-done.21
  927.0 2.3 add_convert_fusion.2.refs_0_
  933.6 2.5 pad_maximum_fusion.2
  936.1 3.6 fusion.9.refs_0_
  939.7 2.0 constant_dynamic-slice_fusion.1
  942.8 17.7 %shard_map.370 = f32[256,2048]{1,0:T(8,128)} custom-call(bf16[256,6144]{1,0:T(8,128)(2,1)} %copy-done.16, bf16[2048,8320]{1,0:T(8,128)(2,1)} %get-tuple-element.62.refs_5_.refs_1_), custom_call_target="tpu_custom_call" | custom-call | flops 1 | bytes 1 | tf_op jit(solution)/shard_map/pallas_call | solution.py:38
  960.4 3.4 fusion.16
  969.2 2.3 copy.114
  971.4 1.8 select_convert_fusion
  974.1 2.1 fusion.37
  980.1 6.4 shard_map.373.refs_2_
  986.6 6.4 shard_map.374.refs_3_
  993.0 6.4 shard_map.371.refs_0_
  999.4 6.8 shard_map.372.refs_1_
  1007.8 181.3 %shard_map.375 = (f32[64,8192]{1,0:T(8,128)}, f32[64,512]{1,0:T(8,128)}, f32[8,256]{1,0:T(8,128)}) custom-call(bf16[1024,2048]{1,0:T(8,128)(2,1)} %shard_map.371.refs_0_, bf16[1024,2048]{1,0:T(8,128)(2,1)} %shard_map.372.refs_1_, bf16[1024,2048]{1,0:T(8,128)(2,1)} %shard_map.373.refs_2_, bf16[1024,2048]{1,0:T(8,128)(2,1)} %shard_map.374.refs_3_, ...), custom_call_target="tpu_custom_call" | custom-call | flops 1 | bytes 1 | tf_op jit(solution)/shard_map/pallas_call | solution.py:1238
  (437 shorter events, 165.0 us)
Async XLA Ops:
  7.2 16.7 %copy-start.40 = (bf16[64,5632]{1,0:T(8,128)(2,1)S(1)}, bf16[64,5632]{1,0:T(8,128)(2,1)}, u32[]{:S(2)}) copy-start(bf16[64,5632]{1,0:T(8,128)(2,1)} %param.42) | copy-start | bytes 2162692
  7.2 18.9 %copy-start.41 = (bf16[64,2048]{1,0:T(8,128)(2,1)S(1)}, bf16[64,2048]{1,0:T(8,128)(2,1)}, u32[]{:S(2)}) copy-start(bf16[64,2048]{1,0:T(8,128)(2,1)} %param.31) | copy-start | bytes 786436
  7.2 18.9 %copy-start.42 = (bf16[64,2048]{1,0:T(8,128)(2,1)S(1)}, bf16[64,2048]{1,0:T(8,128)(2,1)}, u32[]{:S(2)}) copy-start(bf16[64,2048]{1,0:T(8,128)(2,1)} %param.32) | copy-start | bytes 786436
  7.2 18.9 %copy-start.43 = (bf16[64,2048]{1,0:T(8,128)(2,1)S(1)}, bf16[64,2048]{1,0:T(8,128)(2,1)}, u32[]{:S(2)}) copy-start(bf16[64,2048]{1,0:T(8,128)(2,1)} %param.39) | copy-start | bytes 786436
  7.2 262.1 %all-gather.5.cloned.1.call-start = ((), (), s32[]{:S(2)}) async-start(), calls=%async_computation.3 | async-start | bytes 2457600 | tf_op jit(solution)/shard_map/all_gather | solution.py:1297
  7.3 19.0 %copy-start.39 = (bf16[64,5632]{1,0:T(8,128)(2,1)S(1)}, bf16[64,5632]{1,0:T(8,128)(2,1)}, u32[]{:S(2)}) copy-start(bf16[64,5632]{1,0:T(8,128)(2,1)} %param.41) | copy-start | bytes 2162692
  27.9 177.7 %copy-start.21 = (bf16[256,2048]{1,0:T(8,128)(2,1)S(1)}, bf16[256,2048]{1,0:T(8,128)(2,1)}, u32[]{:S(2)}) copy-start(bf16[256,2048]{1,0:T(8,128)(2,1)} %param.25) | copy-start | bytes 3145732
  199.6 53.9 %collective-permute-start = (bf16[512,2304]{1,0:T(8,128)(2,1)}, bf16[512,2304]{1,0:T(8,128)(2,1)}, u32[]{:S(2)}, u32[]{:S(2)}) collective-permute-start(bf16[512,2304]{1,0:T(8,128)(2,1)} %get-tuple-element.60.refs_2_.refs_6_.refs_10_), channel_id=1, source_target_pairs={{0,16},{4,20},{8,24},{12,28},{16,0},{20,4},{24,8},{28,12},{1,17},{... | collective-permute-start | bytes 7077896 | tf_op jit(solution)/shard_map/ppermute | solution.py:485
  201.2 57.0 %collective-permute-start.1 = (bf16[512,2304]{1,0:T(8,128)(2,1)}, bf16[512,2304]{1,0:T(8,128)(2,1)}, u32[]{:S(2)}, u32[]{:S(2)}) collective-permute-start(bf16[512,2304]{1,0:T(8,128)(2,1)} %get-tuple-element.61.refs_14_.refs_18_.refs_22_), channel_id=1, source_target_pairs={{0,8},{4,12},{8,0},{12,4},{16,24},{20,28},{24,16},{28,20},{1,9},{5... | collective-permute-start | bytes 7077896 | tf_op jit(solution)/shard_map/ppermute | solution.py:485
  205.5 169.3 %all-gather.3.cloned.1.call-start = ((), (), s32[]{:S(2)}) async-start(), calls=%async_computation.2 | async-start | bytes 2457600 | tf_op jit(solution)/shard_map/all_gather | solution.py:1297
  206.4 15.1 %copy-start.69 = (f32[256]{0:T(256)}, f32[256]{0:T(256)S(1)}, u32[]{:S(2)}) copy-start(f32[256]{0:T(256)S(1)} %fusion.91) | copy-start | bytes 3076
  209.2 309.3 %copy-start.5 = (bf16[256,2048]{1,0:T(8,128)(2,1)}, bf16[256,2048]{1,0:T(8,128)(2,1)S(1)}, u32[]{:S(2)}) copy-start(bf16[256,2048]{1,0:T(8,128)(2,1)S(1)} %fusion.15) | copy-start | bytes 3145732
  209.2 16.5 %copy-start.76 = (s32[8]{0:T(128)S(1)}, s32[8]{0:T(128)}, u32[]{:S(2)}) copy-start(s32[8]{0:T(128)} %param.27) | copy-start | bytes 100
  223.8 45.6 %collective-permute-start.2 = (bf16[3,6144]{1,0:T(4,128)(2,1)}, bf16[3,6144]{1,0:T(4,128)(2,1)S(1)}, u32[]{:S(2)}, u32[]{:S(2)}) collective-permute-start(bf16[3,6144]{1,0:T(4,128)(2,1)} %slice.515), channel_id=1, source_target_pairs={{0,1},{1,2},{2,3},{3,4},{4,5},{5,6},{6,7},{7,8},{8,9},{9,10},{10,1... | collective-permute-start | bytes 110600 | tf_op jit(solution)/shard_map/ppermute | solution.py:19
  225.1 178.7 %collective-permute-start.11 = (bf16[256,2048]{1,0:T(8,128)(2,1)}, bf16[256,2048]{1,0:T(8,128)(2,1)}, u32[]{:S(2)}, u32[]{:S(2)}) collective-permute-start(bf16[256,2048]{1,0:T(8,128)(2,1)} %param.26), channel_id=1, source_target_pairs={{0,4},{4,0},{8,12},{12,8},{16,20},{20,16},{24,28},{28,24},{1,5},{5... | collective-permute-start | bytes 3145736 | tf_op jit(solution)/shard_map/ppermute | solution.py:485
  225.7 977.9 %reduce-scatter.5.cloned.1.call-start = ((), (), s32[]{:S(2)}) async-start(), calls=%async_computation.5 | async-start | bytes 4915200 | tf_op jit(solution)/shard_map/reduce_scatter | solution.py:558
  225.9 27.6 %copy-start.10 = (bf16[512,2304]{1,0:T(8,128)(2,1)S(1)}, bf16[512,2304]{1,0:T(8,128)(2,1)}, u32[]{:S(2)}) copy-start(bf16[512,2304]{1,0:T(8,128)(2,1)} %get-tuple-element.60.refs_2_.refs_6_.refs_10_) | copy-start | bytes 7077892
  233.1 34.6 %copy-start.60 = (s32[256]{0:T(256)}, s32[256]{0:T(256)S(1)}, u32[]{:S(2)}) copy-start(s32[256]{0:T(256)S(1)} %select_reduce_fusion) | copy-start | bytes 3076
  233.1 25.1 %copy-start.11 = (bf16[512,2304]{1,0:T(8,128)(2,1)S(1)}, bf16[512,2304]{1,0:T(8,128)(2,1)}, u32[]{:S(2)}) copy-start(bf16[512,2304]{1,0:T(8,128)(2,1)} %get-tuple-element.61.refs_14_.refs_18_.refs_22_) | copy-start | bytes 7077892
  257.7 117.1 %collective-permute-start.3 = (bf16[1024,2304]{1,0:T(8,128)(2,1)}, bf16[1024,2304]{1,0:T(8,128)(2,1)}, u32[]{:S(2)}, u32[]{:S(2)}) collective-permute-start(bf16[1024,2304]{1,0:T(8,128)(2,1)} %pad_maximum_fusion), channel_id=1, source_target_pairs={{0,8},{4,12},{8,0},{12,4},{16,24},{20,28},{24,16},{28,20},{1,9},{5... | collective-permute-start | bytes 14155784 | tf_op jit(solution)/shard_map/ppermute | solution.py:485
  262.4 112.5 %collective-permute-start.4 = (bf16[1024,2304]{1,0:T(8,128)(2,1)}, bf16[1024,2304]{1,0:T(8,128)(2,1)}, u32[]{:S(2)}, u32[]{:S(2)}) collective-permute-start(bf16[1024,2304]{1,0:T(8,128)(2,1)} %pad_maximum_fusion.1), channel_id=1, source_target_pairs={{0,16},{4,20},{8,24},{12,28},{16,0},{20,4},{24,8},{28,12},{1,17},{... | collective-permute-start | bytes 14155784 | tf_op jit(solution)/shard_map/ppermute | solution.py:485
  269.3 105.5 %collective-permute-start.5 = (bf16[256,3840]{1,0:T(8,128)(2,1)}, bf16[256,3840]{1,0:T(8,128)(2,1)S(1)}, u32[]{:S(2)}, u32[]{:S(2)}) collective-permute-start(bf16[256,3840]{1,0:T(8,128)(2,1)} %all-gather.5.cloned.1.call-done), channel_id=1, source_target_pairs={{0,4},{4,0},{8,12},{12,8},{16,20},{20,16},{24,28},{28,24},{1,5},{5... | collective-permute-start | bytes 5898248 | tf_op jit(solution)/shard_map/ppermute | solution.py:485
  382.7 112.5 %collective-permute-start.6 = (bf16[512,2304]{1,0:T(8,128)(2,1)}, bf16[512,2304]{1,0:T(8,128)(2,1)}, u32[]{:S(2)}, u32[]{:S(2)}) collective-permute-start(bf16[512,2304]{1,0:T(8,128)(2,1)} %shard_map.352.refs_4_.refs_8_.refs_12_), channel_id=1, source_target_pairs={{0,16},{4,20},{8,24},{12,28},{16,0},{20,4},{24,8},{28,12},{1,17},{... | collective-permute-start | bytes 7077896 | tf_op jit(solution)/shard_map/ppermute | solution.py:485
  383.0 112.1 %collective-permute-start.7 = (bf16[512,2304]{1,0:T(8,128)(2,1)}, bf16[512,2304]{1,0:T(8,128)(2,1)}, u32[]{:S(2)}, u32[]{:S(2)}) collective-permute-start(bf16[512,2304]{1,0:T(8,128)(2,1)} %shard_map.352.refs_4_.refs_8_.refs_12_), channel_id=1, source_target_pairs={{0,8},{4,12},{8,0},{12,4},{16,24},{20,28},{24,16},{28,20},{1,9},{5... | collective-permute-start | bytes 7077896 | tf_op jit(solution)/shard_map/ppermute | solution.py:485
  400.4 94.7 %collective-permute-start.8 = (bf16[512,1536]{1,0:T(8,128)(2,1)}, bf16[512,1536]{1,0:T(8,128)(2,1)}, u32[]{:S(2)}, u32[]{:S(2)}) collective-permute-start(bf16[512,1536]{1,0:T(8,128)(2,1)} %shard_map.353.refs_16_.refs_20_.refs_24_), channel_id=1, source_target_pairs={{0,8},{4,12},{8,0},{12,4},{16,24},{20,28},{24,16},{28,20},{1,9},{5... | collective-permute-start | bytes 4718600 | tf_op jit(solution)/shard_map/ppermute | solution.py:485
  400.7 94.4 %collective-permute-start.9 = (bf16[512,1536]{1,0:T(8,128)(2,1)}, bf16[512,1536]{1,0:T(8,128)(2,1)}, u32[]{:S(2)}, u32[]{:S(2)}) collective-permute-start(bf16[512,1536]{1,0:T(8,128)(2,1)} %shard_map.353.refs_16_.refs_20_.refs_24_), channel_id=1, source_target_pairs={{0,16},{4,20},{8,24},{12,28},{16,0},{20,4},{24,8},{28,12},{1,17},{... | collective-permute-start | bytes 4718600 | tf_op jit(solution)/shard_map/ppermute | solution.py:485
  403.7 2.7 collective-permute-start.25
  406.5 109.2 %copy-start.7 = (bf16[256,2048]{1,0:T(8,128)(2,1)}, bf16[256,2048]{1,0:T(8,128)(2,1)S(1)}, u32[]{:S(2)}) copy-start(bf16[256,2048]{1,0:T(8,128)(2,1)S(1)} %collective-permute-done.25) | copy-start | bytes 3145732
  495.1 12.3 %copy-start.22 = (bf16[256,2048]{1,0:T(8,128)(2,1)S(1)}, bf16[256,2048]{1,0:T(8,128)(2,1)}, u32[]{:S(2)}) copy-start(bf16[256,2048]{1,0:T(8,128)(2,1)} %param.25) | copy-start | bytes 3145732
  513.7 3.0 collective-permute-start.26
  513.8 55.7 %collective-permute-start.12 = (bf16[512,2304]{1,0:T(8,128)(2,1)}, bf16[512,2304]{1,0:T(8,128)(2,1)}, u32[]{:S(2)}, u32[]{:S(2)}) collective-permute-start(bf16[512,2304]{1,0:T(8,128)(2,1)} %collective-permute-done.6.refs_0_.refs_5_.refs_9_.refs_13_), channel_id=1, source_target_pairs={{0,8},{4,12},{8,0},{12,4},{16,24},{20,28},{24,16},{28,20},{1,9},{5... | collective-permute-start | bytes 7077896 | tf_op jit(solution)/shard_map/ppermute | solution.py:485
  515.2 2.7 collective-permute-start.10
  515.7 53.7 %collective-permute-start.13 = (bf16[512,1536]{1,0:T(8,128)(2,1)}, bf16[512,1536]{1,0:T(8,128)(2,1)}, u32[]{:S(2)}, u32[]{:S(2)}) collective-permute-start(bf16[512,1536]{1,0:T(8,128)(2,1)} %collective-permute-done.8.refs_2_.refs_18_.refs_22_.refs_26_), channel_id=1, source_target_pairs={{0,16},{4,20},{8,24},{12,28},{16,0},{20,4},{24,8},{28,12},{1,17},{... | collective-permute-start | bytes 4718600 | tf_op jit(solution)/shard_map/ppermute | solution.py:485
  520.9 31.5 %copy-start.4 = (bf16[512,2048]{1,0:T(8,128)(2,1)}, bf16[512,2048]{1,0:T(8,128)(2,1)S(1)}, u32[]{:S(2)}) copy-start(bf16[512,2048]{1,0:T(8,128)(2,1)S(1)} %fusion.57.refs_4_.refs_5_.refs_0_.refs_1_) | copy-start | bytes 6291460
  566.3 114.4 %collective-permute-start.16 = (bf16[1024,2304]{1,0:T(8,128)(2,1)S(1)}, bf16[1024,2304]{1,0:T(8,128)(2,1)}, u32[]{:S(2)}, u32[]{:S(2)}) collective-permute-start(bf16[1024,2304]{1,0:T(8,128)(2,1)S(1)} %copy-done.9), channel_id=1, source_target_pairs={{0,8},{4,12},{8,0},{12,4},{16,24},{20,28},{24,16},{28,20},{1,9},{5... | collective-permute-start | bytes 14155784 | tf_op jit(solution)/shard_map/ppermute | solution.py:485
  567.4 121.7 %collective-permute-start.17 = (bf16[1024,2304]{1,0:T(8,128)(2,1)}, bf16[1024,2304]{1,0:T(8,128)(2,1)}, u32[]{:S(2)}, u32[]{:S(2)}) collective-permute-start(bf16[1024,2304]{1,0:T(8,128)(2,1)} %shard_map.358.refs_1_), channel_id=1, source_target_pairs={{0,16},{4,20},{8,24},{12,28},{16,0},{20,4},{24,8},{28,12},{1,17},{... | collective-permute-start | bytes 14155784 | tf_op jit(solution)/shard_map/ppermute | solution.py:485
  603.7 44.9 %collective-permute-start.15 = (f32[256,2048]{1,0:T(8,128)}, f32[256,2048]{1,0:T(8,128)}, u32[]{:S(2)}, u32[]{:S(2)}) collective-permute-start(f32[256,2048]{1,0:T(8,128)} %get-tuple-element.185), channel_id=1, source_target_pairs={{0,4},{4,0},{8,12},{12,8},{16,20},{20,16},{24,28},{28,24},{1,5},{5... | collective-permute-start | bytes 6291464 | tf_op jit(solution)/shard_map/ppermute | solution.py:485
  606.0 44.4 %collective-permute-start.14 = (f32[256,2048]{1,0:T(8,128)}, f32[256,2048]{1,0:T(8,128)}, u32[]{:S(2)}, u32[]{:S(2)}) collective-permute-start(f32[256,2048]{1,0:T(8,128)} %get-tuple-element.188), channel_id=1, source_target_pairs={{0,4},{4,0},{8,12},{12,8},{16,20},{20,16},{24,28},{28,24},{1,5},{5... | collective-permute-start | bytes 6291464 | tf_op jit(solution)/shard_map/ppermute | solution.py:485
  614.2 196.5 %collective-permute-start.18 = (bf16[1024,2304]{1,0:T(8,128)(2,1)}, bf16[1024,2304]{1,0:T(8,128)(2,1)}, u32[]{:S(2)}, u32[]{:S(2)}) collective-permute-start(bf16[1024,2304]{1,0:T(8,128)(2,1)} %shard_map.362.refs_2_), channel_id=1, source_target_pairs={{0,8},{4,12},{8,0},{12,4},{16,24},{20,28},{24,16},{28,20},{1,9},{5... | collective-permute-start | bytes 14155784 | tf_op jit(solution)/shard_map/ppermute | solution.py:485
  648.6 149.5 %collective-permute-start.19 = (bf16[1024,1536]{1,0:T(8,128)(2,1)}, bf16[1024,1536]{1,0:T(8,128)(2,1)}, u32[]{:S(2)}, u32[]{:S(2)}) collective-permute-start(bf16[1024,1536]{1,0:T(8,128)(2,1)} %shard_map.363.refs_3_), channel_id=1, source_target_pairs={{0,16},{4,20},{8,24},{12,28},{16,0},{20,4},{24,8},{28,12},{1,17},{... | collective-permute-start | bytes 9437192 | tf_op jit(solution)/shard_map/ppermute | solution.py:485
  807.6 64.3 %collective-permute-start.24 = (bf16[512,1536]{1,0:T(8,128)(2,1)}, bf16[512,1536]{1,0:T(8,128)(2,1)}, u32[]{:S(2)}, u32[]{:S(2)}) collective-permute-start(bf16[512,1536]{1,0:T(8,128)(2,1)} %slice.533), channel_id=1, source_target_pairs={{0,8},{4,12},{8,0},{12,4},{16,24},{20,28},{24,16},{28,20},{1,9},{5... | collective-permute-start | bytes 4718600 | tf_op jit(solution)/shard_map/ppermute | solution.py:485
  808.5 18.3 %collective-permute-start.28 = (bf16[256,1024]{1,0:T(8,128)(2,1)S(1)}, bf16[256,1024]{1,0:T(8,128)(2,1)}, u32[]{:S(2)}, u32[]{:S(2)}) collective-permute-start(bf16[256,1024]{1,0:T(8,128)(2,1)S(1)} %get-tuple-element.260), channel_id=1, source_target_pairs={{0,4},{4,0},{8,12},{12,8},{16,20},{20,16},{24,28},{28,24},{1,5},{5... | collective-permute-start | bytes 1572872 | tf_op jit(solution)/shard_map/ppermute | solution.py:485
  809.5 19.8 %slice-start.4 = ((s8[4718592]{0:T(1024)(128)(4,1)}), s8[4194304]{0:T(1024)(128)(4,1)S(1)}, s32[]{:S(2)}) async-start(s8[4718592]{0:T(1024)(128)(4,1)} %bitcast.69), calls=%async_computation.10 | async-start | bytes 8388608
  810.7 18.6 %slice-start.5 = ((s8[4718592]{0:T(1024)(128)(4,1)}), s8[524288]{0:T(1024)(128)(4,1)S(1)}, s32[]{:S(2)}) async-start(s8[4718592]{0:T(1024)(128)(4,1)} %bitcast.69), calls=%async_computation.11 | async-start | bytes 1048576
  822.5 54.6 %collective-permute-start.23 = (bf16[512,2304]{1,0:T(8,128)(2,1)}, bf16[512,2304]{1,0:T(8,128)(2,1)}, u32[]{:S(2)}, u32[]{:S(2)}) collective-permute-start(bf16[512,2304]{1,0:T(8,128)(2,1)} %slice.531), channel_id=1, source_target_pairs={{0,16},{4,20},{8,24},{12,28},{16,0},{20,4},{24,8},{28,12},{1,17},{... | collective-permute-start | bytes 7077896 | tf_op jit(solution)/shard_map/ppermute | solution.py:485
  834.3 92.7 %collective-permute-start.21 = (bf16[512,2304]{1,0:T(8,128)(2,1)}, bf16[512,2304]{1,0:T(8,128)(2,1)}, u32[]{:S(2)}, u32[]{:S(2)}) collective-permute-start(bf16[512,2304]{1,0:T(8,128)(2,1)} %slice.527), channel_id=1, source_target_pairs={{0,16},{4,20},{8,24},{12,28},{16,0},{20,4},{24,8},{28,12},{1,17},{... | collective-permute-start | bytes 7077896 | tf_op jit(solution)/shard_map/ppermute | solution.py:485
  834.9 79.3 %collective-permute-start.22 = (bf16[512,2304]{1,0:T(8,128)(2,1)}, bf16[512,2304]{1,0:T(8,128)(2,1)}, u32[]{:S(2)}, u32[]{:S(2)}) collective-permute-start(bf16[512,2304]{1,0:T(8,128)(2,1)} %slice.529), channel_id=1, source_target_pairs={{0,8},{4,12},{8,0},{12,4},{16,24},{20,28},{24,16},{28,20},{1,9},{5... | collective-permute-start | bytes 7077896 | tf_op jit(solution)/shard_map/ppermute | solution.py:485
  871.0 10.5 slice-start.10
  876.6 13.7 %collective-permute-start.33 = (bf16[256,1536]{1,0:T(8,128)(2,1)}, bf16[256,1536]{1,0:T(8,128)(2,1)}, u32[]{:S(2)}, u32[]{:S(2)}) collective-permute-start(bf16[256,1536]{1,0:T(8,128)(2,1)} %get-tuple-element.237), channel_id=1, source_target_pairs={{0,4},{4,0},{8,12},{12,8},{16,20},{20,16},{24,28},{28,24},{1,5},{5... | collective-permute-start | bytes 2359304 | tf_op jit(solution)/shard_map/ppermute | solution.py:485
  881.3 9.0 collective-permute-start.32
  893.4 311.7 %reduce-scatter.3.cloned.1.call-start = ((), (), s32[]{:S(2)}) async-start(), calls=%async_computation.4 | async-start | bytes 5898240 | tf_op jit(solution)/shard_map/reduce_scatter | solution.py:558
  894.1 20.1 %slice-start.8 = ((s8[4718592]{0:T(1024)(128)(4,1)}), s8[4194304]{0:T(1024)(128)(4,1)S(1)}, s32[]{:S(2)}) async-start(s8[4718592]{0:T(1024)(128)(4,1)} %bitcast.73), calls=%async_computation.14 | async-start | bytes 8388608
  894.1 32.8 %slice-start.6 = ((s8[4718592]{0:T(1024)(128)(4,1)}), s8[4194304]{0:T(1024)(128)(4,1)S(1)}, s32[]{:S(2)}) async-start(s8[4718592]{0:T(1024)(128)(4,1)} %bitcast.71), calls=%async_computation.12 | async-start | bytes 8388608
  904.8 9.5 slice-start.9
  904.8 22.2 %slice-start.7 = ((s8[4718592]{0:T(1024)(128)(4,1)}), s8[524288]{0:T(1024)(128)(4,1)S(1)}, s32[]{:S(2)}) async-start(s8[4718592]{0:T(1024)(128)(4,1)} %bitcast.71), calls=%async_computation.13 | async-start | bytes 1048576
  912.9 23.2 %collective-permute-start.20 = (bf16[3,6144]{1,0:T(4,128)(2,1)S(1)}, bf16[3,6144]{1,0:T(4,128)(2,1)S(1)}, u32[]{:S(2)}, u32[]{:S(2)}) collective-permute-start(bf16[3,6144]{1,0:T(4,128)(2,1)S(1)} %slice.708), channel_id=1, source_target_pairs={{1,0},{2,1},{3,2},{4,3},{5,4},{6,5},{7,6},{8,7},{9,8},{10,9},{11,1... | collective-permute-start | bytes 110600 | tf_op jit(solution)/shard_map/ppermute | solution.py:19
  918.9 13.2 %collective-permute-start.31 = (bf16[256,2304]{1,0:T(8,128)(2,1)S(1)}, bf16[256,2304]{1,0:T(8,128)(2,1)S(1)}, u32[]{:S(2)}, u32[]{:S(2)}) collective-permute-start(bf16[256,2304]{1,0:T(8,128)(2,1)S(1)} %get-tuple-element.200), channel_id=1, source_target_pairs={{0,4},{4,0},{8,12},{12,8},{16,20},{20,16},{24,28},{28,24},{1,5},{5... | collective-permute-start | bytes 3538952 | tf_op jit(solution)/shard_map/ppermute | solution.py:485
  930.7 2.8 collective-permute-start.30
  942.3 31.8 %collective-permute-start.27 = (bf16[256,3072]{1,0:T(8,128)(2,1)}, bf16[256,3072]{1,0:T(8,128)(2,1)}, u32[]{:S(2)}, u32[]{:S(2)}) collective-permute-start(bf16[256,3072]{1,0:T(8,128)(2,1)} %get-tuple-element.195), channel_id=1, source_target_pairs={{0,4},{4,0},{8,12},{12,8},{16,20},{20,16},{24,28},{28,24},{1,5},{5... | collective-permute-start | bytes 4718600 | tf_op jit(solution)/shard_map/ppermute | solution.py:485
  942.7 17.7 %copy-start.23 = (bf16[256,2048]{1,0:T(8,128)(2,1)S(1)}, bf16[256,2048]{1,0:T(8,128)(2,1)}, u32[]{:S(2)}) copy-start(bf16[256,2048]{1,0:T(8,128)(2,1)} %param.25) | copy-start | bytes 3145732
  942.7 17.7 %copy-start.53 = (f32[2048]{0:T(1024)S(1)}, f32[2048]{0:T(1024)}, u32[]{:S(2)}) copy-start(f32[2048]{0:T(1024)} %copy-done.52) | copy-start | bytes 24580
  942.7 17.7 %copy-start.70 = (f32[256]{0:T(256)S(1)}, f32[256]{0:T(256)}, u32[]{:S(2)}) copy-start(f32[256]{0:T(256)} %copy-done.69) | copy-start | bytes 3076
  965.4 3.8 collective-permute-start.29
  1189.2 9.7 copy-start.32
  (64 other events, 230.3 us)
Sparse Core Ops, SparseCore 0:
  205.6 41.9 all-gather.4
  249.7 42.2 all-gather.2
  893.5 72.8 reduce-scatter.4
  968.6 85.5 reduce-scatter.2

commit v3 on v2

--- a/solution.py
+++ b/solution.py
@@ -11,6 +11,10 @@
 LOW = jnp.bfloat16
 EPSILON = 1e-06
 VMEM_LIMIT = 56 * 1024 * 1024
+SPAN_HEADS = 4
+BACK_HEADS = 2
+HALO = 16
+AHEAD = 1
 
 
 def passed_along(value, axis, steps):
@@ -71,20 +75,21 @@
 FIRST_FIRST = ((0,), (0,))
 
 
-def inverse_unit_lower(lower, size):
+def inverse_unit_lower(lowers, size):
     row = lax.broadcasted_iota(jnp.int32, (size, size), 0)
     column = lax.broadcasted_iota(jnp.int32, (size, size), 1)
-    inverse = jnp.where(row == column, 1.0, 0.0).astype(F32)
+    eye = jnp.where(row == column, 1.0, 0.0).astype(F32)
+    inverses = [eye for _ in lowers]
     span = 1
     while span < size:
         joined = (row // (2 * span) == column // (2 * span)) & (row // span != column // span)
-        part = jnp.where(joined, lower, 0.0)
-        if span == 1:
-            inverse = inverse - part
-        else:
-            inverse = inverse - dot_three(inverse, dot_three(part, inverse))
+        parts = [jnp.where(joined, lower, 0.0) for lower in lowers]
+        if span > 1:
+            parts = [dot_three(part, inverse) for part, inverse in zip(parts, inverses)]
+            parts = [dot_three(inverse, part) for part, inverse in zip(parts, inverses)]
+        inverses = [inverse - part for part, inverse in zip(parts, inverses)]
         span = span * 2
-    return inverse
+    return inverses
 
 
 def unit(active):
@@ -101,69 +106,115 @@
     return jnp.sum(jnp.where(lane == index, block, 0.0), axis=1, keepdims=True)
 
 
+def convolved(rows, taps, flags, tap_count):
+    extended = rows[HALO - 8 :].astype(F32)
+    total = extended[8:] * taps[tap_count - 1 : tap_count]
+    for offset in range(1, tap_count):
+        moved = pltpu.roll(extended, offset, 0)[8:] * flags[:, 2 + offset : 3 + offset]
+        total = total + moved * taps[tap_count - 1 - offset : tap_count - offset]
+    return (total, extended)
+
+
+def convolved_back(d_total, extended, taps, flags, tap_count):
+    rows = extended.shape[0]
+    before = jnp.zeros((8, d_total.shape[1]), F32)
+    d_rows = jnp.concatenate([before, d_total * taps[tap_count - 1 : tap_count]], axis=0)
+    d_taps = [jnp.sum(d_total * extended[8:], axis=0, keepdims=True)]
+    for offset in range(1, tap_count):
+        kept = d_total * flags[:, 2 + offset : 3 + offset]
+        moved = pltpu.roll(extended, offset, 0)[8:]
+        d_taps = [jnp.sum(kept * moved, axis=0, keepdims=True)] + d_taps
+        scaled = jnp.concatenate(
+            [before, kept * taps[tap_count - 1 - offset : tap_count - offset]], axis=0
+        )
+        d_rows = d_rows + pltpu.roll(scaled, rows - offset, 0)
+    d_taps = d_taps + [jnp.zeros((8 - tap_count, d_total.shape[1]), F32)]
+    return (d_rows[8:], d_rows[:8], jnp.concatenate(d_taps, axis=0))
+
+
+def silu_of(total):
+    gate = 1.0 / (1.0 + jnp.exp(-total))
+    return (total * gate, gate)
+
+
 def span_kernel(
-    starts_col, starts_row, flags, betas, queries, keys, values,
+    many, tap_count, starts_col, starts_row, flags, betas, rows_q, rows_k, rows_v,
+    taps_q, taps_k, taps_v,
     inverse_out, wy_out, scores_out, reach_out, local_out, pair_out,
 ):
-    head = pl.program_id(0)
-    count = queries.shape[0]
-    width = queries.shape[1]
+    count = flags.shape[0]
+    width = rows_q.shape[1] // many
+    queries, keys, values = [
+        silu_of(convolved(rows[...], taps[...], flags, tap_count)[0])[0]
+        for rows, taps in ((rows_q, taps_q), (rows_k, taps_k), (rows_v, taps_v))
+    ]
     row = lax.broadcasted_iota(jnp.int32, (count, count), 0)
     column = lax.broadcasted_iota(jnp.int32, (count, count), 1)
     same_doc = starts_col[...] == starts_row[...]
     first = flags[:, 0:1]
     last_part = flags[:, 1:2]
-    beta = pick_lane(betas[...], head)
-    query, _ = unit(queries[...])
-    key, _ = unit(keys[...])
-    value = values[...]
-    products = dot_three(jnp.concatenate([key, query], axis=0), key, ROWS_ROWS)
-    lower = jnp.where(same_doc & (row > column), beta * products[:count], 0.0)
-    scores = jnp.where(same_doc & (row >= column), products[count:], 0.0)
-    inverse = inverse_unit_lower(lower, count)
-    wy = dot_three(inverse, jnp.concatenate([key * (beta * first), value * beta], axis=1))
-    applied = dot_three(scores, wy)
-    inverse_out[0] = inverse
-    wy_out[0] = wy
-    scores_out[0] = scores
-    reach_out[...] = first * query - applied[:, :width]
-    local_out[...] = applied[:, width:]
-    pair = dot_three(key * last_part, wy, FIRST_FIRST)
     eye = jnp.where(
         lax.broadcasted_iota(jnp.int32, (width, width), 0)
         == lax.broadcasted_iota(jnp.int32, (width, width), 1),
         1.0,
         0.0,
     )
-    change = (flags[count - 1 : count, 0:1] - 1.0) * eye - pair[:, :width]
-    pair_out[0] = jnp.concatenate([change, pair[:, width:]], axis=1).astype(LOW)
+    spots = [slice(at * width, (at + 1) * width) for at in range(many)]
+    beta = [pick_lane(betas[...], pl.program_id(0) * many + at) for at in range(many)]
+    query = [unit(queries[:, spot])[0] for spot in spots]
+    key = [unit(keys[:, spot])[0] for spot in spots]
+    products = [
+        dot_three(jnp.concatenate([k, q], axis=0), k, ROWS_ROWS) for q, k in zip(query, key)
+    ]
+    lower = [
+        jnp.where(same_doc & (row > column), b * p[:count], 0.0) for b, p in zip(beta, products)
+    ]
+    scores = [jnp.where(same_doc & (row >= column), p[count:], 0.0) for p in products]
+    inverse = inverse_unit_lower(lower, count)
+    for at, spot in enumerate(spots):
+        scaled = jnp.concatenate(
+            [key[at] * (beta[at] * first), values[:, spot] * beta[at]], axis=1
+        )
+        wy = dot_three(inverse[at], scaled)
+        applied = dot_three(scores[at], wy)
+        inverse_out[at] = inverse[at]
+        wy_out[at] = wy
+        scores_out[at] = scores[at]
+        reach_out[:, spot] = first * query[at] - applied[:, :width]
+        local_out[:, spot] = applied[:, width:]
+        pair = dot_three(key[at] * last_part, wy, FIRST_FIRST)
+        change = (flags[count - 1 : count, 0:1] - 1.0) * eye - pair[:, :width]
+        pair_out[at] = jnp.concatenate([change, pair[:, width:]], axis=1).astype(LOW)
 
 
 def rows_specs(count, width, head_count):
+    steps = head_count
     return [
-        pl.BlockSpec((count, width), lambda head, part=part: (0, part * head_count + head))
+        pl.BlockSpec((count, width), lambda step, part=part: (0, part * steps + step))
         for part in range(3)
     ]
 
 
-def span_call(starts, flags, betas, active, head_count, after=()):
-    count, width = active.shape[0], active.shape[1] // (3 * head_count)
-    rows = pl.BlockSpec((count, width), lambda head: (0, head))
-    whole = lambda shape: pl.BlockSpec(shape, lambda head: (0, 0))
-    square = pl.BlockSpec((1, count, count), lambda head: (head, 0, 0))
+def span_call(starts, flags, betas, extended, taps, tap_count, head_count, after=()):
+    many = SPAN_HEADS
+    count, width = flags.shape[0], extended.shape[1] // (3 * head_count)
+    rows = pl.BlockSpec((count, many * width), lambda step: (0, step))
+    whole = lambda shape: pl.BlockSpec(shape, lambda step: (0, 0))
+    square = pl.BlockSpec((many, count, count), lambda step: (step, 0, 0))
     return launch(
-        span_kernel,
+        functools.partial(span_kernel, many, tap_count),
         after,
-        grid=(head_count,),
+        grid=(head_count // many,),
         in_specs=[
             whole((count, 1)), whole((1, count)), whole(flags.shape), whole(betas.shape),
         ]
-        + rows_specs(count, width, head_count),
+        + rows_specs(extended.shape[0], many * width, head_count // many)
+        + rows_specs(8, many * width, head_count // many),
         out_specs=[
             square,
-            pl.BlockSpec((1, count, 2 * width), lambda head: (head, 0, 0)),
+            pl.BlockSpec((many, count, 2 * width), lambda step: (step, 0, 0)),
             square, rows, rows,
-            pl.BlockSpec((1, width, 2 * width), lambda head: (head, 0, 0)),
+            pl.BlockSpec((many, width, 2 * width), lambda step: (step, 0, 0)),
         ],
         out_shape=[
             jax.ShapeDtypeStruct((head_count, count, count), F32),
@@ -173,8 +224,11 @@
             jax.ShapeDtypeStruct((count, head_count * width), F32),
             jax.ShapeDtypeStruct((head_count, width, 2 * width), LOW),
         ],
-        cost_estimate=estimate(100 * head_count * count**3, 24 * active.shape[0] * active.shape[1]),
-        operands=(starts[:, None], starts[None, :], flags, betas, active, active, active,),
+        cost_estimate=estimate(1, 1),
+        operands=(
+            starts[:, None], starts[None, :], flags, betas, extended, extended, extended,
+            taps, taps, taps,
+        ),
     )
 
 
@@ -256,81 +310,119 @@
 
 
 def back_kernel(
-    starts_col, starts_row, flags, betas, queries, keys, values,
-    inverse_in, wy_in, scores_in, state_in, end_in, grads,
-    d_query_out, d_key_out, d_value_out, d_beta_out,
+    many, tap_count, starts_col, starts_row, flags, betas, rows_q, rows_k, rows_v,
+    taps_q, taps_k, taps_v, inverse_in, wy_in, scores_in, state_in, end_in, grads,
+    d_rows_out, d_tail_out, d_before_out, d_taps_out, d_beta_out,
 ):
-    head = pl.program_id(0)
-    count = queries.shape[0]
-    width = queries.shape[1]
+    count = flags.shape[0]
+    width = rows_q.shape[1] // many
+    all_rows, all_taps = (rows_q, rows_k, rows_v), (taps_q, taps_k, taps_v)
     row = lax.broadcasted_iota(jnp.int32, (count, count), 0)
     column = lax.broadcasted_iota(jnp.int32, (count, count), 1)
     same_doc = starts_col[...] == starts_row[...]
     first = flags[:, 0:1]
     last_part = flags[:, 1:2]
-    beta = pick_lane(betas[...], head)
-    query, query_scale = unit(queries[...])
-    key, key_scale = unit(keys[...])
-    value, grad = values[...], grads[...]
-    inverse, wy, scores = inverse_in[0], wy_in[0], scores_in[0]
-    state, end = state_in[0].astype(F32), end_in[0].astype(F32)
-    fresh = wy[:, width:] - dot_three(wy[:, :width], state)
-    d_fresh = dot_three(scores, grad, FIRST_FIRST) + dot_three(key * last_part, end)
-    pulled = dot_three(inverse, d_fresh, FIRST_FIRST)
-    both = jnp.concatenate([grad, pulled], axis=0)
-    through_state = dot_three(both, state, ROWS_ROWS)
-    through_fresh = dot_three(both, fresh, ROWS_ROWS)
-    d_scores = jnp.where(same_doc & (row >= column), through_fresh[:count], 0.0)
-    d_lower = jnp.where(same_doc & (row > column), -through_fresh[count:], 0.0)
-    by_keys = dot_three(jnp.concatenate([d_scores, d_lower], axis=0), key)
-    d_query = first * through_state[:count] + by_keys[:count]
-    d_query_out[...] = unit_back(d_query, query, query_scale)
-    recalled = -through_state[count:]
-    row_part = by_keys[count:]
-    d_key = (
-        dot_three(d_scores, query, FIRST_FIRST)
-        + dot_three(d_lower, beta * key, FIRST_FIRST)
-        + last_part * dot_three(fresh, end, ROWS_ROWS)
-        + (beta * first) * recalled
-        + beta * row_part
-    )
-    d_key_out[...] = unit_back(d_key, key, key_scale)
-    d_value_out[...] = beta * pulled
-    d_beta = jnp.sum(
-        (row_part + first * recalled) * key + pulled * value, axis=1, keepdims=True
-    )
-
-    @pl.when(head == 0)
+    lane = lax.broadcasted_iota(jnp.int32, d_beta_out.shape, 1)
+    d_betas = jnp.zeros(d_beta_out.shape, F32)
+    for at in range(many):
+        spot = slice(at * width, (at + 1) * width)
+        head = pl.program_id(0) * many + at
+        beta = pick_lane(betas[...], head)
+        summed = [
+            convolved(rows[:, spot], taps[:, spot], flags, tap_count)
+            for rows, taps in zip(all_rows, all_taps)
+        ]
+        active = [silu_of(total) for total, _ in summed]
+        query, query_scale = unit(active[0][0])
+        key, key_scale = unit(active[1][0])
+        value, grad = active[2][0], grads[:, spot]
+        inverse, wy, scores = inverse_in[at], wy_in[at], scores_in[at]
+        state, end = state_in[at].astype(F32), end_in[at].astype(F32)
+        fresh = wy[:, width:] - dot_three(wy[:, :width], state)
+        d_fresh = dot_three(scores, grad, FIRST_FIRST) + dot_three(key * last_part, end)
+        pulled = dot_three(inverse, d_fresh, FIRST_FIRST)
+        both = jnp.concatenate([grad, pulled], axis=0)
+        through_state = dot_three(both, state, ROWS_ROWS)
+        through_fresh = dot_three(both, fresh, ROWS_ROWS)
+        d_scores = jnp.where(same_doc & (row >= column), through_fresh[:count], 0.0)
+        d_lower = jnp.where(same_doc & (row > column), -through_fresh[count:], 0.0)
+        by_keys = dot_three(jnp.concatenate([d_scores, d_lower], axis=0), key)
+        d_query = first * through_state[:count] + by_keys[:count]
+        recalled = -through_state[count:]
+        row_part = by_keys[count:]
+        d_key = (
+            dot_three(d_scores, query, FIRST_FIRST)
+            + dot_three(d_lower, beta * key, FIRST_FIRST)
+            + last_part * dot_three(fresh, end, ROWS_ROWS)
+            + (beta * first) * recalled
+            + beta * row_part
+        )
+        d_active = (
+            unit_back(d_query, query, query_scale),
+            unit_back(d_key, key, key_scale),
+            beta * pulled,
+        )
+        for kind in range(3):
+            total, gate = summed[kind][0], active[kind][1]
+            d_total = d_active[kind] * gate * (1.0 + total * (1.0 - gate))
+            d_rows, d_before, d_taps = convolved_back(
+                d_total, summed[kind][1], all_taps[kind][:, spot], flags, tap_count
+            )
+            d_rows_out[kind, :, spot] = d_rows.astype(LOW)
+            d_tail_out[kind, :, spot] = d_rows[count - 8 :]
+            d_before_out[kind, :, spot] = d_before
+            d_taps_out[kind, :, spot] = d_taps
+        d_beta = jnp.sum(
+            (row_part + first * recalled) * key + pulled * value, axis=1, keepdims=True
+        )
+        d_betas = d_betas + jnp.where(lane == head, d_beta, 0.0)
+
+    @pl.when(pl.program_id(0) == 0)
     def _():
-        d_beta_out[...] = jnp.zeros_like(d_beta_out)
-
-    lane = lax.broadcasted_iota(jnp.int32, d_beta_out.shape, 1)
-    d_beta_out[...] += jnp.where(lane == head, d_beta, 0.0)
-
-
-def back_call(starts, flags, betas, active, inverse, wy, scores, states, ends, grads, after=()):
+        d_beta_out[...] = d_betas
+
+    @pl.when(pl.program_id(0) > 0)
+    def _():
+        d_beta_out[...] += d_betas
+
+
+def back_call(
+    starts, flags, betas, extended, taps, tap_count, inverse, wy, scores, states, ends, grads,
+    after=(),
+):
+    many = BACK_HEADS
     head_count, width = states.shape[0], states.shape[1]
-    count = active.shape[0]
-    rows = pl.BlockSpec((count, width), lambda head: (0, head))
-    whole = lambda shape: pl.BlockSpec(shape, lambda head: (0, 0))
-    per_head = lambda shape: pl.BlockSpec((1,) + shape, lambda head: (head, 0, 0))
+    count = flags.shape[0]
+    steps = head_count // many
+    kinds = lambda height: pl.BlockSpec((3, height, many * width), lambda step: (0, 0, step))
+    rows = pl.BlockSpec((count, many * width), lambda step: (0, step))
+    whole = lambda shape: pl.BlockSpec(shape, lambda step: (0, 0))
+    per_head = lambda shape: pl.BlockSpec((many,) + shape, lambda step: (step, 0, 0))
     return launch(
-        back_kernel,
+        functools.partial(back_kernel, many, tap_count),
         after,
-        grid=(head_count,),
+        grid=(head_count // many,),
         in_specs=[
             whole((count, 1)), whole((1, count)), whole(flags.shape), whole(betas.shape),
-            *rows_specs(count, width, head_count),
+            *rows_specs(extended.shape[0], many * width, steps),
+            *rows_specs(8, many * width, steps),
             per_head((count, count)), per_head((count, 2 * width)), per_head((count, count)),
             per_head((width, width)), per_head((width, width)),
             rows,
         ],
-        out_specs=[rows, rows, rows, whole(betas.shape)],
-        out_shape=[jax.ShapeDtypeStruct(grads.shape, F32)] * 3
-        + [jax.ShapeDtypeStruct(betas.shape, F32)],
+        out_specs=[kinds(count), kinds(8), kinds(8), kinds(8), whole(betas.shape)],
+        out_shape=[
+            jax.ShapeDtypeStruct((3,) + grads.shape, LOW),
+            jax.ShapeDtypeStruct((3, 8, grads.shape[1]), F32),
+            jax.ShapeDtypeStruct((3, 8, grads.shape[1]), F32),
+            jax.ShapeDtypeStruct((3, 8, grads.shape[1]), F32),
+            jax.ShapeDtypeStruct(betas.shape, F32),
+        ],
         cost_estimate=estimate(36 * head_count * count**3, 40 * grads.shape[0] * grads.shape[1]),
-        operands=(starts[:, None], starts[None, :], flags, betas, active, active, active, inverse, wy, scores,
-        states, ends, grads,),
+        operands=(
+            starts[:, None], starts[None, :], flags, betas, extended, extended, extended,
+            taps, taps, taps, inverse, wy, scores, states, ends, grads,
+        ),
     )
 
 
@@ -516,20 +608,6 @@
     )
 
 
-def absolute(values, masks):
-    count = lax.axis_size("seq")
-    width = values.shape[1] // count
-    mine = lax.axis_index("seq")
-    where_mask = jnp.array([masks.index(mask) for mask in range(count)], jnp.int32)
-    return jnp.concatenate(
-        [
-            lax.dynamic_slice_in_dim(values, where_mask[mine ^ place] * width, width, 1)
-            for place in range(count)
-        ],
-        axis=1,
-    )
-
-
 def spread_views(block, order, joined):
     views = [(block, 0)]
     for bit in order:
@@ -548,10 +626,26 @@
     return views
 
 
-def halved_sum(kept, bit):
-    half = kept.shape[0] // 2
+def add_kernel(kept, arrived, total):
+    total[...] = (kept[...].astype(F32) + arrived[...].astype(F32)).astype(LOW)
+
+
+def halved_sum(kept, bit, after=()):
+    rows, width = kept.shape
+    half = rows // 2
     arrived = swapped(kept[half:], bit)
-    return (kept[:half].astype(F32) + arrived.astype(F32)).astype(LOW)
+    tile = tile_of(width, 512)
+    spot = pl.BlockSpec((half, tile), lambda step: (0, step))
+    return launch(
+        add_kernel,
+        after,
+        grid=(width // tile,),
+        in_specs=[spot, spot],
+        out_specs=spot,
+        out_shape=jax.ShapeDtypeStruct((half, width), LOW),
+        cost_estimate=estimate(1, 1),
+        operands=(kept, arrived),
+    )
 
 
 def over_groups(rows):
@@ -563,6 +657,24 @@
     while width % tile:
         tile = tile // 2
     return tile
+
+
+def copy_kernel(source, target):
+    target[...] = source[...]
+
+
+def columns(block, start, width):
+    rows = block.shape[0]
+    return launch(
+        copy_kernel,
+        (),
+        grid=(1,),
+        in_specs=[pl.BlockSpec((rows, width), lambda step: (0, start // width))],
+        out_specs=pl.BlockSpec((rows, width), lambda step: (0, 0)),
+        out_shape=jax.ShapeDtypeStruct((rows, width), block.dtype),
+        cost_estimate=estimate(1, 1),
+        operands=(block,),
+    )
 
 
 def join_kernel(first, second, target):
@@ -618,17 +730,56 @@
     )
 
 
-def feed_kernel(count, cuts, resumed, feed, slopes, *refs):
+def chip_spots(orders, depth):
+    chip = lax.axis_index("seq") // 2
+    spots = []
+    for mask in orders:
+        place = chip
+        bit = 1
+        while bit <= mask:
+            if mask & bit:
+                place = place + bit - 2 * bit * lax.rem(chip // bit, 2)
+            bit = bit * 2
+        spots.append(pl.ds(pl.multiple_of(place * depth, depth), depth))
+    return spots
+
+
+def cores_turned(block):
+    half = block.shape[1] // 2
+    turned = jnp.concatenate([block[:, half:], block[:, :half]], axis=1)
+    return jnp.where(lax.rem(lax.axis_index("seq"), 2) == 0, block, turned)
+
+
+def feed_kernel(count, cuts, masks, stage, *refs):
+    if stage == 0:
+        given, refs = refs[:4], refs[4:]
+    else:
+        (feed, slopes), refs = refs[:2], refs[2:]
     weights, refs = refs[: 6 * count], refs[6 * count :]
-    if resumed:
-        before, refs = refs[:2], refs[2:]
-    grads_first, grads_second, out_total, d_total = refs
+    if stage == 0:
+        grads_first, grads_second, feed, slopes, out_total, d_total = refs
+    else:
+        out_before, d_before, grads_first, grads_second, out_own, out_other, d_own, d_other = refs[:8]
+        out_total, d_total = refs[8:]
     step = pl.program_id(0)
+    tokens, model = feed.shape
+    depth = model // count
+    spans = [slice(place * depth, (place + 1) * depth) for place in range(count)]
 
     @pl.when(step == 0)
     def _():
-        out_total[...] = before[0][...] if resumed else jnp.zeros_like(out_total)
-        d_total[...] = before[1][...] if resumed else jnp.zeros_like(d_total)
+        if stage == 0:
+            spots = chip_spots(masks, depth)
+            half = tokens // 2
+            for target, (own, other) in ((feed, given[:2]), (slopes, given[2:])):
+                for span, spot in zip(spans, spots):
+                    target[:half, span] = cores_turned(own[:, spot].astype(F32)).astype(LOW)
+                    target[half:, span] = cores_turned(other[:, spot].astype(F32)).astype(LOW)
+            out_total[...] = jnp.zeros_like(out_total)
+            d_total[...] = jnp.zeros_like(d_total)
+        else:
+            out_total[...] = out_before[...]
+            d_total[...] = d_before[...]
 
     back = functools.partial(
         lax.dot_general, dimension_numbers=(((1,), (1,)), ((), ())), preferred_element_type=F32
@@ -663,15 +814,27 @@
     def _():
         tile_step(weights[3 * count :], grads_second)
 
-
-def feed_call(feed, slopes, piece_lists, before, tile, after=()):
-    tokens, depth = feed.shape
+    if stage:
+
+        @pl.when(step == cuts[0] + cuts[1] - 1)
+        def _():
+            spots = chip_spots(masks, depth)
+            half = tokens // 2
+            for source, own, other in ((out_total, out_own, out_other), (d_total, d_own, d_other)):
+                for span, spot in zip(spans, spots):
+                    own[:, spot] = cores_turned(source[:half, span])
+                    other[:, spot] = cores_turned(source[half:, span])
+
+
+def feed_call(rows, piece_lists, before, masks, tile, after=()):
+    tokens, depth = (2 * rows[0].shape[0] if before is None else rows[0].shape[0]), rows[0].shape[1]
     cuts = [pieces[0][0].shape[1] // (3 * tile) for pieces in piece_lists]
     block_rows = depth // len(piece_lists[0])
     count = len(piece_lists[0])
     first = lambda step: jnp.minimum(step, cuts[0] - 1)
     second = lambda step: jnp.maximum(step - cuts[0], 0)
     whole = pl.BlockSpec((tokens, depth), lambda step: (0, 0))
+    single = pl.BlockSpec((tokens // 2, depth), lambda step: (0, 0))
     weights = [
         pl.BlockSpec(
             (block_rows, tile),
@@ -681,29 +844,32 @@
         for kind in range(3)
         for _, at in pieces
     ]
-    width = (cuts[0] + cuts[1]) * tile
+    both = jax.ShapeDtypeStruct((tokens, depth), F32)
+    one = jax.ShapeDtypeStruct((tokens // 2, depth), F32)
+    kept = jax.ShapeDtypeStruct((tokens, depth), LOW)
     return launch(
-        functools.partial(feed_kernel, count, cuts, before is not None),
+        functools.partial(feed_kernel, count, cuts, masks, 0 if before is None else 1),
         after,
         grid=(cuts[0] + cuts[1],),
-        in_specs=[whole, whole] + weights + ([whole, whole] if before is not None else []),
+        in_specs=([single] * 4 if before is None else [whole] * 2)
+        + weights
+        + ([] if before is None else [whole] * 2),
         out_specs=[
             pl.BlockSpec((3, tokens, tile), lambda step: (0, 0, first(step))),
             pl.BlockSpec((3, tokens, tile), lambda step: (0, 0, second(step))),
-            whole,
-            whole,
-        ],
+        ]
+        + ([whole] * 4 if before is None else [single] * 4),
         out_shape=[
             jax.ShapeDtypeStruct((3, tokens, cuts[0] * tile), LOW),
             jax.ShapeDtypeStruct((3, tokens, cuts[1] * tile), LOW),
-            jax.ShapeDtypeStruct((tokens, depth), F32),
-            jax.ShapeDtypeStruct((tokens, depth), F32),
-        ],
-        cost_estimate=estimate(
-            12 * tokens * depth * width, 6 * depth * width, 3 * tokens * width
-        ),
+        ]
+        + ([kept, kept, both, both] if before is None else [one] * 4),
+        scratch_shapes=[]
+        if before is None
+        else [pltpu.VMEM((tokens, depth), F32), pltpu.VMEM((tokens, depth), F32)],
+        cost_estimate=estimate(1, 1),
         operands=(
-            feed, slopes,
+            *rows,
             *([array for array, _ in piece_lists[0]] * 3),
             *([array for array, _ in piece_lists[1]] * 3),
             *(before if before is not None else ()),
@@ -1011,7 +1177,7 @@
     )(shard, feed)
 
 
-def reduce_kernel(waited, group_size, orders, groups, *refs):
+def reduce_kernel(waited, group_size, all_orders, groups, *refs):
     refs = refs[waited:]
     sets = len(groups)
     inputs, refs = refs[: 4 * sets + 1], refs[4 * sets + 1 :]
@@ -1020,13 +1186,11 @@
     vector_out, vector_in = refs[:2]
     send_sem, recv_sem, core_send, core_recv, line_send, line_recv, v_send, v_recv = refs[2:]
     my_seq, my_group = lax.axis_index("seq"), lax.axis_index("grp")
-    levels = len(orders[0])
     peers = [lax.rem(my_group + step, group_size) for step in range(1, group_size)]
-    bits = [1] + list(orders[1])
+    most = max(len(orders[0]) for orders in all_orders)
+    bits = [1] + max(all_orders, key=lambda orders: len(orders[0]))[1]
     units = [(place, group) for place in range(sets) for group in range(groups[place])]
-    lower_rows = inputs[0].shape[0]
-    final = lower_rows // 2 ** (levels - 1)
-    half = final // 2
+    half = inputs[0].shape[0] // 2 ** len(all_orders[0][0])
     rows = half // group_size
 
     def partner(bit):
@@ -1050,34 +1214,39 @@
             device_id=device, device_id_type=pl.DeviceIdType.MESH,
         )
 
-    def held(level):
-        return lower_rows // 2**level
-
-    def begins(level):
-        return sum(held(before) for before in range(level))
+    def orders_of(unit):
+        return all_orders[units[unit][0]]
+
+    def held(unit, level):
+        return inputs[4 * units[unit][0]].shape[0] // 2**level
+
+    def begins(unit, level):
+        return sum(held(unit, before) for before in range(level))
 
     def parts_of(unit):
         place, group = units[unit]
-        return inputs[4 * place : 4 * place + 4], buffers[5 * place : 5 * place + 5], group
+        given, own = inputs[4 * place : 4 * place + 4], buffers[5 * place : 5 * place + 5]
+        return given, (own[:2], own[2], own[3], own[4]), group
 
     def chip_copy(unit, part, level):
-        given, (arrived, leaving, _, _, _), group = parts_of(unit)
-        width = arrived.shape[-1]
-        count = held(level)
+        given, (arrived, _, _, _), group = parts_of(unit)
+        width = arrived[part].shape[-1]
+        count = held(unit, level)
+        order = orders_of(unit)[part]
         if level == 0:
             source = given[part].at[:, pl.ds(group * width, width)]
         else:
-            source = leaving.at[part, group, pl.ds(begins(level) - held(0), count)]
+            source = arrived[part].at[group, pl.ds(begins(unit, level - 1) + count, count)]
         return remote(
             source,
-            arrived.at[part, group, pl.ds(begins(level), count)],
+            arrived[part].at[group, pl.ds(begins(unit, level), count)],
             send_sem.at[unit, part, level],
             recv_sem.at[unit, part, level],
-            (partner(orders[part][levels - 1 - level]), my_group),
+            (partner(order[len(order) - 1 - level]), my_group),
         )
 
     def core_copy(unit):
-        _, (_, _, chip_total, core_in, _), group = parts_of(unit)
+        _, (_, chip_total, core_in, _), group = parts_of(unit)
         return remote(
             chip_total.at[group, pl.ds(half, half)],
             core_in.at[group],
@@ -1086,26 +1255,66 @@
             (partner(1), my_group),
         )
 
-    def line_copies(unit):
-        _, (_, _, chip_total, core_in, line_in), group = parts_of(unit)
-        copies = []
-        for at, peer in enumerate(peers):
-            spot = pl.ds(pl.multiple_of(peer * rows, rows), rows)
-            for side, source in enumerate((chip_total.at[group, spot], core_in.at[group, spot])):
-                copies.append(
-                    remote(
-                        source,
-                        line_in.at[group, at, side],
-                        line_send.at[unit, at, side],
-                        line_recv.at[unit, at, side],
-                        (my_seq, peer),
-                    )
-                )
-        return copies
+    def block_at(group):
+        return pl.ds(group * rows, rows)
+
+    def line_copy(unit, side, sender, target):
+        _, (_, chip_total, core_in, line_in), group = parts_of(unit)
+        source = (chip_total, core_in)[side].at[group, block_at(target)]
+        receiver = sender + 1 if target > sender else sender - 1
+        spot = group_size if target == receiver < sender else target
+        return remote(
+            source,
+            line_in.at[group, spot, side],
+            line_send.at[unit, spot, side],
+            line_recv.at[unit, spot, side],
+            (my_seq, receiver),
+        )
+
+    def line_step(unit, place, hop, up):
+        _, (_, chip_total, core_in, line_in), group = parts_of(unit)
+        targets = range(place + 1, group_size) if up else range(place)
+        for target in targets:
+            for side, source in enumerate((chip_total, core_in)):
+                if hop:
+                    line_copy(unit, side, place - 1 if up else place + 1, target).wait_recv()
+                    value = source[group, target * rows : (target + 1) * rows].astype(F32)
+                    value = value + line_in[group, target, side].astype(F32)
+                    source[group, target * rows : (target + 1) * rows] = value.astype(LOW)
+                line_copy(unit, side, place, target).start()
+
+    def line_hop(unit, hop):
+        for up, place in ((True, hop), (False, group_size - 1 - hop)):
+
+            @pl.when(my_group == place)
+            def _():
+                line_step(unit, place, hop, up)
+
+    def line_end(unit, place):
+        _, (_, chip_total, core_in, line_in), group = parts_of(unit)
+        total = totals[units[unit][0]]
+        both = chip_total.shape[-1]
+        for side, source in enumerate((chip_total, core_in)):
+            value = source[group, place * rows : (place + 1) * rows].astype(F32)
+            if place > 0:
+                line_copy(unit, side, place - 1, place).wait_recv()
+                value = value + line_in[group, place, side].astype(F32)
+            if place + 1 < group_size:
+                line_copy(unit, side, place + 1, place).wait_recv()
+                value = value + line_in[group, group_size, side].astype(F32)
+            spot = (group * 2 + side) * both
+            total[:, spot : spot + both] = value
+
+    def line_drain(unit, place):
+        for target in range(group_size):
+            if target != place:
+                for side in range(2):
+                    line_copy(unit, side, place, target).wait_send()
 
     def stage(unit, lag):
-        given, (arrived, leaving, chip_total, core_in, line_in), group = parts_of(unit)
-        width = arrived.shape[-1]
+        given, (arrived, chip_total, core_in, line_in), group = parts_of(unit)
+        levels = len(orders_of(unit)[0])
+        widths = [buffer.shape[-1] for buffer in arrived]
         if lag == 0:
             for part in range(2):
                 chip_copy(unit, part, 0).start()
@@ -1113,46 +1322,37 @@
             level = lag - 1
             for part in range(2):
                 chip_copy(unit, part, level).wait_recv()
-                count = held(level)
+                count, width = held(unit, level), widths[part]
 
                 def added(low, high):
-                    base = begins(level)
-                    value = arrived[part, group, base + low : base + high].astype(F32)
+                    base = begins(unit, level)
+                    value = arrived[part][group, base + low : base + high].astype(F32)
                     if level == 0:
                         kept = given[2 + part][low:high, group * width : (group + 1) * width]
                     else:
-                        before = begins(level - 1)
-                        kept = arrived[part, group, before + low : before + high]
+                        before = begins(unit, level - 1)
+                        kept = arrived[part][group, before + low : before + high]
                     return value + kept.astype(F32)
 
                 if lag < levels:
                     middle = count // 2
-                    spot = begins(level + 1) - held(0)
-                    leaving[part, group, spot : spot + middle] = added(middle, count).astype(LOW)
+                    base = begins(unit, level)
+                    arrived[part][group, base + middle : base + count] = added(
+                        middle, count
+                    ).astype(LOW)
                     chip_copy(unit, part, level + 1).start()
-                    base = begins(level)
-                    arrived[part, group, base : base + middle] = added(0, middle).astype(LOW)
+                    arrived[part][group, base : base + middle] = added(0, middle).astype(LOW)
                 else:
-                    chip_total[group, :, part * width : (part + 1) * width] = added(
-                        0, count
-                    ).astype(LOW)
+                    at = part * widths[0]
+                    chip_total[group, :, at : at + width] = added(0, count).astype(LOW)
             if lag == levels:
                 core_copy(unit).start()
         elif lag == levels + 1:
             core_copy(unit).wait_recv()
-            for copy in line_copies(unit):
-                copy.start()
+            if group_size > 1:
+                line_hop(unit, 0)
         else:
-            own = pl.ds(pl.multiple_of(my_group * rows, rows), rows)
-            for copy in line_copies(unit):
-                copy.wait_recv()
-            total = totals[units[unit][0]]
-            for side, source in enumerate((chip_total, core_in)):
-                value = source[group, own].astype(F32)
-                for at in range(len(peers)):
-                    value = value + line_in[group, at, side].astype(F32)
-                spot = (group * 2 + side) * 2 * width
-                total[:, spot : spot + 2 * width] = value
+            line_hop(unit, lag - levels - 1)
 
     def vector_copies(step):
         if step < len(bits):
@@ -1187,70 +1387,81 @@
             for copy in vector_copies(step):
                 copy.start()
 
-    last_step = len(units) + levels + 2
+    last_step = len(units) + most + group_size - 1
+    ahead = AHEAD
+    for unit in range(min(ahead, len(units))):
+        stage(unit, 0)
     for step in range(last_step):
-        for lag in range(levels + 3):
-            if 0 <= step - lag < len(units):
-                stage(step - lag, lag)
+        if step + ahead < len(units):
+            stage(step + ahead, 0)
+        for lag in range(1, most + group_size):
+            unit = step - lag
+            if 0 <= unit < len(units) and lag < len(orders_of(unit)[0]) + max(group_size, 2):
+                stage(unit, lag)
         if step <= len(bits) + 1:
             vector_step(step)
     for step in range(last_step, len(bits) + 2):
         vector_step(step)
+    for place in range(group_size):
+
+        @pl.when(my_group == place)
+        def _():
+            for unit in range(len(units)):
+                line_end(unit, place)
     for step in range(len(bits) + 1):
         for copy in vector_copies(step):
             copy.wait_send()
     for unit in range(len(units)):
         for part in range(2):
-            for level in range(levels):
+            for level in range(len(orders_of(unit)[0])):
                 chip_copy(unit, part, level).wait_send()
         core_copy(unit).wait_send()
-        for copy in line_copies(unit):
-            copy.wait_send()
-
-
-def reduce_call(sets, vector, orders, collective_id, after=()):
+    for place in range(group_size):
+
+        @pl.when(my_group == place)
+        def _():
+            for unit in range(len(units)):
+                line_drain(unit, place)
+
+
+def reduce_call(sets, vector, collective_id, after=()):
     group_size = lax.axis_size("grp")
-    depth = sets[0][0][0].shape[0]
-    levels = len(orders[0])
-    final = depth // 2 ** (levels - 1)
-    half = final // 2
+    groups = [group for _, _, group, _ in sets]
+    all_orders = [orders for _, _, _, orders in sets]
+    half = sets[0][0][0].shape[0] // 2 ** len(all_orders[0][0])
     rows = half // group_size
-    held_all = sum(depth // 2**level for level in range(levels))
-    groups = [group for _, _, group in sets]
     units = sum(groups)
-    bits = levels + 1
+    most = max(len(orders[0]) for orders in all_orders)
+    bits = most + 1
     in_vmem = pl.BlockSpec(memory_space=pltpu.VMEM)
     in_any = pl.BlockSpec(memory_space=pl.ANY)
     dma = pltpu.SemaphoreType.DMA
-    widths = [lowers[0].shape[1] // group for lowers, _, group in sets]
-    scratch = []
-    for group, width in zip(groups, widths):
+    scratch, operands, results = [], [], []
+    for lowers, uppers, group, orders in sets:
+        depth = lowers[0].shape[0]
+        held_all = sum(depth // 2**level for level in range(len(orders[0])))
+        widths = [lower.shape[1] // group for lower in lowers]
+        both = sum(widths)
+        operands += [*lowers, *uppers]
+        scratch += [pltpu.VMEM((group, held_all, width), LOW) for width in widths]
         scratch += [
-            pltpu.VMEM((2, group, held_all, width), LOW),
-            pltpu.VMEM((2, group, max(held_all - depth, 16), width), LOW),
-            pltpu.VMEM((group, final, 2 * width), LOW),
-            pltpu.VMEM((group, half, 2 * width), LOW),
-            pltpu.VMEM((group, max(group_size - 1, 1), 2, rows, 2 * width), LOW),
+            pltpu.VMEM((group, 2 * half, both), LOW),
+            pltpu.VMEM((group, half, both), LOW),
+            pltpu.VMEM((group, group_size + 1, 2, rows, both), LOW),
         ]
-    operands = []
-    for lowers, uppers, _ in sets:
-        operands += [*lowers, *uppers]
+        results.append(jax.ShapeDtypeStruct((rows, group * 2 * both), F32))
     return pl.pallas_call(
-        functools.partial(reduce_kernel, len(after), group_size, orders, groups),
+        functools.partial(reduce_kernel, len(after), group_size, all_orders, groups),
         in_specs=[in_any] * len(after) + [in_any, in_any, in_vmem, in_vmem] * len(sets) + [in_vmem],
         out_specs=[in_vmem] * (len(sets) + 1),
-        out_shape=[
-            jax.ShapeDtypeStruct((rows, group * 4 * width), F32)
-            for group, width in zip(groups, widths)
-        ]
-        + [jax.ShapeDtypeStruct(vector.shape, F32)],
+        out_shape=results + [jax.ShapeDtypeStruct(vector.shape, F32)],
         scratch_shapes=scratch
         + [
             pltpu.VMEM((bits + 1,) + vector.shape, F32),
             pltpu.VMEM((bits + group_size,) + vector.shape, F32),
-            dma((units, 2, levels)), dma((units, 2, levels)),
+            dma((units, 2, most)), dma((units, 2, most)),
             dma((units,)), dma((units,)),
-            dma((units, group_size, 2)), dma((units, group_size, 2)),
+            dma((units, group_size + 1, 2)), dma((units, group_size + 1, 2)),
             dma((bits + group_size,)), dma((bits + group_size,)),
         ],
         cost_estimate=estimate(1, 1),
@@ -1310,9 +1521,9 @@
     unit_width = hidden_units // 2
     tile = tile_of(unit_width, 256)
     tiles = unit_width // tile
-    half_tiles = -(-tiles // 2)
-    rest = tiles - half_tiles
-    counts = [-(-half_tiles // 2), half_tiles // 2, -(-rest // 2), rest // 2]
+    early_tiles = -(-tiles // 2)
+    rest = tiles - early_tiles
+    counts = [-(-early_tiles // 2), early_tiles // 2, -(-rest // 2), rest // 2]
     edges = [sum(counts[:place]) * tile for place in range(5)]
     spans = list(zip(edges[:-1], edges[1:]))
     feed_shards = (gate_weight, up_weight, down_weight)
@@ -1338,16 +1549,23 @@
         pl.ds(widths[0], widths[1]),
         pl.ds(widths[0] + widths[1], widths[0] + widths[1]),
     )
+    tokens_before = jnp.concatenate(
+        [
+            jnp.zeros((HALO - (tap_count - 1), model_width), tokens.dtype),
+            passed_along(tokens[row_count - (tap_count - 1) :], ("seq", "grp"), 1),
+        ],
+        axis=0,
+    )
     full, pair_first, pair_second, _ = gather_call(
         plain_shard, feed_shard, plain_cuts, feed_cuts, plain_orders, 2
     )
     w_qkv, w_out = full[:, : 3 * model_width], full[:, 3 * model_width : 4 * model_width]
-    small = full[:, 4 * model_width : 4 * model_width + small_width]
+    small = columns(full, 4 * model_width, 128)
     gain_mixer, gain_feed = small[:, 0], small[:, 1]
     c_query = small[:, 2 : 2 + tap_count]
     c_key = small[:, 2 + tap_count : 2 + 2 * tap_count]
     c_value = small[:, 2 + 2 * tap_count : 2 + 3 * tap_count]
-    w_beta = small[:, 2 + 3 * tap_count :]
+    w_beta = small[:, 2 + 3 * tap_count : small_width]
 
     feed_blocks = [
         along_groups(
@@ -1373,44 +1591,40 @@
     places = anchor + jnp.arange(row_count, dtype=jnp.int32)
     starts = jnp.cumsum(lengths) - lengths
     row_start = jnp.max(jnp.where(starts[None, :] <= places[:, None], starts[None, :], 0), axis=1)
-    valid = jnp.stack(
-        [(places - offset >= row_start).astype(jnp.float32) for offset in range(1, tap_count)]
-    )
+    valid = [
+        (places - offset >= row_start).astype(jnp.float32) for offset in range(1, tap_count)
+    ]
     live_rows = pad_mask.astype(jnp.float32)
     inputs32 = tokens.astype(jnp.float32)
     normed_a, norm_a_back = jax.vjp(rms_scale, inputs32, gain_mixer.astype(jnp.float32))
     normed_low = normed_a.astype(jnp.bfloat16)
-    own_pre = jnp.dot(normed_low, w_qkv, preferred_element_type=F32).astype(LOW)
+    normed_before = rms_scale(tokens_before.astype(F32), gain_mixer.astype(F32)).astype(LOW)
+    extended = jnp.dot(
+        jnp.concatenate([normed_before, normed_low], axis=0), w_qkv, preferred_element_type=F32
+    ).astype(LOW)
     logit_part = jnp.dot(normed_low, w_beta, preferred_element_type=jnp.float32)
     sigmoid_val = jax.nn.sigmoid(logit_part + beta_bias)
     beta_rows = sigmoid_val * live_rows[:, None]
-    earlier_rows = passed_along(own_pre[row_count - (tap_count - 1) :], ("seq", "grp"), 1)
-    extended = jnp.concatenate([earlier_rows, own_pre], axis=0).astype(jnp.float32)
-    kernel = jnp.concatenate([c_query, c_key, c_value], axis=0).astype(jnp.float32)
-
-    def conv_act(padded, kernel_all):
-        summed = padded[tap_count - 1 :] * kernel_all[:, tap_count - 1]
-        for offset in range(1, tap_count):
-            moved = padded[tap_count - 1 - offset : tap_count - 1 - offset + row_count]
-            summed = (
-                summed + moved * valid[offset - 1][:, None] * kernel_all[:, tap_count - 1 - offset]
-            )
-        return jax.nn.silu(summed)
-
-    active, conv_pull = jax.vjp(conv_act, extended, kernel)
+    taps = jnp.pad(
+        jnp.transpose(jnp.concatenate([c_query, c_key, c_value], axis=0).astype(jnp.float32)),
+        ((0, 8 - tap_count), (0, 0)),
+    )
     flags = jnp.stack(
         [
             (row_start < anchor).astype(jnp.float32),
             (row_start == row_start[-1]).astype(jnp.float32),
             live_rows,
-        ],
+        ]
+        + valid,
         axis=1,
     )
     inverse, wy, scores, reach, local_out, pairs = span_call(
         row_start,
         flags,
         beta_rows,
-        active,
+        extended,
+        taps,
+        tap_count,
         head_count,
         after=(feed_pieces[0][1][0], feed_pieces[1][1][0]),
     )
@@ -1432,10 +1646,6 @@
     hidden_one = inputs32 + jnp.dot(head_low, w_out, preferred_element_type=F32)
     normed_f, norm_f_back = jax.vjp(rms_scale, hidden_one, gain_feed.astype(jnp.float32))
     feed_low = normed_f.astype(jnp.bfloat16)
-    both_feed = jnp.concatenate([feed_low, swapped(feed_low, 1)], axis=0)
-    both_slopes = jnp.concatenate([cotangent, swapped(cotangent, 1)], axis=0)
-    feed_rel = relative(both_feed, pair_masks[0])
-    slopes_rel = relative(both_slopes, pair_masks[0])
     depth = model_width // len(feed_pieces[0])
     second_places = [pair_masks[1][::2].index(mask) for mask in pair_masks[0][::2]]
     first_places = [pair_masks[0][::2].index(mask) for mask in pair_masks[1][::2]]
@@ -1444,59 +1654,65 @@
         [list(range(chip_count // 2)), list(range(chip_count // 2, chip_count))],
         [first_places[: chip_count // 2], first_places[chip_count // 2 :]],
     ]
-    sources = (feed_rel, slopes_rel)
-    totals = None
-    feed_grads, lower_halves, sent = [], [], []
+    rows = (feed_low, swapped(feed_low, 1), cotangent, swapped(cotangent, 1))
+    chip_masks = [mask // 2 for mask in pair_masks[0][::2]]
+    before = None
+    feed_grads, lower_halves = [], []
+
+    def feed_lower(chunk, after):
+        return [
+            outer_call(sources, feed_grads[2 * chunk + part], half_places[part][1], after=after)
+            for part in range(2)
+        ]
+
+    def feed_sent(chunk, lowers):
+        return [swapped(lower, chip_orders[part][-1]) for part, lower in enumerate(lowers)]
+
     for chunk in range(2):
-        grads_first, grads_second, *totals = feed_call(
-            feed_rel,
-            slopes_rel,
+        grads_first, grads_second, *results = feed_call(
+            rows,
             [
                 feed_pieces[2 * chunk],
                 [feed_pieces[2 * chunk + 1][place] for place in second_places],
             ],
-            totals,
+            before,
+            chip_masks,
             tile,
             after=lower_halves,
         )
+        if chunk == 0:
+            rows, before = results[:2], results[2:]
+            sources = rows
         feed_grads += [grads_first, grads_second]
-        for part, grads in enumerate((grads_first, grads_second)):
-            places = half_places[part][1]
-            pieces = [outer_call(sources, grads, places)]
-            lower_halves += pieces
-            sent.append([swapped(piece, chip_orders[part][-1]) for piece in pieces])
-    out_total, d_total = totals
-    their_masks = [mask ^ 1 for mask in pair_masks[0]]
-    d_feed = absolute(d_total[:row_count], pair_masks[0]) + absolute(
-        swapped(d_total[row_count:], 1), their_masks
-    )
-    block_out = (
-        hidden_one
-        + absolute(out_total[:row_count], pair_masks[0])
-        + absolute(swapped(out_total[row_count:], 1), their_masks)
-    ).astype(jnp.bfloat16)
+        if chunk == 0:
+            lower_halves = feed_lower(0, ())
+            sent = feed_sent(0, lower_halves)
+    out_own, out_other, d_own, d_other = results
+    d_feed = d_own + swapped(d_other, 1)
+    block_out = (hidden_one + (out_own + swapped(out_other, 1))).astype(jnp.bfloat16)
     grad_out = cotangent.astype(jnp.float32)
     d_hidden_part, d_gain_feed = norm_f_back(d_feed)
     d_hidden = grad_out + d_hidden_part
     d_attn = d_hidden.astype(jnp.bfloat16)
-    d_head = contract_rows(d_attn, full, 3 * model_width, after=lower_halves)
-
-    def feed_upper(place, after):
-        starts = (0, 1)[: len(sent[place])]
+    d_head = contract_rows(
+        d_attn, full, 3 * model_width, after=lower_halves
+    )
+
+    def feed_upper(place, arrived, after):
         return outer_call(
-            sources, feed_grads[place], half_places[place % 2][0], None, sent[place], starts, after
-        )
-
-    def chip_sum(total, part):
+            sources, feed_grads[place], half_places[place % 2][0], None, (arrived,), (0,), after
+        )
+
+    def chip_sum(total, part, after):
         for bit in reversed(chip_orders[part][:-1]):
-            total = halved_sum(total, bit)
+            total = halved_sum(total, bit, after)
         return total
 
-    def device_sum(totals):
+    def both_owners(totals):
         half = totals[0].shape[0] // 2
         mine = [total[:half] for total in totals]
         theirs = [swapped(total[half:], 1) for total in totals]
-        return over_groups(jnp.concatenate(mine + theirs, axis=1))
+        return jnp.concatenate(mine + theirs, axis=1)
 
     def both_halves(grads):
         width = grads.shape[1] // 2
@@ -1505,41 +1721,52 @@
         return jnp.concatenate([mine, swapped(theirs, 1)], axis=0)
 
     d_mixed, d_head_gain, back_pairs = pull_call(
-        reach, mixed, d_head, head_gain, flags, pairs, after=(sent[0][0], sent[1][0])
-    )
-    upper_first = [feed_upper(place, ()) for place in range(2)]
-    end_states = scan_call(back_pairs, True, 1, after=upper_first)
-    chip_first = [chip_sum(total, part) for part, total in enumerate(upper_first)]
-    upper_second = [feed_upper(place, (end_states,)) for place in range(2, 4)]
-    chip_second = [chip_sum(total, part) for part, total in enumerate(upper_second)]
+        reach, mixed, d_head, head_gain, flags, pairs
+    )
+    end_states = scan_call(back_pairs, True, 1)
+    upper_first = [feed_upper(place, sent[place], (end_states,)) for place in range(2)]
     both_attn = both_halves(d_attn)
     plain_sources = [
         relative(jnp.concatenate([rows, swapped(rows, 1)], axis=0), pair_masks[0])
         for rows in (normed_low, head_low)
     ]
-    d_queries, d_keys, d_values, d_betas = back_call(
+    d_rows, d_tail, d_before, d_taps, d_betas = back_call(
         row_start,
         flags,
         beta_rows,
-        active,
+        extended,
+        taps,
+        tap_count,
         inverse,
         wy,
         scores,
         start_states,
         end_states,
         d_mixed,
-        after=upper_second,
+        after=upper_first,
     )
     d_logit32 = d_betas * live_rows[:, None] * sigmoid_val * (1.0 - sigmoid_val)
     d_logit = d_logit32.astype(jnp.bfloat16)
-    d_extended, d_kernel = conv_pull(jnp.concatenate([d_queries, d_keys, d_values], axis=1))
+    lower_second = feed_lower(1, (d_betas,))
+    sent_second = feed_sent(1, lower_second)
+    chip_first = [
+        chip_sum(total, part, lower_second) for part, total in enumerate(upper_first)
+    ]
+    early_rows = both_owners(chip_first)
     from_next = passed_along(
-        d_extended[: tap_count - 1].astype(jnp.bfloat16), ("seq", "grp"), -1
+        d_before[:, 9 - tap_count :].astype(jnp.bfloat16), ("seq", "grp"), -1
     ).astype(jnp.float32)
-    d_own = d_extended[tap_count - 1 :] + jnp.pad(
-        from_next, ((row_count - (tap_count - 1), 0), (0, 0))
-    )
-    d_pre = d_own.astype(jnp.bfloat16)
+    fixed = d_tail.at[:, 9 - tap_count :].add(from_next).astype(LOW)
+    d_pre = jnp.concatenate(
+        [
+            jnp.concatenate([d_rows[kind, : row_count - 8], fixed[kind]], axis=0)
+            for kind in range(3)
+        ],
+        axis=1,
+    )
+    d_kernel = jnp.concatenate(
+        [jnp.transpose(d_taps[kind, :tap_count]) for kind in range(3)], axis=0
+    )
     both_pre = both_halves(d_pre)
     fine = model_width // 4
 
@@ -1552,16 +1779,20 @@
 
     plain_slopes = [plain_grads(part) for part in range(2)]
     plain_lower = [
-        outer_call(
-            plain_sources, plain_slopes[part], half_places[part][1], after=(*chip_first, *chip_second)
-        )
+        outer_call(plain_sources, plain_slopes[part], half_places[part][1], after=chip_first)
         for part in range(2)
     ]
     plain_upper = [
-        outer_call(plain_sources, plain_slopes[part], half_places[part][0]) for part in range(2)
+        outer_call(plain_sources, plain_slopes[part], half_places[part][0], after=plain_lower)
+        for part in range(2)
     ]
-    d_normed = contract(d_logit, w_beta) + contract_rows(d_pre, full, 0)
-    feed_kept = [device_sum(chip_first), device_sum(chip_second)]
+    d_normed = contract(d_logit, w_beta) + contract_rows(
+        d_pre, full, 0, after=(*plain_upper, early_rows)
+    )
+    upper_second = [
+        feed_upper(2 + part, sent_second[part], (d_normed,)) for part in range(2)
+    ]
+    feed_early = over_groups(early_rows)
     d_input_part, d_gain_mixer = norm_a_back(d_normed)
     input_grad = (d_hidden + d_input_part).astype(jnp.bfloat16)
     small_grads = jnp.concatenate(
@@ -1593,13 +1824,20 @@
     small_lower = jnp.concatenate(small_blocks[half_blocks:], axis=0)
     vector = jnp.concatenate([d_head_gain[0], jnp.sum(d_logit32, axis=0)])
     padded = jnp.zeros((8, 256), F32).at[0, : vector.shape[0]].set(vector)
-    plain_sum, small_sum, everywhere = reduce_call(
+    rest_orders = [order[:-1] for order in chip_orders]
+    rest_half = upper_second[0].shape[0] // 2
+    feed_late, plain_sum, small_sum, everywhere = reduce_call(
         [
-            (plain_lower, plain_upper, 8),
-            ((small_lower, small_lower), (small_upper, small_upper), 1),
+            (
+                [total[rest_half:] for total in upper_second],
+                [total[:rest_half] for total in upper_second],
+                6,
+                rest_orders,
+            ),
+            (plain_lower, plain_upper, 16, chip_orders),
+            ((small_lower, small_lower), (small_upper, small_upper), 1, chip_orders),
         ],
         padded,
-        chip_orders,
         3,
     )
     replicated = everywhere[0, : vector.shape[0]]
@@ -1609,38 +1847,40 @@
             [jnp.where(my_core == 0, mine, other), jnp.where(my_core == 0, other, mine)], axis=1
         )
 
-    fine = fine // 2
-    groups = [plain_sum[:, at * fine : (at + 1) * fine] for at in range(32)]
+    fine = fine // 4
+    groups = [plain_sum[:, at * fine : (at + 1) * fine] for at in range(64)]
     qkv_grad, out_grad = [
         in_order(
             *[
                 jnp.concatenate(
                     [
-                        groups[4 * kind + 2 * owner + part]
+                        groups[4 * group + 2 * owner + part]
                         for part in range(2)
-                        for kind in range(*span)
+                        for group in range(*span)
                     ],
                     axis=1,
                 )
                 for owner in range(2)
             ]
         )
-        for span in ((0, 6), (6, 8))
+        for span in ((0, 12), (12, 16))
     ]
     feed_sums = []
     for kind in range(3):
         halves = []
         for owner in range(2):
-            for chunk in range(2):
-                at = owner * feed_kept[chunk].shape[1] // 2
-                for start, stop in spans[2 * chunk : 2 * chunk + 2]:
-                    width = stop - start
-                    halves.append(
-                        feed_kept[chunk][:, at + kind * width : at + (kind + 1) * width]
-                    )
-                    at = at + 3 * width
+            at = owner * feed_early.shape[1] // 2
+            for start, stop in spans[:2]:
+                width = stop - start
+                halves.append(feed_early[:, at + kind * width : at + (kind + 1) * width])
+                at = at + 3 * width
+            late = [(stop - start) // 2 for start, stop in spans[2:]]
+            for part in range(2):
+                for group in (2 * kind, 2 * kind + 1):
+                    at = (2 * group + owner) * sum(late) + part * late[0]
+                    halves.append(feed_late[:, at : at + late[part]])
         feed_sums.append(
-            in_order(jnp.concatenate(halves[:4], axis=1), jnp.concatenate(halves[4:], axis=1))
+            in_order(jnp.concatenate(halves[:6], axis=1), jnp.concatenate(halves[6:], axis=1))
         )
     gate_grad, up_grad, down_grad = feed_sums
     sharded = jnp.where(my_core == 0, small_sum[:, :128], small_sum[:, 256:384])

time: 1230 us -> 1170 us (0.951)
  waiting for transfers between devices: 29.7 us -> 85.8 us
  local copies, waits for them, and re-layouts: 149 us -> 93.3 us
  other arithmetic: 101 us -> 47.3 us
    ppermute x32 -> x28, waiting for transfers between devices: 29.6 us -> 85.7 us  [swapped(): lax.ppermute(value, 'seq', [(place, place ^ bit) for place in range(count)])]
    pallas_call x1, Pallas kernels: 181 us -> 229 us  [reduce_call(): pl.pallas_call(functools.partial(reduce_kernel, len(after), group_size, a...]
    unnamed x262 -> x187, local copies, waits for them, and re-layouts: 92.8 us -> 55.1 us
    pallas_call x22 -> x25, Pallas kernels: 336 us -> 311 us  [launch(): pl.pallas_call(body, in_specs=[pl.BlockSpec(memory_space=pl.ANY)] * count...]
    pallas_call x2, Pallas kernels: 175 us -> 156 us  [scan_call(): pl.pallas_call(functools.partial(scan_kernel, len(after), backwards, grou...]
    mul x2 -> x0, other arithmetic: 18.4 us -> none  [the longest x1 10.6 us: conv_act(): moved * valid[offset - 1][:, None] * kernel_all[:, tap_count - 1 - offset]]
    convert_element_type x8 -> x3, other arithmetic: 18.1 us -> 1.52 us  [the longest x1 1.42 us: over_groups(): lax.psum_scatter(rows, 'grp', scatter_dimension=0, tiled=True).astype(F32)]
  transfers between devices with their start and end apart: 38 -> 33, of which waited for: 5 -> 5; matrix products, arithmetic and copies ran while one was open for 19% -> 12% of each run, Pallas kernels for 56% -> 60%
where the time goes in v3:
time: 1170 us; the launch traced here: 1160 us
  Pallas kernels  866 us (74%)
  local copies, waits for them, and re-layouts  93.3 us (8%)
  waiting for transfers between devices  85.8 us (7%)
  other arithmetic  47.3 us (4%)
  starting transfers between devices  25.5 us (2%)
  matrix products  25.5 us (2%)
  between operations  15.2 us (1%)
    pallas_call x25, Pallas kernels, launch(): pl.pallas_call(body, in_specs=[pl.BlockSpec(memory_space=pl.ANY)] * count...  311 us
    pallas_call x1, Pallas kernels, reduce_call(): pl.pallas_call(functools.partial(reduce_kernel, len(after), group_size, a...  229 us
    pallas_call x1, Pallas kernels, gather_call(): pl.pallas_call(functools.partial(gather_kernel, group_size, bits, orders,...  170 us
    pallas_call x2, Pallas kernels, scan_call(): pl.pallas_call(functools.partial(scan_kernel, len(after), backwards, grou...  156 us
    ppermute x28, waiting for transfers between devices, swapped(): lax.ppermute(value, 'seq', [(place, place ^ bit) for place in range(count)])  85.7 us
    unnamed x187, local copies, waits for them, and re-layouts  55.1 us
  transfers between devices with their start and end apart: 33, of which 5 were waited for; matrix products, arithmetic and copies ran while one was open for 12% of the time, Pallas kernels for 60%

profile of v3, /device:TPU:0, one launch (start us, length us, event | category | flops | bytes accessed | tf_op | source)
XLA Modules:
  0.0 1158.8 jit_solution(15430082999401312927)
XLA Ops:
  24.8 170.0 %shard_map.314 = (bf16[2048,8320]{1,0:T(8,128)(2,1)}, bf16[512,2304]{1,0:T(8,128)(2,1)}, bf16[512,2304]{1,0:T(8,128)(2,1)}, bf16[256,4608]{1,0:T(8,128)(2,1)}) custom-call(bf16[64,8320]{1,0:T(8,128)(2,1)} %copy-done.25, bf16[64,9216]{1,0:T(8,128)(2,1)} %copy-done.26), custom_call_target="tpu_custom_call" | custom-call | flops 1 | bytes 1 | tf_op jit(solution)/shard_map/pallas_call | solution.py:1158
  195.4 1.5 collective-permute-start
  198.3 1.9 shard_map.315
  200.7 1.7 convert_reduce_fusion
  204.1 1.6 fusion.72
  205.7 43.2 %collective-permute-done.1.refs_1_.refs_18_.refs_22_.refs_26_ = bf16[512,2304]{1,0:T(8,128)(2,1)} collective-permute-done((bf16[512,2304]{1,0:T(8,128)(2,1)}, bf16[512,2304]{1,0:T(8,128)(2,1)}, u32[]{:S(2)}, u32[]{:S(2)}) %collective-permute-start.1) | collective-permute-done | bytes 2359328 | tf_op jit(solution)/shard_map/ppermute | solution.py:577
  248.9 4.1 pad_maximum_fusion.1
  253.0 1.3 collective-permute-start.4
  254.4 4.1 pad_maximum_fusion
  267.0 13.2 %fusion.4.refs_6_.refs_7_.refs_8_ = bf16[272,6144]{1,0:T(8,128)(2,1)} fusion(bf16[2048,8320]{1,0:T(8,128)(2,1)} %get-tuple-element.80.refs_0_.refs_3_.refs_4_, bf16[256,2048]{1,0:T(8,128)(2,1)S(1)} %fusion.11, bf16[16,2048]{1,0:T(8,128)(2,1)S(1)} %fusion.52), kind=kOutput, calls=%fused_computation.4 | convolution fusion | flops 6849003520 | bytes 29622272 | tf_op jit(solution)/shard_map/dot_general | solution.py:1602
  280.2 45.9 %shard_map.316 = (f32[16,256,256]{2,1,0:T(8,128)}, f32[16,256,256]{2,1,0:T(8,128)}, f32[16,256,256]{2,1,0:T(8,128)}, f32[256,2048]{1,0:T(8,128)}, f32[256,2048]{1,0:T(8,128)}, /*index=5*/bf16[16,128,256]{2,1,0:T(8,128)(2,1)}) custom-call(bf16[512,2304]{1,0:T(8,128)(2,1)} %collective-permute-done.refs_0_.refs_5_.refs_9_.refs_13_, ...), custom_call_target="tpu_custom_call" | custom-call | flops 1 | bytes 1 | tf_op jit(solution)/shard_map/pallas_call | solution.py:42
  326.1 30.5 %collective-permute-done.4.refs_2_.refs_17_.refs_19_.refs_21_.refs_23_.refs_25_.refs_27_ = bf16[1024,2304]{1,0:T(8,128)(2,1)} collective-permute-done((bf16[1024,2304]{1,0:T(8,128)(2,1)}, bf16[1024,2304]{1,0:T(8,128)(2,1)}, u32[]{:S(2)}, u32[]{:S(2)}) %collective-permute-start.4) | collective-permute-done | bytes 4718624 | tf_op jit(solution)/shard_map/ppermute | solution.py:577
  356.6 5.2 collective-permute-done.3.refs_1_.refs_6_.refs_7_.refs_10_.refs_11_.refs_14_.refs_15_
  361.8 6.5 shard_map.317.refs_4_.refs_8_.refs_12_
  369.5 4.7 shard_map.318.refs_16_.refs_20_.refs_24_
  374.2 1.5 collective-permute-start.8
  375.7 1.4 collective-permute-start.9
  377.1 96.7 %shard_map.319.refs_6_.refs_15_ = bf16[16,128,128]{2,1,0:T(8,128)(2,1)} custom-call(bf16[16,128,256]{2,1,0:T(8,128)(2,1)} %get-tuple-element.81.refs_0_.refs_5_), custom_call_target="tpu_custom_call" | custom-call | flops 1 | bytes 1 | tf_op jit(solution)/shard_map/pallas_call | solution.py:553
  476.7 12.0 %shard_map.320 = (f32[256,2048]{1,0:T(8,128)}, bf16[256,2048]{1,0:T(8,128)(2,1)}) custom-call(bf16[512,2304]{1,0:T(8,128)(2,1)} %copy-done.1, bf16[512,2304]{1,0:T(8,128)(2,1)} %copy-done.2, bf16[512,1536]{1,0:T(8,128)(2,1)} %copy-done.9, bf16[512,1536]{1,0:T(8,128)(2,1)} %collective-permute-done.9.refs_3_.refs_17_.refs_21_.refs_25_, ...), custom_call_target="tpu_custom_call" | custom-call | flops 1 | bytes 1 | tf_op jit(solution)/shard_map/pallas_call | solution.py:42
  488.7 6.5 multiply_reduce_fusion.2
  497.1 2.3 collective-permute-done.10.refs_1_
  499.4 33.1 %shard_map.321 = (bf16[3,512,768]{2,1,0:T(8,128)(2,1)}, bf16[3,512,768]{2,1,0:T(8,128)(2,1)}, bf16[512,2048]{1,0:T(8,128)(2,1)}, bf16[512,2048]{1,0:T(8,128)(2,1...) custom-call(bf16[256,2048]{1,0:T(8,128)(2,1)} %copy-done.19, bf16[256,2048]{1,0:T(8,128)(2,1)} %collective-permute-done.10.refs_1_, ...), custom_call_target="tpu_custom_call" | custom-call | flops 1 | bytes 1 | tf_op jit(solution)/shard_map/pallas_call | solution.py:42
  532.5 6.8 shard_map.323.refs_1_
  539.3 1.4 collective-permute-start.17
  540.6 6.7 shard_map.322.refs_0_
  548.7 30.5 %shard_map.324 = (bf16[3,512,768]{2,1,0:T(8,128)(2,1)}, bf16[3,512,512]{2,1,0:T(8,128)(2,1)}, f32[256,2048]{1,0:T(8,128)}, f32[256,2048]{1,0:T(8,128)}, f32[256,2048]{1,0:T(8,128)}, /*index=5*/f32[256,2048]{1,0:T(8,128)}) custom-call(bf16[1024,2304]{1,0:T(8,128)(2,1)} %shard_map.322.refs_0_, bf16[1024,2304]{1,0:T(8,128)(2,1)} %shard_map.323.refs_1_, ...), custom_call_target="tpu_custom_call" | custom-call | flops 1 | bytes 1 | tf_op jit(solution)/shard_map/pallas_call | solution.py:42
  593.4 3.3 fusion.65
  601.1 7.4 shard_map.325.refs_2_
  608.5 14.5 %shard_map.326 = (f32[256,2048]{1,0:T(8,128)}, f32[1,128]{1,0:T(1,128)}, bf16[16,128,256]{2,1,0:T(8,128)(2,1)}) custom-call(f32[256,2048]{1,0:T(8,128)} %get-tuple-element.84.refs_4_.refs_0_, f32[256,2048]{1,0:T(8,128)} %get-tuple-element.97.refs_1_, f32[256,2048]{1,0:T(8,128)} %shard_map.325.refs_2_, f32[1,128]{1,0:T(1,128)} %bitcast.76, ...), custom_call_target="tpu_custom_call" | custom-call | flops 1 | bytes 1 | tf_op jit(solution)/shard_map/pallas_call | solution.py:42
  623.0 59.3 %shard_map.327.refs_0_.refs_16_ = bf16[16,128,128]{2,1,0:T(8,128)(2,1)} custom-call(bf16[16,128,256]{2,1,0:T(8,128)(2,1)} %get-tuple-element.98.refs_0_), custom_call_target="tpu_custom_call" | custom-call | flops 1 | bytes 1 | tf_op jit(solution)/shard_map/pallas_call | solution.py:553
  683.4 8.3 shard_map.329.refs_1_.refs_2_
  691.8 3.2 slice.664
  695.0 1.4 collective-permute-start.19
  696.4 8.3 shard_map.328.refs_0_.refs_2_
  704.6 3.3 slice.663
  707.9 1.4 collective-permute-start.18
  709.3 39.1 %shard_map.330 = (bf16[3,256,2048]{2,1,0:T(8,128)(2,1)}, f32[3,8,2048]{2,1,0:T(8,128)}, f32[3,8,2048]{2,1,0:T(8,128)}, f32[3,8,2048]{2,1,0:T(8,128)}, f32[256,16]{1,0:T(8,128)}) custom-call(bf16[1024,2304]{1,0:T(8,128)(2,1)} %shard_map.328.refs_0_.refs_2_, bf16[1024,2304]{1,0:T(8,128)(2,1)} %shard_map.329.refs_1_.refs_2_, s32[256,1]{1,0:T(8,128)} %copy.114.refs_2_, ...), custom_call_target="tpu_custom_call" | custom-call | flops 1 | bytes 1 | tf_op jit(solution)/shard_map/pallas_call | solution.py:42
  750.6 3.1 slice_bitcast_fusion.2
  753.7 6.8 shard_map.331.refs_0_
  760.5 5.8 shard_map.332.refs_1_
  766.3 4.6 collective-permute-start.28
  771.9 3.1 maximum_maximum_fusion.refs_3_
  774.9 1.6 constant_dynamic-slice_fusion.2
  777.1 6.9 shard_map.334.refs_1_
  784.0 2.8 fusion.70
  787.3 6.9 shard_map.333.refs_0_
  794.2 2.8 fusion.69
  799.3 2.2 pad_maximum_fusion.3
  801.5 6.4 shard_map.336.refs_1_.refs_5_
  807.9 6.4 shard_map.335.refs_0_.refs_4_
  814.9 6.4 shard_map.338.refs_1_.refs_7_
  821.3 6.4 shard_map.337.refs_0_.refs_6_
  827.8 4.5 pad_maximum_fusion.2.refs_2_
  832.3 18.6 %shard_map.339 = f32[256,2048]{1,0:T(8,128)} custom-call(bf16[1024,2048]{1,0:T(8,128)(2,1)} %shard_map.337.refs_0_.refs_6_, bf16[1024,2048]{1,0:T(8,128)(2,1)} %shard_map.338.refs_1_.refs_7_, bf16[256,9216]{1,0:T(8,128)(2,1)} %pad_maximum_fusion.2.refs_2_, bf16[256,6144]{1,0:T(8,128)(2,1)} %copy-done.6, ...), custom_call_target="tpu_custom_call" | custom-call | flops 1 | bytes 1 | tf_op jit(solution)/shard_map/pallas_call | solution.py:42
  851.0 4.3 fusion.12
  856.0 6.7 shard_map.341
  862.8 1.6 fusion.15
  865.1 1.9 fusion.68
  870.4 4.5 collective-permute-done.27.refs_6_
  874.9 8.4 shard_map.340
  883.3 4.9 fusion.67
  888.1 229.0 %shard_map.342 = (f32[64,7680]{1,0:T(8,128)}, f32[64,8192]{1,0:T(8,128)}, f32[64,512]{1,0:T(8,128)}, f32[8,256]{1,0:T(8,128)}) custom-call(bf16[512,2304]{1,0:T(8,128)(2,1)} %get-tuple-element.196.refs_0_, bf16[512,1536]{1,0:T(8,128)(2,1)} %get-tuple-element.198.refs_1_, bf16[512,2304]{1,0:T(8,128)(2,1)} %get-tuple-element.195.refs_2_, ...), custom_call_target="tpu_custom_call" | custom-call | flops 1 | bytes 1 | tf_op jit(solution)/shard_map/pallas_call | solution.py:1453
  1145.1 1.4 convert_element_type.151
  1146.7 1.3 copy-done.24
  (319 shorter events, 100.7 us)
Async XLA Ops:
  7.2 10.0 copy-start.29
  7.2 9.3 copy-start.55
  7.2 9.4 copy-start.56
  7.2 9.5 copy-start.51
  7.2 9.6 copy-start.52
  7.2 9.7 copy-start.53
  7.3 9.9 copy-start.49
  7.3 259.7 %all-gather.5.cloned.1.call-start = ((), (), s32[]{:S(2)}) async-start(), calls=%async_computation.2 | async-start | bytes 2457600 | tf_op jit(solution)/shard_map/all_gather | solution.py:1508
  11.0 10.3 copy-start.33
  21.4 175.6 %copy-start.12 = (bf16[256,2048]{1,0:T(8,128)(2,1)S(1)}, bf16[256,2048]{1,0:T(8,128)(2,1)}, u32[]{:S(2)}) copy-start(bf16[256,2048]{1,0:T(8,128)(2,1)} %param.23) | copy-start | bytes 3145732
  194.7 131.4 %all-gather.3.cloned.1.call-start = ((), (), s32[]{:S(2)}) async-start(), calls=%async_computation.1 | async-start | bytes 2457600 | tf_op jit(solution)/shard_map/all_gather | solution.py:1508
  194.8 54.1 %collective-permute-start.1 = (bf16[512,2304]{1,0:T(8,128)(2,1)}, bf16[512,2304]{1,0:T(8,128)(2,1)}, u32[]{:S(2)}, u32[]{:S(2)}) collective-permute-start(bf16[512,2304]{1,0:T(8,128)(2,1)} %get-tuple-element.79.refs_16_.refs_20_.refs_24_), channel_id=1, source_target_pairs={{0,8},{4,12},{8,0},{12,4},{16,24},{20,28},{24,16},{28,20},{1,9},{5... | collective-permute-start | bytes 7077896 | tf_op jit(solution)/shard_map/ppermute | solution.py:577
  195.4 59.0 %collective-permute-start = (bf16[512,2304]{1,0:T(8,128)(2,1)}, bf16[512,2304]{1,0:T(8,128)(2,1)}, u32[]{:S(2)}, u32[]{:S(2)}) collective-permute-start(bf16[512,2304]{1,0:T(8,128)(2,1)} %get-tuple-element.78.refs_4_.refs_8_.refs_12_), channel_id=1, source_target_pairs={{0,16},{4,20},{8,24},{12,28},{16,0},{20,4},{24,8},{28,12},{1,17},{... | collective-permute-start | bytes 7077896 | tf_op jit(solution)/shard_map/ppermute | solution.py:577
  196.9 69.7 %collective-permute-start.2 = (bf16[3,2048]{1,0:T(4,128)(2,1)S(1)}, bf16[3,2048]{1,0:T(4,128)(2,1)S(1)}, u32[]{:S(2)}, u32[]{:S(2)}) collective-permute-start(bf16[3,2048]{1,0:T(4,128)(2,1)S(1)} %slice.506), channel_id=1, source_target_pairs={{0,1},{1,2},{2,3},{3,4},{4,5},{5,6},{6,7},{7,8},{8,9},{9,10},{10,1... | collective-permute-start | bytes 36872 | tf_op jit(solution)/shard_map/ppermute | solution.py:23
  198.3 946.8 %reduce-scatter.2.cloned.1.call-start = ((), (), s32[]{:S(2)}) async-start(), calls=%async_computation.3 | async-start | bytes 5898240 | tf_op jit(solution)/shard_map/reduce_scatter | solution.py:652
  200.3 65.6 %copy-start.45 = (f32[256]{0:T(256)}, f32[256]{0:T(256)S(1)}, u32[]{:S(2)}) copy-start(f32[256]{0:T(256)S(1)} %convert_element_type.130) | copy-start | bytes 3076
  202.5 64.3 %copy-start.34 = (f32[2048]{0:T(1024)}, f32[2048]{0:T(1024)S(1)}, u32[]{:S(2)}) copy-start(f32[2048]{0:T(1024)S(1)} %get-tuple-element.188) | copy-start | bytes 24580
  204.1 44.8 %copy-start.4 = (bf16[512,2304]{1,0:T(8,128)(2,1)S(1)}, bf16[512,2304]{1,0:T(8,128)(2,1)}, u32[]{:S(2)}) copy-start(bf16[512,2304]{1,0:T(8,128)(2,1)} %get-tuple-element.79.refs_16_.refs_20_.refs_24_) | copy-start | bytes 7077892
  205.7 48.7 %copy-start.3 = (bf16[512,2304]{1,0:T(8,128)(2,1)S(1)}, bf16[512,2304]{1,0:T(8,128)(2,1)}, u32[]{:S(2)}) copy-start(bf16[512,2304]{1,0:T(8,128)(2,1)} %get-tuple-element.78.refs_4_.refs_8_.refs_12_) | copy-start | bytes 7077892
  253.0 103.6 %collective-permute-start.4 = (bf16[1024,2304]{1,0:T(8,128)(2,1)}, bf16[1024,2304]{1,0:T(8,128)(2,1)}, u32[]{:S(2)}, u32[]{:S(2)}) collective-permute-start(bf16[1024,2304]{1,0:T(8,128)(2,1)} %pad_maximum_fusion.1), channel_id=1, source_target_pairs={{0,16},{4,20},{8,24},{12,28},{16,0},{20,4},{24,8},{28,12},{1,17},{... | collective-permute-start | bytes 14155784 | tf_op jit(solution)/shard_map/ppermute | solution.py:577
  258.5 103.3 %collective-permute-start.3 = (bf16[1024,2304]{1,0:T(8,128)(2,1)}, bf16[1024,2304]{1,0:T(8,128)(2,1)}, u32[]{:S(2)}, u32[]{:S(2)}) collective-permute-start(bf16[1024,2304]{1,0:T(8,128)(2,1)} %pad_maximum_fusion), channel_id=1, source_target_pairs={{0,8},{4,12},{8,0},{12,4},{16,24},{20,28},{24,16},{28,20},{1,9},{5... | collective-permute-start | bytes 14155784 | tf_op jit(solution)/shard_map/ppermute | solution.py:577
  263.1 17.2 %copy-start.41 = (s32[256]{0:T(256)}, s32[256]{0:T(256)S(1)}, u32[]{:S(2)}) copy-start(s32[256]{0:T(256)S(1)} %select_reduce_fusion) | copy-start | bytes 3076
  266.9 59.2 %collective-permute-start.5 = (bf16[256,3840]{1,0:T(8,128)(2,1)}, bf16[256,3840]{1,0:T(8,128)(2,1)S(1)}, u32[]{:S(2)}, u32[]{:S(2)}) collective-permute-start(bf16[256,3840]{1,0:T(8,128)(2,1)} %all-gather.5.cloned.1.call-done), channel_id=1, source_target_pairs={{0,4},{4,0},{8,12},{12,8},{16,20},{20,16},{24,28},{28,24},{1,5},{5... | collective-permute-start | bytes 5898248 | tf_op jit(solution)/shard_map/ppermute | solution.py:577
  326.1 35.7 %copy-start.18 = (bf16[256,3840]{1,0:T(8,128)(2,1)}, bf16[256,3840]{1,0:T(8,128)(2,1)S(1)}, u32[]{:S(2)}) copy-start(bf16[256,3840]{1,0:T(8,128)(2,1)S(1)} %collective-permute-done.5.refs_4_) | copy-start | bytes 5898244
  368.3 106.2 %collective-permute-start.6 = (bf16[512,2304]{1,0:T(8,128)(2,1)}, bf16[512,2304]{1,0:T(8,128)(2,1)S(1)}, u32[]{:S(2)}, u32[]{:S(2)}) collective-permute-start(bf16[512,2304]{1,0:T(8,128)(2,1)} %shard_map.317.refs_4_.refs_8_.refs_12_), channel_id=1, source_target_pairs={{0,16},{4,20},{8,24},{12,28},{16,0},{20,4},{24,8},{28,12},{1,17},{... | collective-permute-start | bytes 7077896 | tf_op jit(solution)/shard_map/ppermute | solution.py:577
  369.0 106.1 %collective-permute-start.7 = (bf16[512,2304]{1,0:T(8,128)(2,1)}, bf16[512,2304]{1,0:T(8,128)(2,1)S(1)}, u32[]{:S(2)}, u32[]{:S(2)}) collective-permute-start(bf16[512,2304]{1,0:T(8,128)(2,1)} %shard_map.317.refs_4_.refs_8_.refs_12_), channel_id=1, source_target_pairs={{0,8},{4,12},{8,0},{12,4},{16,24},{20,28},{24,16},{28,20},{1,9},{5... | collective-permute-start | bytes 7077896 | tf_op jit(solution)/shard_map/ppermute | solution.py:577
  374.2 99.6 %collective-permute-start.8 = (bf16[512,1536]{1,0:T(8,128)(2,1)}, bf16[512,1536]{1,0:T(8,128)(2,1)S(1)}, u32[]{:S(2)}, u32[]{:S(2)}) collective-permute-start(bf16[512,1536]{1,0:T(8,128)(2,1)} %shard_map.318.refs_16_.refs_20_.refs_24_), channel_id=1, source_target_pairs={{0,8},{4,12},{8,0},{12,4},{16,24},{20,28},{24,16},{28,20},{1,9},{5... | collective-permute-start | bytes 4718600 | tf_op jit(solution)/shard_map/ppermute | solution.py:577
  375.7 99.3 %collective-permute-start.9 = (bf16[512,1536]{1,0:T(8,128)(2,1)}, bf16[512,1536]{1,0:T(8,128)(2,1)}, u32[]{:S(2)}, u32[]{:S(2)}) collective-permute-start(bf16[512,1536]{1,0:T(8,128)(2,1)} %shard_map.318.refs_16_.refs_20_.refs_24_), channel_id=1, source_target_pairs={{0,16},{4,20},{8,24},{12,28},{16,0},{20,4},{24,8},{28,12},{1,17},{... | collective-permute-start | bytes 4718600 | tf_op jit(solution)/shard_map/ppermute | solution.py:577
  377.1 120.0 %collective-permute-start.11 = (bf16[256,2048]{1,0:T(8,128)(2,1)}, bf16[256,2048]{1,0:T(8,128)(2,1)}, u32[]{:S(2)}, u32[]{:S(2)}) collective-permute-start(bf16[256,2048]{1,0:T(8,128)(2,1)} %refs_2_.1), channel_id=1, source_target_pairs={{0,4},{4,0},{8,12},{12,8},{16,20},{20,16},{24,28},{28,24},{1,5},{5... | collective-permute-start | bytes 3145736 | tf_op jit(solution)/shard_map/ppermute | solution.py:577
  473.8 74.8 %collective-permute-start.13 = (bf16[512,1536]{1,0:T(8,128)(2,1)S(1)}, bf16[512,1536]{1,0:T(8,128)(2,1)}, u32[]{:S(2)}, u32[]{:S(2)}) collective-permute-start(bf16[512,1536]{1,0:T(8,128)(2,1)S(1)} %collective-permute-done.8.refs_2_.refs_18_.refs_22_.refs_26_), channel_id=1, source_target_pairs={{0,16},{4,20},{8,24},{12,28},{16,0},{20,4},{24,8},{28,12},{1,17},{... | collective-permute-start | bytes 4718600 | tf_op jit(solution)/shard_map/ppermute | solution.py:577
  474.6 74.1 %collective-permute-start.12 = (bf16[512,2304]{1,0:T(8,128)(2,1)S(1)}, bf16[512,2304]{1,0:T(8,128)(2,1)}, u32[]{:S(2)}, u32[]{:S(2)}) collective-permute-start(bf16[512,2304]{1,0:T(8,128)(2,1)S(1)} %collective-permute-done.6.refs_0_.refs_5_.refs_9_.refs_13_), channel_id=1, source_target_pairs={{0,8},{4,12},{8,0},{12,4},{16,24},{20,28},{24,16},{28,20},{1,9},{5... | collective-permute-start | bytes 7077896 | tf_op jit(solution)/shard_map/ppermute | solution.py:577
  495.2 37.3 %copy-start.10 = (f32[256,2048]{1,0:T(8,128)}, f32[256,2048]{1,0:T(8,128)S(1)}, u32[]{:S(2)}) copy-start(f32[256,2048]{1,0:T(8,128)S(1)} %get-tuple-element.375) | copy-start | bytes 6291460
  496.6 2.8 collective-permute-start.10
  496.6 82.7 %collective-permute-start.20 = (bf16[256,2048]{1,0:T(8,128)(2,1)S(1)}, bf16[256,2048]{1,0:T(8,128)(2,1)}, u32[]{:S(2)}, u32[]{:S(2)}) collective-permute-start(bf16[256,2048]{1,0:T(8,128)(2,1)S(1)} %fusion.11), channel_id=1, source_target_pairs={{0,4},{4,0},{8,12},{12,8},{16,20},{20,16},{24,28},{28,24},{1,5},{5... | collective-permute-start | bytes 3145736 | tf_op jit(solution)/shard_map/ppermute | solution.py:577
  539.3 144.2 %collective-permute-start.17 = (bf16[1024,2304]{1,0:T(8,128)(2,1)}, bf16[1024,2304]{1,0:T(8,128)(2,1)}, u32[]{:S(2)}, u32[]{:S(2)}) collective-permute-start(bf16[1024,2304]{1,0:T(8,128)(2,1)} %shard_map.323.refs_1_), channel_id=1, source_target_pairs={{0,16},{4,20},{8,24},{12,28},{16,0},{20,4},{24,8},{28,12},{1,17},{... | collective-permute-start | bytes 14155784 | tf_op jit(solution)/shard_map/ppermute | solution.py:577
  547.3 149.0 %collective-permute-start.16 = (bf16[1024,2304]{1,0:T(8,128)(2,1)}, bf16[1024,2304]{1,0:T(8,128)(2,1)}, u32[]{:S(2)}, u32[]{:S(2)}) collective-permute-start(bf16[1024,2304]{1,0:T(8,128)(2,1)} %shard_map.322.refs_0_), channel_id=1, source_target_pairs={{0,8},{4,12},{8,0},{12,4},{16,24},{20,28},{24,16},{28,20},{1,9},{5... | collective-permute-start | bytes 14155784 | tf_op jit(solution)/shard_map/ppermute | solution.py:577
  579.1 12.3 %collective-permute-start.15 = (f32[256,2048]{1,0:T(8,128)}, f32[256,2048]{1,0:T(8,128)S(1)}, u32[]{:S(2)}, u32[]{:S(2)}) collective-permute-start(f32[256,2048]{1,0:T(8,128)} %get-tuple-element.96), channel_id=1, source_target_pairs={{0,4},{4,0},{8,12},{12,8},{16,20},{20,16},{24,28},{28,24},{1,5},{5... | collective-permute-start | bytes 6291464 | tf_op jit(solution)/shard_map/ppermute | solution.py:577
  580.6 7.4 collective-permute-start.21
  582.0 10.4 collective-permute-start.14
  596.7 3.7 copy-start.15
  596.7 85.6 %collective-permute-start.24 = (bf16[256,1024]{1,0:T(8,128)(2,1)S(1)}, bf16[256,1024]{1,0:T(8,128)(2,1)S(1)}, u32[]{:S(2)}, u32[]{:S(2)}) collective-permute-start(bf16[256,1024]{1,0:T(8,128)(2,1)S(1)} %get-tuple-element.325), channel_id=1, source_target_pairs={{0,4},{4,0},{8,12},{12,8},{16,20},{20,16},{24,28},{28,24},{1,5},{5... | collective-permute-start | bytes 1572872 | tf_op jit(solution)/shard_map/ppermute | solution.py:577
  695.0 82.1 %collective-permute-start.19 = (bf16[512,2304]{1,0:T(8,128)(2,1)}, bf16[512,2304]{1,0:T(8,128)(2,1)}, u32[]{:S(2)}, u32[]{:S(2)}) collective-permute-start(bf16[512,2304]{1,0:T(8,128)(2,1)} %slice.664), channel_id=1, source_target_pairs={{0,8},{4,12},{8,0},{12,4},{16,24},{20,28},{24,16},{28,20},{1,9},{5... | collective-permute-start | bytes 7077896 | tf_op jit(solution)/shard_map/ppermute | solution.py:577
  707.9 79.4 %collective-permute-start.18 = (bf16[512,2304]{1,0:T(8,128)(2,1)}, bf16[512,2304]{1,0:T(8,128)(2,1)}, u32[]{:S(2)}, u32[]{:S(2)}) collective-permute-start(bf16[512,2304]{1,0:T(8,128)(2,1)} %slice.663), channel_id=1, source_target_pairs={{0,16},{4,20},{8,24},{12,28},{16,0},{20,4},{24,8},{28,12},{1,17},{... | collective-permute-start | bytes 7077896 | tf_op jit(solution)/shard_map/ppermute | solution.py:577
  749.3 22.0 %collective-permute-start.22 = (bf16[3,3,2048]{2,1,0:T(4,128)(2,1)S(1)}, bf16[3,3,2048]{2,1,0:T(4,128)(2,1)S(1)}, u32[]{:S(2)}, u32[]{:S(2)}) collective-permute-start(bf16[3,3,2048]{2,1,0:T(4,128)(2,1)S(1)} %slice.890), channel_id=1, source_target_pairs={{1,0},{2,1},{3,2},{4,3},{5,4},{6,5},{7,6},{8,7},{9,8},{10,9},{11,1... | collective-permute-start | bytes 110600 | tf_op jit(solution)/shard_map/ppermute | solution.py:23
  760.5 10.8 copy-start.32
  766.3 89.7 %collective-permute-start.28 = (bf16[1024,1536]{1,0:T(8,128)(2,1)}, bf16[1024,1536]{1,0:T(8,128)(2,1)}, u32[]{:S(2)}, u32[]{:S(2)}) collective-permute-start(bf16[1024,1536]{1,0:T(8,128)(2,1)} %shard_map.332.refs_1_), channel_id=1, source_target_pairs={{0,16},{4,20},{8,24},{12,28},{16,0},{20,4},{24,8},{28,12},{1,17},{... | collective-permute-start | bytes 9437192 | tf_op jit(solution)/shard_map/ppermute | solution.py:577
  770.8 104.0 %collective-permute-start.27 = (bf16[1024,2304]{1,0:T(8,128)(2,1)}, bf16[1024,2304]{1,0:T(8,128)(2,1)}, u32[]{:S(2)}, u32[]{:S(2)}) collective-permute-start(bf16[1024,2304]{1,0:T(8,128)(2,1)} %shard_map.331.refs_0_), channel_id=1, source_target_pairs={{0,8},{4,12},{8,0},{12,4},{16,24},{20,28},{24,16},{28,20},{1,9},{5... | collective-permute-start | bytes 14155784 | tf_op jit(solution)/shard_map/ppermute | solution.py:577
  777.1 21.0 %collective-permute-start.23 = (bf16[256,3072]{1,0:T(8,128)(2,1)}, bf16[256,3072]{1,0:T(8,128)(2,1)S(1)}, u32[]{:S(2)}, u32[]{:S(2)}) collective-permute-start(bf16[256,3072]{1,0:T(8,128)(2,1)} %get-tuple-element.205), channel_id=1, source_target_pairs={{0,4},{4,0},{8,12},{12,8},{16,20},{20,16},{24,28},{28,24},{1,5},{5... | collective-permute-start | bytes 4718600 | tf_op jit(solution)/shard_map/ppermute | solution.py:577
  786.8 41.0 %collective-permute-start.26 = (bf16[256,2304]{1,0:T(8,128)(2,1)}, bf16[256,2304]{1,0:T(8,128)(2,1)}, u32[]{:S(2)}, u32[]{:S(2)}) collective-permute-start(bf16[256,2304]{1,0:T(8,128)(2,1)} %get-tuple-element.225), channel_id=1, source_target_pairs={{0,4},{4,0},{8,12},{12,8},{16,20},{20,16},{24,28},{28,24},{1,5},{5... | collective-permute-start | bytes 3538952 | tf_op jit(solution)/shard_map/ppermute | solution.py:577
  794.1 3.6 copy-start.57
  797.0 30.8 %collective-permute-start.25 = (bf16[256,2304]{1,0:T(8,128)(2,1)}, bf16[256,2304]{1,0:T(8,128)(2,1)}, u32[]{:S(2)}, u32[]{:S(2)}) collective-permute-start(bf16[256,2304]{1,0:T(8,128)(2,1)} %get-tuple-element.223), channel_id=1, source_target_pairs={{0,4},{4,0},{8,12},{12,8},{16,20},{20,16},{24,28},{28,24},{1,5},{5... | collective-permute-start | bytes 3538952 | tf_op jit(solution)/shard_map/ppermute | solution.py:577
  832.3 18.6 %copy-start.8 = (bf16[2048,128]{1,0:T(8,128)(2,1)S(1)}, bf16[2048,128]{1,0:T(8,128)(2,1)}, u32[]{:S(2)}) copy-start(bf16[2048,128]{1,0:T(8,128)(2,1)} %shard_map.315) | copy-start | bytes 1572868
  832.3 18.6 %copy-start.13 = (bf16[256,2048]{1,0:T(8,128)(2,1)S(1)}, bf16[256,2048]{1,0:T(8,128)(2,1)}, u32[]{:S(2)}) copy-start(bf16[256,2048]{1,0:T(8,128)(2,1)} %param.23) | copy-start | bytes 3145732
  832.3 18.6 %copy-start.35 = (f32[2048]{0:T(1024)S(1)}, f32[2048]{0:T(1024)}, u32[]{:S(2)}) copy-start(f32[2048]{0:T(1024)} %copy-done.34) | copy-start | bytes 24580
  832.3 18.6 %copy-start.43 = (f32[256]{0:T(256)S(1)}, f32[256]{0:T(256)}, u32[]{:S(2)}) copy-start(f32[256]{0:T(256)} %copy-done.42) | copy-start | bytes 3076
  850.9 4.3 copy-start.37
  850.9 4.3 copy-start.38
  851.0 4.3 copy-start.39
  855.4 12.0 %collective-permute-start.29 = (f32[2048,30]{0,1:T(8,128)S(1)}, f32[2048,30]{0,1:T(8,128)}, u32[]{:S(2)}, u32[]{:S(2)}) collective-permute-start(f32[2048,30]{0,1:T(8,128)S(1)} %concatenate.145), channel_id=1, source_target_pairs={{0,4},{4,0},{8,12},{12,8},{16,20},{20,16},{24,28},{28,24},{1,5},{5... | collective-permute-start | bytes 737288 | tf_op jit(solution)/shard_map/ppermute | solution.py:577
  856.0 6.8 copy-start.48
  856.0 6.8 copy-start.50
  856.0 6.8 copy-start.5
  856.0 6.8 copy-start.16
  856.0 6.8 copy-start.44
  (30 other events, 62.1 us)
Sparse Core Ops, SparseCore 0:
  194.9 41.4 all-gather.4
  238.5 41.7 all-gather.2
  832.4 83.1 reduce-scatter.1

commit v4 on v3

--- a/solution.py
+++ b/solution.py
@@ -630,11 +630,10 @@
     total[...] = (kept[...].astype(F32) + arrived[...].astype(F32)).astype(LOW)
 
 
-def halved_sum(kept, bit, after=()):
-    rows, width = kept.shape
-    half = rows // 2
-    arrived = swapped(kept[half:], bit)
-    tile = tile_of(width, 512)
+def halved_sum(kept, lower, bit, after=()):
+    half, width = kept.shape
+    arrived = swapped(lower, bit)
+    tile = wide_tile(width)
     spot = pl.BlockSpec((half, tile), lambda step: (0, step))
     return launch(
         add_kernel,
@@ -650,6 +649,14 @@
 
 def over_groups(rows):
     return lax.psum_scatter(rows, "grp", scatter_dimension=0, tiled=True).astype(F32)
+
+
+def wide_tile(width, start=0):
+    for parts in (1, 2, 3, 4, 6, 9):
+        tile = width // parts
+        if width % parts == 0 and tile % 128 == 0 and tile <= 1024 and start % tile == 0:
+            return tile
+    return 128
 
 
 def tile_of(width, largest):
@@ -684,9 +691,7 @@
 
 
 def join_columns(first, second, start, width, after=()):
-    tile = tile_of(width, 1024)
-    while start % tile:
-        tile = tile // 2
+    tile = wide_tile(width, start)
     rows = first.shape[0]
     return launch(
         join_kernel,
@@ -712,7 +717,7 @@
 
 def contract_rows(grads, weights, start, after=()):
     tokens, width = grads.shape
-    tile = tile_of(width, 512)
+    tile = tile_of(width, 1024)
     depth = weights.shape[0]
     first = start // tile
     return launch(
@@ -744,10 +749,27 @@
     return spots
 
 
-def cores_turned(block):
-    half = block.shape[1] // 2
-    turned = jnp.concatenate([block[:, half:], block[:, :half]], axis=1)
-    return jnp.where(lax.rem(lax.axis_index("seq"), 2) == 0, block, turned)
+def fill_by_core(pairs):
+    def store(turn):
+        for put, block in pairs:
+            half = block.shape[1] // 2
+            if turn:
+                wide = block.astype(F32) if half % 128 else block
+                wide = jnp.concatenate([wide[:, half:], wide[:, :half]], axis=1)
+                put(wide.astype(block.dtype))
+            else:
+                put(block)
+
+    core = lax.rem(lax.axis_index("seq"), 2)
+    pl.when(core == 0)(functools.partial(store, False))
+    pl.when(core == 1)(functools.partial(store, True))
+
+
+def putter(target, rows, columns_now):
+    def put(value):
+        target[rows, columns_now] = value
+
+    return put
 
 
 def feed_kernel(count, cuts, masks, stage, *refs):
@@ -771,10 +793,15 @@
         if stage == 0:
             spots = chip_spots(masks, depth)
             half = tokens // 2
+            first_rows, second_rows = slice(0, half), slice(half, tokens)
             for target, (own, other) in ((feed, given[:2]), (slopes, given[2:])):
                 for span, spot in zip(spans, spots):
-                    target[:half, span] = cores_turned(own[:, spot].astype(F32)).astype(LOW)
-                    target[half:, span] = cores_turned(other[:, spot].astype(F32)).astype(LOW)
+                    fill_by_core(
+                        [
+                            (putter(target, first_rows, span), own[:, spot]),
+                            (putter(target, second_rows, span), other[:, spot]),
+                        ]
+                    )
             out_total[...] = jnp.zeros_like(out_total)
             d_total[...] = jnp.zeros_like(d_total)
         else:
@@ -822,8 +849,12 @@
             half = tokens // 2
             for source, own, other in ((out_total, out_own, out_other), (d_total, d_own, d_other)):
                 for span, spot in zip(spans, spots):
-                    own[:, spot] = cores_turned(source[:half, span])
-                    other[:, spot] = cores_turned(source[half:, span])
+                    fill_by_core(
+                        [
+                            (putter(own, slice(None), spot), source[:half, span]),
+                            (putter(other, slice(None), spot), source[half:, span]),
+                        ]
+                    )
 
 
 def feed_call(rows, piece_lists, before, masks, tile, after=()):
@@ -877,11 +908,12 @@
     )
 
 
-def outer_kernel(count, kinds, starts, first_kind, *refs):
+def outer_kernel(count, kinds, starts, first_kind, outs, *refs):
     sources = (refs[:count], refs[count : 2 * count])
-    grads, arrived, out = refs[2 * count], refs[2 * count + 1 : -1], refs[-1]
+    grads, arrived, results = refs[2 * count], refs[2 * count + 1 : -outs], refs[-outs:]
     kind = pl.program_id(0) + first_kind
-    depth = out.shape[0] // count
+    depth = outs * results[0].shape[0] // count
+    each = count // outs
 
     def fill(source, added):
         for place in range(count):
@@ -892,7 +924,8 @@
             )
             if added is not None:
                 total = total + added[rows].astype(F32)
-            out[rows] = total.astype(LOW)
+            inside = place % each
+            results[place // each][inside * depth : (inside + 1) * depth] = total.astype(LOW)
 
     for which in range(2):
         wanted = (kind == kinds - 1) if which else (kind < kinds - 1)
@@ -905,7 +938,7 @@
             pl.when(wanted & inside)(functools.partial(fill, sources[which], added))
 
 
-def outer_call(sources, grads, places, span=None, arrived=(), starts=(0,), after=()):
+def outer_call(sources, grads, places, span=None, arrived=(), starts=(0,), after=(), outs=1):
     tokens, model = sources[0].shape
     kinds, _, width = grads.shape
     blocks = 2 * len(places)
@@ -923,20 +956,21 @@
             (half, width), lambda kind: (0, jnp.clip(kind + first_kind - start, 0, most))
         )
 
-    return launch(
-        functools.partial(outer_kernel, len(places), kinds, starts, first_kind),
+    results = launch(
+        functools.partial(outer_kernel, len(places), kinds, starts, first_kind, outs),
         after,
         grid=(last,),
         in_specs=[own(place) for place in places] * 2
         + [pl.BlockSpec((1, tokens, width), lambda kind: (first_kind + kind, 0, 0))]
         + [added(array, start) for array, start in zip(arrived, starts)],
-        out_specs=pl.BlockSpec((half, width), lambda kind: (0, kind)),
-        out_shape=jax.ShapeDtypeStruct((half, last * width), LOW),
+        out_specs=[pl.BlockSpec((half // outs, width), lambda kind: (0, kind))] * outs,
+        out_shape=[jax.ShapeDtypeStruct((half // outs, last * width), LOW)] * outs,
         cost_estimate=estimate(1, 1),
         operands=(
             *([sources[0]] * len(places)), *([sources[1]] * len(places)), grads, *arrived,
         ),
     )
+    return results[0] if outs == 1 else tuple(results)
 
 
 def gather_kernel(
@@ -1660,10 +1694,13 @@
     feed_grads, lower_halves = [], []
 
     def feed_lower(chunk, after):
-        return [
-            outer_call(sources, feed_grads[2 * chunk + part], half_places[part][1], after=after)
-            for part in range(2)
-        ]
+        lowers = []
+        for part in range(2):
+            grads = feed_grads[2 * chunk + part]
+            lowers.append(
+                outer_call(sources, grads, half_places[part][1], after=(*after, *lowers))
+            )
+        return lowers
 
     def feed_sent(chunk, lowers):
         return [swapped(lower, chip_orders[part][-1]) for part, lower in enumerate(lowers)]
@@ -1700,12 +1737,23 @@
 
     def feed_upper(place, arrived, after):
         return outer_call(
-            sources, feed_grads[place], half_places[place % 2][0], None, (arrived,), (0,), after
-        )
-
-    def chip_sum(total, part, after):
-        for bit in reversed(chip_orders[part][:-1]):
-            total = halved_sum(total, bit, after)
+            sources,
+            feed_grads[place],
+            half_places[place % 2][0],
+            None,
+            (arrived,),
+            (0,),
+            after,
+            2,
+        )
+
+    def chip_sum(halves, part, after):
+        bits = list(reversed(chip_orders[part][:-1]))
+        for place, bit in enumerate(bits):
+            total = halved_sum(*halves, bit, after)
+            middle = total.shape[0] // 2
+            if place + 1 < len(bits):
+                halves = (total[:middle], total[middle:])
         return total
 
     def both_owners(totals):
@@ -1743,7 +1791,7 @@
         start_states,
         end_states,
         d_mixed,
-        after=upper_first,
+        after=[half for halves in upper_first for half in halves],
     )
     d_logit32 = d_betas * live_rows[:, None] * sigmoid_val * (1.0 - sigmoid_val)
     d_logit = d_logit32.astype(jnp.bfloat16)
@@ -1825,17 +1873,16 @@
     vector = jnp.concatenate([d_head_gain[0], jnp.sum(d_logit32, axis=0)])
     padded = jnp.zeros((8, 256), F32).at[0, : vector.shape[0]].set(vector)
     rest_orders = [order[:-1] for order in chip_orders]
-    rest_half = upper_second[0].shape[0] // 2
-    feed_late, plain_sum, small_sum, everywhere = reduce_call(
+    small_sum, feed_late, plain_sum, everywhere = reduce_call(
         [
+            ((small_lower, small_lower), (small_upper, small_upper), 1, chip_orders),
             (
-                [total[rest_half:] for total in upper_second],
-                [total[:rest_half] for total in upper_second],
+                [lower for _, lower in upper_second],
+                [upper for upper, _ in upper_second],
                 6,
                 rest_orders,
             ),
             (plain_lower, plain_upper, 16, chip_orders),
-            ((small_lower, small_lower), (small_upper, small_upper), 1, chip_orders),
         ],
         padded,
         3,

time: 1170 us -> 1160 us (level)
  local copies, waits for them, and re-layouts: 93.3 us -> 78.1 us
    slice x4 -> x0, local copies, waits for them, and re-layouts: 13.3 us -> none  [the longest x2 6.77 us: local(): total[:rest_half]]
    unnamed x187 -> x189, local copies, waits for them, and re-layouts: 55.1 us -> 51.3 us
  transfers between devices with their start and end apart: 33 -> 33, of which waited for: 5 -> 5; matrix products, arithmetic and copies ran while one was open for 12% -> 10% of each run, Pallas kernels for 60% -> 61%
where the time goes in v4:
time: 1160 us; the launch traced here: 1150 us
  Pallas kernels  874 us (75%)
  waiting for transfers between devices  88 us (8%)
  local copies, waits for them, and re-layouts  78.1 us (7%)
  other arithmetic  47.4 us (4%)
  starting transfers between devices  24.6 us (2%)
  matrix products  23 us (2%)
  between operations  15.2 us (1%)
    pallas_call x25, Pallas kernels, launch(): pl.pallas_call(body, in_specs=[pl.BlockSpec(memory_space=pl.ANY)] * count...  306 us
    pallas_call x1, Pallas kernels, reduce_call(): pl.pallas_call(functools.partial(reduce_kernel, len(after), group_size, a...  239 us
    pallas_call x1, Pallas kernels, gather_call(): pl.pallas_call(functools.partial(gather_kernel, group_size, bits, orders,...  170 us
    pallas_call x2, Pallas kernels, scan_call(): pl.pallas_call(functools.partial(scan_kernel, len(after), backwards, grou...  159 us
    ppermute x28, waiting for transfers between devices, swapped(): lax.ppermute(value, 'seq', [(place, place ^ bit) for place in range(count)])  87.9 us
    unnamed x189, local copies, waits for them, and re-layouts  51.3 us
  transfers between devices with their start and end apart: 33, of which 5 were waited for; matrix products, arithmetic and copies ran while one was open for 10% of the time, Pallas kernels for 61%

profile of v4, /device:TPU:0, one launch (start us, length us, event | category | flops | bytes accessed | tf_op | source)
XLA Modules:
  0.0 1150.2 jit_solution(7400583215989188519)
XLA Ops:
  27.8 170.0 %shard_map.314 = (bf16[2048,8320]{1,0:T(8,128)(2,1)}, bf16[512,2304]{1,0:T(8,128)(2,1)}, bf16[512,2304]{1,0:T(8,128)(2,1)}, bf16[256,4608]{1,0:T(8,128)(2,1)}) custom-call(bf16[64,8320]{1,0:T(8,128)(2,1)} %copy-done.30, bf16[64,9216]{1,0:T(8,128)(2,1)} %copy-done.31), custom_call_target="tpu_custom_call" | custom-call | flops 1 | bytes 1 | tf_op jit(solution)/shard_map/pallas_call | solution.py:1192
  198.5 1.5 collective-permute-start
  201.4 1.9 shard_map.315
  203.8 1.9 convert_reduce_fusion
  207.4 1.6 fusion.65
  209.0 42.8 %collective-permute-done.1.refs_1_.refs_18_.refs_22_.refs_26_ = bf16[512,2304]{1,0:T(8,128)(2,1)S(1)} collective-permute-done((bf16[512,2304]{1,0:T(8,128)(2,1)}, bf16[512,2304]{1,0:T(8,128)(2,1)S(1)}, u32[]{:S(2)}, u32[]{:S(2)}) %collective-permute-start.1) | collective-permute-done | bytes 2359328 | tf_op jit(solution)/shard_map/ppermute | solution.py:577
  251.8 2.6 pad_maximum_fusion.1
  254.7 1.3 collective-permute-start.4
  256.1 4.2 pad_maximum_fusion
  265.8 13.2 %fusion.4.refs_6_.refs_7_.refs_8_.refs_9_.refs_10_ = bf16[272,6144]{1,0:T(8,128)(2,1)} fusion(bf16[2048,8320]{1,0:T(8,128)(2,1)} %get-tuple-element.88.refs_0_.refs_3_.refs_4_, bf16[256,2048]{1,0:T(8,128)(2,1)S(1)} %fusion.11, bf16[16,2048]{1,0:T(8,128)(2,1)S(1)} %fusion.52), kind=kOutput, calls=%fused_computation.4 | convolution fusion | flops 6849003520 | bytes 29622272 | tf_op jit(solution)/shard_map/dot_general | solution.py:1636
  279.0 45.7 %shard_map.316 = (f32[16,256,256]{2,1,0:T(8,128)}, f32[16,256,256]{2,1,0:T(8,128)}, f32[16,256,256]{2,1,0:T(8,128)}, f32[256,2048]{1,0:T(8,128)}, f32[256,2048]{1,0:T(8,128)}, /*index=5*/bf16[16,128,256]{2,1,0:T(8,128)(2,1)}) custom-call(bf16[512,2304]{1,0:T(8,128)(2,1)} %collective-permute-done.refs_0_.refs_5_.refs_9_.refs_13_, ...), custom_call_target="tpu_custom_call" | custom-call | flops 1 | bytes 1 | tf_op jit(solution)/shard_map/pallas_call | solution.py:42
  324.7 33.7 %collective-permute-done.4.refs_2_.refs_17_.refs_19_.refs_21_.refs_23_.refs_25_.refs_27_ = bf16[1024,2304]{1,0:T(8,128)(2,1)} collective-permute-done((bf16[1024,2304]{1,0:T(8,128)(2,1)}, bf16[1024,2304]{1,0:T(8,128)(2,1)}, u32[]{:S(2)}, u32[]{:S(2)}) %collective-permute-start.4) | collective-permute-done | bytes 4718624 | tf_op jit(solution)/shard_map/ppermute | solution.py:577
  358.4 5.3 collective-permute-done.3.refs_1_.refs_6_.refs_7_.refs_10_.refs_11_.refs_14_.refs_15_
  363.7 3.9 shard_map.317.refs_4_.refs_8_.refs_12_
  368.9 2.3 shard_map.318.refs_16_.refs_20_.refs_24_
  371.3 1.5 collective-permute-start.8
  372.8 1.3 collective-permute-start.9
  374.1 99.2 %shard_map.319.refs_6_.refs_17_ = bf16[16,128,128]{2,1,0:T(8,128)(2,1)} custom-call(bf16[16,128,256]{2,1,0:T(8,128)(2,1)} %get-tuple-element.89.refs_0_.refs_5_), custom_call_target="tpu_custom_call" | custom-call | flops 1 | bytes 1 | tf_op jit(solution)/shard_map/pallas_call | solution.py:553
  476.7 12.0 %shard_map.320 = (f32[256,2048]{1,0:T(8,128)}, bf16[256,2048]{1,0:T(8,128)(2,1)}) custom-call(bf16[512,2304]{1,0:T(8,128)(2,1)} %copy-done.2, bf16[512,2304]{1,0:T(8,128)(2,1)} %copy-done.3, bf16[512,1536]{1,0:T(8,128)(2,1)} %collective-permute-done.8.refs_2_.refs_18_.refs_22_.refs_26_, bf16[512,1536]{1,0:T(8,128)(2,1)} %copy-done.10, ...), custom_call_target="tpu_custom_call" | custom-call | flops 1 | bytes 1 | tf_op jit(solution)/shard_map/pallas_call | solution.py:42
  488.7 6.5 multiply_reduce_fusion.2
  496.0 3.0 collective-permute-done.10.refs_1_
  499.0 40.6 %shard_map.321 = (bf16[3,512,768]{2,1,0:T(8,128)(2,1)}, bf16[3,512,768]{2,1,0:T(8,128)(2,1)}, bf16[512,2048]{1,0:T(8,128)(2,1)}, bf16[512,2048]{1,0:T(8,128)(2,1...) custom-call(bf16[256,2048]{1,0:T(8,128)(2,1)} %copy-done.20, bf16[256,2048]{1,0:T(8,128)(2,1)} %collective-permute-done.10.refs_1_, ...), custom_call_target="tpu_custom_call" | custom-call | flops 1 | bytes 1 | tf_op jit(solution)/shard_map/pallas_call | solution.py:42
  539.6 6.7 shard_map.322.refs_0_
  546.3 6.7 shard_map.323.refs_1_
  553.0 1.3 collective-permute-start.17
  554.4 1.3 collective-permute-start.16
  555.7 30.4 %shard_map.324 = (bf16[3,512,768]{2,1,0:T(8,128)(2,1)}, bf16[3,512,512]{2,1,0:T(8,128)(2,1)}, f32[256,2048]{1,0:T(8,128)}, f32[256,2048]{1,0:T(8,128)}, f32[256,2048]{1,0:T(8,128)}, /*index=5*/f32[256,2048]{1,0:T(8,128)}) custom-call(bf16[1024,2304]{1,0:T(8,128)(2,1)} %shard_map.322.refs_0_, bf16[1024,2304]{1,0:T(8,128)(2,1)} %shard_map.323.refs_1_, ...), custom_call_target="tpu_custom_call" | custom-call | flops 1 | bytes 1 | tf_op jit(solution)/shard_map/pallas_call | solution.py:42
  588.8 3.1 collective-permute-done.21
  594.3 2.6 multiply_reduce_fusion
  596.9 4.9 fusion.60
  606.0 7.0 shard_map.325.refs_2_
  612.9 14.1 %shard_map.326 = (f32[256,2048]{1,0:T(8,128)}, f32[1,128]{1,0:T(1,128)}, bf16[16,128,256]{2,1,0:T(8,128)(2,1)}) custom-call(f32[256,2048]{1,0:T(8,128)} %get-tuple-element.92.refs_4_.refs_0_, f32[256,2048]{1,0:T(8,128)} %get-tuple-element.105.refs_1_, f32[256,2048]{1,0:T(8,128)} %shard_map.325.refs_2_, f32[1,128]{1,0:T(1,128)} %bitcast.76, ...), custom_call_target="tpu_custom_call" | custom-call | flops 1 | bytes 1 | tf_op jit(solution)/shard_map/pallas_call | solution.py:42
  627.1 59.5 %shard_map.327.refs_0_.refs_18_ = bf16[16,128,128]{2,1,0:T(8,128)(2,1)} custom-call(bf16[16,128,256]{2,1,0:T(8,128)(2,1)} %get-tuple-element.106.refs_0_), custom_call_target="tpu_custom_call" | custom-call | flops 1 | bytes 1 | tf_op jit(solution)/shard_map/pallas_call | solution.py:553
  687.6 8.3 shard_map.329
  695.9 1.3 collective-permute-start.19
  697.2 8.3 shard_map.328
  705.5 1.3 collective-permute-start.18
  706.9 39.3 %shard_map.330 = (bf16[3,256,2048]{2,1,0:T(8,128)(2,1)}, f32[3,8,2048]{2,1,0:T(8,128)}, f32[3,8,2048]{2,1,0:T(8,128)}, f32[3,8,2048]{2,1,0:T(8,128)}, f32[256,16]{1,0:T(8,128)}) custom-call(bf16[512,2304]{1,0:T(8,128)(2,1)} %get-tuple-element.107.refs_0_.refs_2_, bf16[512,2304]{1,0:T(8,128)(2,1)} %get-tuple-element.108.refs_1_, ...), custom_call_target="tpu_custom_call" | custom-call | flops 1 | bytes 1 | tf_op jit(solution)/shard_map/pallas_call | solution.py:42
  746.1 6.7 shard_map.331.refs_1_.refs_0_
  753.6 5.8 shard_map.332.refs_1_
  763.0 4.0 collective-permute-start.29
  768.5 3.1 maximum_maximum_fusion.refs_3_
  771.6 1.6 constant_dynamic-slice_fusion.2
  773.9 4.7 shard_map.334.refs_1_
  778.6 2.8 fusion.63
  781.7 4.7 shard_map.333.refs_0_
  786.4 2.8 fusion.62
  789.5 1.8 fusion.39
  792.8 2.3 pad_maximum_fusion.3
  795.1 6.4 shard_map.336.refs_1_.refs_9_
  801.5 6.4 shard_map.335.refs_0_.refs_8_
  808.5 6.4 shard_map.338.refs_1_.refs_11_
  815.0 6.4 shard_map.337.refs_0_.refs_10_
  821.4 4.4 pad_maximum_fusion.2.refs_2_
  825.9 15.6 %shard_map.339 = f32[256,2048]{1,0:T(8,128)} custom-call(bf16[1024,2048]{1,0:T(8,128)(2,1)} %shard_map.337.refs_0_.refs_10_, bf16[1024,2048]{1,0:T(8,128)(2,1)} %shard_map.338.refs_1_.refs_11_, bf16[256,9216]{1,0:T(8,128)(2,1)} %pad_maximum_fusion.2.refs_2_, bf16[256,6144]{1,0:T(8,128)(2,1)} %copy-done.7, ...), custom_call_target="tpu_custom_call" | custom-call | flops 1 | bytes 1 | tf_op jit(solution)/shard_map/pallas_call | solution.py:42
  841.6 3.0 fusion.12
  844.6 1.7 concatenate.145
  847.3 3.2 fusion.15
  850.5 6.7 shard_map.341
  857.6 1.3 copy.121
  860.6 8.3 shard_map.340
  869.0 239.5 %shard_map.342 = (f32[64,512]{1,0:T(8,128)}, f32[64,7680]{1,0:T(8,128)}, f32[64,8192]{1,0:T(8,128)}, f32[8,256]{1,0:T(8,128)}) custom-call(bf16[1024,128]{1,0:T(8,128)(2,1)} %pad_maximum_fusion.12.refs_0_.refs_1_, bf16[1024,128]{1,0:T(8,128)(2,1)} %pad_maximum_fusion.12.refs_0_.refs_1_, bf16[1024,128]{1,0:T(8,128)(2,1)} %pad_maximum_fusion.13.refs_2_.refs_3_, ...), custom_call_target="tpu_custom_call" | custom-call | flops 1 | bytes 1 | tf_op jit(solution)/shard_map/pallas_call | solution.py:1487
  1136.4 1.4 convert_element_type.151
  1138.0 1.3 copy-done.29
  (318 shorter events, 90.0 us)
Async XLA Ops:
  7.2 13.6 %copy-start.34 = (bf16[64,5632]{1,0:T(8,128)(2,1)S(1)}, bf16[64,5632]{1,0:T(8,128)(2,1)}, u32[]{:S(2)}) copy-start(bf16[64,5632]{1,0:T(8,128)(2,1)} %param.39) | copy-start | bytes 2162692
  7.2 9.4 copy-start.56
  7.2 10.1 copy-start.57
  7.2 10.8 copy-start.52
  7.2 11.5 copy-start.53
  7.2 12.2 %copy-start.54 = (bf16[64,4]{0,1:T(4,128)(2,1)S(1)}, bf16[64,4]{0,1:T(4,128)(2,1)}, u32[]{:S(2)}) copy-start(bf16[64,4]{0,1:T(4,128)(2,1)} %param.33) | copy-start | bytes 1540
  7.3 12.9 %copy-start.51 = (bf16[64,16]{0,1:T(8,128)(2,1)S(1)}, bf16[64,16]{0,1:T(8,128)(2,1)}, u32[]{:S(2)}) copy-start(bf16[64,16]{0,1:T(8,128)(2,1)} %param.34) | copy-start | bytes 6148
  7.3 258.4 %all-gather.5.cloned.1.call-start = ((), (), s32[]{:S(2)}) async-start(), calls=%async_computation.2 | async-start | bytes 2457600 | tf_op jit(solution)/shard_map/all_gather | solution.py:1542
  11.0 13.9 %copy-start.38 = (bf16[64,2048]{1,0:T(8,128)(2,1)S(1)}, bf16[64,2048]{1,0:T(8,128)(2,1)}, u32[]{:S(2)}) copy-start(bf16[64,2048]{1,0:T(8,128)(2,1)} %param.29) | copy-start | bytes 786436
  13.7 11.2 copy-start.39
  25.0 175.0 %copy-start.13 = (bf16[256,2048]{1,0:T(8,128)(2,1)S(1)}, bf16[256,2048]{1,0:T(8,128)(2,1)}, u32[]{:S(2)}) copy-start(bf16[256,2048]{1,0:T(8,128)(2,1)} %param.23) | copy-start | bytes 3145732
  197.8 126.9 %all-gather.3.cloned.1.call-start = ((), (), s32[]{:S(2)}) async-start(), calls=%async_computation.1 | async-start | bytes 2457600 | tf_op jit(solution)/shard_map/all_gather | solution.py:1542
  197.9 54.0 %collective-permute-start.1 = (bf16[512,2304]{1,0:T(8,128)(2,1)}, bf16[512,2304]{1,0:T(8,128)(2,1)S(1)}, u32[]{:S(2)}, u32[]{:S(2)}) collective-permute-start(bf16[512,2304]{1,0:T(8,128)(2,1)} %get-tuple-element.87.refs_16_.refs_20_.refs_24_), channel_id=1, source_target_pairs={{0,8},{4,12},{8,0},{12,4},{16,24},{20,28},{24,16},{28,20},{1,9},{5... | collective-permute-start | bytes 7077896 | tf_op jit(solution)/shard_map/ppermute | solution.py:577
  198.5 57.6 %collective-permute-start = (bf16[512,2304]{1,0:T(8,128)(2,1)}, bf16[512,2304]{1,0:T(8,128)(2,1)}, u32[]{:S(2)}, u32[]{:S(2)}) collective-permute-start(bf16[512,2304]{1,0:T(8,128)(2,1)} %get-tuple-element.86.refs_4_.refs_8_.refs_12_), channel_id=1, source_target_pairs={{0,16},{4,20},{8,24},{12,28},{16,0},{20,4},{24,8},{28,12},{1,17},{... | collective-permute-start | bytes 7077896 | tf_op jit(solution)/shard_map/ppermute | solution.py:577
  200.0 65.4 %collective-permute-start.2 = (bf16[3,2048]{1,0:T(4,128)(2,1)S(1)}, bf16[3,2048]{1,0:T(4,128)(2,1)S(1)}, u32[]{:S(2)}, u32[]{:S(2)}) collective-permute-start(bf16[3,2048]{1,0:T(4,128)(2,1)S(1)} %slice.488), channel_id=1, source_target_pairs={{0,1},{1,2},{2,3},{3,4},{4,5},{5,6},{6,7},{7,8},{8,9},{9,10},{10,1... | collective-permute-start | bytes 36872 | tf_op jit(solution)/shard_map/ppermute | solution.py:23
  201.4 935.0 %reduce-scatter.2.cloned.1.call-start = ((), (), s32[]{:S(2)}) async-start(), calls=%async_computation.3 | async-start | bytes 5898240 | tf_op jit(solution)/shard_map/reduce_scatter | solution.py:651
  203.3 61.3 %copy-start.48 = (f32[256]{0:T(256)}, f32[256]{0:T(256)S(1)}, u32[]{:S(2)}) copy-start(f32[256]{0:T(256)S(1)} %convert_element_type.130) | copy-start | bytes 3076
  205.7 59.8 %copy-start.41 = (f32[2048]{0:T(1024)}, f32[2048]{0:T(1024)S(1)}, u32[]{:S(2)}) copy-start(f32[2048]{0:T(1024)S(1)} %get-tuple-element.204) | copy-start | bytes 24580
  207.4 44.5 %copy-start.5 = (bf16[512,2304]{1,0:T(8,128)(2,1)S(1)}, bf16[512,2304]{1,0:T(8,128)(2,1)}, u32[]{:S(2)}) copy-start(bf16[512,2304]{1,0:T(8,128)(2,1)} %get-tuple-element.87.refs_16_.refs_20_.refs_24_) | copy-start | bytes 7077892
  209.0 47.1 %copy-start.4 = (bf16[512,2304]{1,0:T(8,128)(2,1)S(1)}, bf16[512,2304]{1,0:T(8,128)(2,1)}, u32[]{:S(2)}) copy-start(bf16[512,2304]{1,0:T(8,128)(2,1)} %get-tuple-element.86.refs_4_.refs_8_.refs_12_) | copy-start | bytes 7077892
  254.7 103.7 %collective-permute-start.4 = (bf16[1024,2304]{1,0:T(8,128)(2,1)}, bf16[1024,2304]{1,0:T(8,128)(2,1)}, u32[]{:S(2)}, u32[]{:S(2)}) collective-permute-start(bf16[1024,2304]{1,0:T(8,128)(2,1)} %pad_maximum_fusion.1), channel_id=1, source_target_pairs={{0,16},{4,20},{8,24},{12,28},{16,0},{20,4},{24,8},{28,12},{1,17},{... | collective-permute-start | bytes 14155784 | tf_op jit(solution)/shard_map/ppermute | solution.py:577
  256.1 5.4 copy-start.25
  260.3 103.4 %collective-permute-start.3 = (bf16[1024,2304]{1,0:T(8,128)(2,1)}, bf16[1024,2304]{1,0:T(8,128)(2,1)}, u32[]{:S(2)}, u32[]{:S(2)}) collective-permute-start(bf16[1024,2304]{1,0:T(8,128)(2,1)} %pad_maximum_fusion), channel_id=1, source_target_pairs={{0,8},{4,12},{8,0},{12,4},{16,24},{20,28},{24,16},{28,20},{1,9},{5... | collective-permute-start | bytes 14155784 | tf_op jit(solution)/shard_map/ppermute | solution.py:577
  261.8 17.1 %copy-start.45 = (s32[256]{0:T(256)}, s32[256]{0:T(256)S(1)}, u32[]{:S(2)}) copy-start(s32[256]{0:T(256)S(1)} %select_reduce_fusion) | copy-start | bytes 3076
  265.7 59.0 %collective-permute-start.5 = (bf16[256,3840]{1,0:T(8,128)(2,1)}, bf16[256,3840]{1,0:T(8,128)(2,1)S(1)}, u32[]{:S(2)}, u32[]{:S(2)}) collective-permute-start(bf16[256,3840]{1,0:T(8,128)(2,1)} %all-gather.5.cloned.1.call-done), channel_id=1, source_target_pairs={{0,4},{4,0},{8,12},{12,8},{16,20},{20,16},{24,28},{28,24},{1,5},{5... | collective-permute-start | bytes 5898248 | tf_op jit(solution)/shard_map/ppermute | solution.py:577
  324.7 39.0 %copy-start.19 = (bf16[256,3840]{1,0:T(8,128)(2,1)}, bf16[256,3840]{1,0:T(8,128)(2,1)S(1)}, u32[]{:S(2)}) copy-start(bf16[256,3840]{1,0:T(8,128)(2,1)S(1)} %collective-permute-done.5.refs_4_) | copy-start | bytes 5898244
  367.7 106.4 %collective-permute-start.6 = (bf16[512,2304]{1,0:T(8,128)(2,1)}, bf16[512,2304]{1,0:T(8,128)(2,1)S(1)}, u32[]{:S(2)}, u32[]{:S(2)}) collective-permute-start(bf16[512,2304]{1,0:T(8,128)(2,1)} %shard_map.317.refs_4_.refs_8_.refs_12_), channel_id=1, source_target_pairs={{0,16},{4,20},{8,24},{12,28},{16,0},{20,4},{24,8},{28,12},{1,17},{... | collective-permute-start | bytes 7077896 | tf_op jit(solution)/shard_map/ppermute | solution.py:577
  368.4 106.3 %collective-permute-start.7 = (bf16[512,2304]{1,0:T(8,128)(2,1)}, bf16[512,2304]{1,0:T(8,128)(2,1)S(1)}, u32[]{:S(2)}, u32[]{:S(2)}) collective-permute-start(bf16[512,2304]{1,0:T(8,128)(2,1)} %shard_map.317.refs_4_.refs_8_.refs_12_), channel_id=1, source_target_pairs={{0,8},{4,12},{8,0},{12,4},{16,24},{20,28},{24,16},{28,20},{1,9},{5... | collective-permute-start | bytes 7077896 | tf_op jit(solution)/shard_map/ppermute | solution.py:577
  371.3 102.1 %collective-permute-start.8 = (bf16[512,1536]{1,0:T(8,128)(2,1)}, bf16[512,1536]{1,0:T(8,128)(2,1)}, u32[]{:S(2)}, u32[]{:S(2)}) collective-permute-start(bf16[512,1536]{1,0:T(8,128)(2,1)} %shard_map.318.refs_16_.refs_20_.refs_24_), channel_id=1, source_target_pairs={{0,8},{4,12},{8,0},{12,4},{16,24},{20,28},{24,16},{28,20},{1,9},{5... | collective-permute-start | bytes 4718600 | tf_op jit(solution)/shard_map/ppermute | solution.py:577
  372.8 101.9 %collective-permute-start.9 = (bf16[512,1536]{1,0:T(8,128)(2,1)}, bf16[512,1536]{1,0:T(8,128)(2,1)S(1)}, u32[]{:S(2)}, u32[]{:S(2)}) collective-permute-start(bf16[512,1536]{1,0:T(8,128)(2,1)} %shard_map.318.refs_16_.refs_20_.refs_24_), channel_id=1, source_target_pairs={{0,16},{4,20},{8,24},{12,28},{16,0},{20,4},{24,8},{28,12},{1,17},{... | collective-permute-start | bytes 4718600 | tf_op jit(solution)/shard_map/ppermute | solution.py:577
  374.1 121.9 %collective-permute-start.11 = (bf16[256,2048]{1,0:T(8,128)(2,1)}, bf16[256,2048]{1,0:T(8,128)(2,1)}, u32[]{:S(2)}, u32[]{:S(2)}) collective-permute-start(bf16[256,2048]{1,0:T(8,128)(2,1)} %refs_2_.1), channel_id=1, source_target_pairs={{0,4},{4,0},{8,12},{12,8},{16,20},{20,16},{24,28},{28,24},{1,5},{5... | collective-permute-start | bytes 3145736 | tf_op jit(solution)/shard_map/ppermute | solution.py:577
  473.3 82.4 %collective-permute-start.13 = (bf16[512,1536]{1,0:T(8,128)(2,1)}, bf16[512,1536]{1,0:T(8,128)(2,1)}, u32[]{:S(2)}, u32[]{:S(2)}) collective-permute-start(bf16[512,1536]{1,0:T(8,128)(2,1)} %collective-permute-done.8.refs_2_.refs_18_.refs_22_.refs_26_), channel_id=1, source_target_pairs={{0,16},{4,20},{8,24},{12,28},{16,0},{20,4},{24,8},{28,12},{1,17},{... | collective-permute-start | bytes 4718600 | tf_op jit(solution)/shard_map/ppermute | solution.py:577
  474.1 81.6 %collective-permute-start.12 = (bf16[512,2304]{1,0:T(8,128)(2,1)S(1)}, bf16[512,2304]{1,0:T(8,128)(2,1)}, u32[]{:S(2)}, u32[]{:S(2)}) collective-permute-start(bf16[512,2304]{1,0:T(8,128)(2,1)S(1)} %collective-permute-done.6.refs_0_.refs_5_.refs_9_.refs_13_), channel_id=1, source_target_pairs={{0,8},{4,12},{8,0},{12,4},{16,24},{20,28},{24,16},{28,20},{1,9},{5... | collective-permute-start | bytes 7077896 | tf_op jit(solution)/shard_map/ppermute | solution.py:577
  495.2 44.5 %copy-start.11 = (f32[256,2048]{1,0:T(8,128)}, f32[256,2048]{1,0:T(8,128)S(1)}, u32[]{:S(2)}) copy-start(f32[256,2048]{1,0:T(8,128)S(1)} %get-tuple-element.388) | copy-start | bytes 6291460
  495.4 3.6 collective-permute-start.10
  495.5 90.7 %collective-permute-start.20 = (bf16[256,2048]{1,0:T(8,128)(2,1)S(1)}, bf16[256,2048]{1,0:T(8,128)(2,1)S(1)}, u32[]{:S(2)}, u32[]{:S(2)}) collective-permute-start(bf16[256,2048]{1,0:T(8,128)(2,1)S(1)} %fusion.11), channel_id=1, source_target_pairs={{0,4},{4,0},{8,12},{12,8},{16,20},{20,16},{24,28},{28,24},{1,5},{5... | collective-permute-start | bytes 3145736 | tf_op jit(solution)/shard_map/ppermute | solution.py:577
  553.0 134.6 %collective-permute-start.17 = (bf16[1024,2304]{1,0:T(8,128)(2,1)}, bf16[1024,2304]{1,0:T(8,128)(2,1)}, u32[]{:S(2)}, u32[]{:S(2)}) collective-permute-start(bf16[1024,2304]{1,0:T(8,128)(2,1)} %shard_map.323.refs_1_), channel_id=1, source_target_pairs={{0,16},{4,20},{8,24},{12,28},{16,0},{20,4},{24,8},{28,12},{1,17},{... | collective-permute-start | bytes 14155784 | tf_op jit(solution)/shard_map/ppermute | solution.py:577
  554.4 142.9 %collective-permute-start.16 = (bf16[1024,2304]{1,0:T(8,128)(2,1)}, bf16[1024,2304]{1,0:T(8,128)(2,1)}, u32[]{:S(2)}, u32[]{:S(2)}) collective-permute-start(bf16[1024,2304]{1,0:T(8,128)(2,1)} %shard_map.322.refs_0_), channel_id=1, source_target_pairs={{0,8},{4,12},{8,0},{12,4},{16,24},{20,28},{24,16},{28,20},{1,9},{5... | collective-permute-start | bytes 14155784 | tf_op jit(solution)/shard_map/ppermute | solution.py:577
  586.1 8.2 collective-permute-start.15
  587.3 4.5 collective-permute-start.21
  588.1 8.8 collective-permute-start.14
  588.7 5.6 copy-start.18
  588.8 5.5 copy-start.12
  601.9 84.7 %collective-permute-start.24 = (bf16[256,1024]{1,0:T(8,128)(2,1)S(1)}, bf16[256,1024]{1,0:T(8,128)(2,1)S(1)}, u32[]{:S(2)}, u32[]{:S(2)}) collective-permute-start(bf16[256,1024]{1,0:T(8,128)(2,1)S(1)} %get-tuple-element.338), channel_id=1, source_target_pairs={{0,4},{4,0},{8,12},{12,8},{16,20},{20,16},{24,28},{28,24},{1,5},{5... | collective-permute-start | bytes 1572872 | tf_op jit(solution)/shard_map/ppermute | solution.py:577
  695.9 78.0 %collective-permute-start.19 = (bf16[512,2304]{1,0:T(8,128)(2,1)}, bf16[512,2304]{1,0:T(8,128)(2,1)}, u32[]{:S(2)}, u32[]{:S(2)}) collective-permute-start(bf16[512,2304]{1,0:T(8,128)(2,1)} %get-tuple-element.110.refs_3_), channel_id=1, source_target_pairs={{0,8},{4,12},{8,0},{12,4},{16,24},{20,28},{24,16},{28,20},{1,9},{5... | collective-permute-start | bytes 7077896 | tf_op jit(solution)/shard_map/ppermute | solution.py:577
  705.5 76.2 %collective-permute-start.18 = (bf16[512,2304]{1,0:T(8,128)(2,1)}, bf16[512,2304]{1,0:T(8,128)(2,1)}, u32[]{:S(2)}, u32[]{:S(2)}) collective-permute-start(bf16[512,2304]{1,0:T(8,128)(2,1)} %get-tuple-element.108.refs_1_), channel_id=1, source_target_pairs={{0,16},{4,20},{8,24},{12,28},{16,0},{20,4},{24,8},{28,12},{1,17},{... | collective-permute-start | bytes 7077896 | tf_op jit(solution)/shard_map/ppermute | solution.py:577
  752.9 107.7 %collective-permute-start.28 = (bf16[1024,2304]{1,0:T(8,128)(2,1)}, bf16[1024,2304]{1,0:T(8,128)(2,1)}, u32[]{:S(2)}, u32[]{:S(2)}) collective-permute-start(bf16[1024,2304]{1,0:T(8,128)(2,1)} %shard_map.331.refs_1_.refs_0_), channel_id=1, source_target_pairs={{0,8},{4,12},{8,0},{12,4},{16,24},{20,28},{24,16},{28,20},{1,9},{5... | collective-permute-start | bytes 14155784 | tf_op jit(solution)/shard_map/ppermute | solution.py:577
  753.6 8.1 copy-start.22
  760.4 7.4 collective-permute-start.22
  761.7 5.3 copy-start.44
  761.7 5.9 copy-start.32
  761.7 5.9 copy-start.43
  761.7 5.9 copy-start.49
  761.7 6.0 copy-start.37
  763.0 87.6 %collective-permute-start.29 = (bf16[1024,1536]{1,0:T(8,128)(2,1)}, bf16[1024,1536]{1,0:T(8,128)(2,1)}, u32[]{:S(2)}, u32[]{:S(2)}) collective-permute-start(bf16[1024,1536]{1,0:T(8,128)(2,1)} %shard_map.332.refs_1_), channel_id=1, source_target_pairs={{0,16},{4,20},{8,24},{12,28},{16,0},{20,4},{24,8},{28,12},{1,17},{... | collective-permute-start | bytes 9437192 | tf_op jit(solution)/shard_map/ppermute | solution.py:577
  773.7 17.9 %collective-permute-start.23 = (bf16[256,3072]{1,0:T(8,128)(2,1)}, bf16[256,3072]{1,0:T(8,128)(2,1)S(1)}, u32[]{:S(2)}, u32[]{:S(2)}) collective-permute-start(bf16[256,3072]{1,0:T(8,128)(2,1)} %get-tuple-element.218), channel_id=1, source_target_pairs={{0,4},{4,0},{8,12},{12,8},{16,20},{20,16},{24,28},{28,24},{1,5},{5... | collective-permute-start | bytes 4718600 | tf_op jit(solution)/shard_map/ppermute | solution.py:577
  781.4 40.1 %collective-permute-start.26 = (bf16[256,2304]{1,0:T(8,128)(2,1)}, bf16[256,2304]{1,0:T(8,128)(2,1)}, u32[]{:S(2)}, u32[]{:S(2)}) collective-permute-start(bf16[256,2304]{1,0:T(8,128)(2,1)} %get-tuple-element.238), channel_id=1, source_target_pairs={{0,4},{4,0},{8,12},{12,8},{16,20},{20,16},{24,28},{28,24},{1,5},{5... | collective-permute-start | bytes 3538952 | tf_op jit(solution)/shard_map/ppermute | solution.py:577
  789.2 32.2 %collective-permute-start.25 = (bf16[256,2304]{1,0:T(8,128)(2,1)}, bf16[256,2304]{1,0:T(8,128)(2,1)}, u32[]{:S(2)}, u32[]{:S(2)}) collective-permute-start(bf16[256,2304]{1,0:T(8,128)(2,1)} %get-tuple-element.236), channel_id=1, source_target_pairs={{0,4},{4,0},{8,12},{12,8},{16,20},{20,16},{24,28},{28,24},{1,5},{5... | collective-permute-start | bytes 3538952 | tf_op jit(solution)/shard_map/ppermute | solution.py:577
  825.9 15.7 %copy-start.15 = (bf16[256,2048]{1,0:T(8,128)(2,1)S(1)}, bf16[256,2048]{1,0:T(8,128)(2,1)}, u32[]{:S(2)}) copy-start(bf16[256,2048]{1,0:T(8,128)(2,1)} %param.23) | copy-start | bytes 3145732
  825.9 15.7 %copy-start.17 = (f32[256,2048]{1,0:T(8,128)S(1)}, f32[256,2048]{1,0:T(8,128)}, u32[]{:S(2)}) copy-start(f32[256,2048]{1,0:T(8,128)} %fusion.39) | copy-start | bytes 6291460
  825.9 15.7 %copy-start.42 = (f32[2048]{0:T(1024)S(1)}, f32[2048]{0:T(1024)}, u32[]{:S(2)}) copy-start(f32[2048]{0:T(1024)} %copy-done.41) | copy-start | bytes 24580
  825.9 15.7 %copy-start.47 = (f32[256]{0:T(256)S(1)}, f32[256]{0:T(256)}, u32[]{:S(2)}) copy-start(f32[256]{0:T(256)} %copy-done.46) | copy-start | bytes 3076
  844.6 6.0 copy-start.6
  846.3 11.3 collective-permute-start.27
  (31 other events, 76.6 us)
Sparse Core Ops, SparseCore 0:
  197.9 41.5 all-gather.4
  241.6 41.7 all-gather.2
  826.0 87.2 reduce-scatter.1
